TPU v7x, 32 devices: a whole 2x2x4 slice. The times are simulated.
32 devices in a mesh: dp: 8 (over y, x, core), tensor: 4 (over z).
Axes of the slice: x: 2, y: 2, z: 4, core: 2. Of those that a mesh axis runs over, the one named last changes fastest.
Arguments:
- tokens: bfloat16 [16384, 768], P(('dp', 'tensor')), may hold values from -6 to 6
- token_ids: int32 [16384], P(('dp', 'tensor')), may hold values from 0 to 50256
- hash_table: int32 [50257], replicated, may hold values from 0 to 15
- ln1_gain: float32 [768], replicated, may hold values from 0.5 to 1.5
- ln1_bias: float32 [768], replicated, may hold values from -1 to 1
- w_qkv: float32 [768, 12, 192], P('dp', 'tensor'), may hold values from -0.21875 to 0.21875
- w_out: float32 [768, 768], P('tensor', 'dp'), may hold values from -1.25 to 1.25
- ln2_gain: float32 [768], replicated, may hold values from 0.5 to 1.5
- ln2_bias: float32 [768], replicated, may hold values from -1 to 1
- expert_in: float32 [16, 768, 3072], P('dp', None, 'tensor'), may hold values from -0.21875 to 0.21875
- expert_out: float32 [16, 3072, 768], P('dp', 'tensor'), may hold values from -0.109375 to 0.109375
- cotangent: bfloat16 [16384, 768], P(('dp', 'tensor')), may hold values from -6 to 6
Outputs:
- out: bfloat16 [16384, 768], P(('dp', 'tensor'))
- grad_tokens: bfloat16 [16384, 768], P(('dp', 'tensor'))
- grad_ln1_gain: float32 [768], replicated
- grad_ln1_bias: float32 [768], replicated
- grad_w_qkv: float32 [768, 12, 192], P('dp', 'tensor')
- grad_w_out: float32 [768, 768], P('tensor', 'dp')
- grad_ln2_gain: float32 [768], replicated
- grad_ln2_bias: float32 [768], replicated
- grad_expert_in: float32 [16, 768, 3072], P('dp', None, 'tensor')
- grad_expert_out: float32 [16, 3072, 768], P('dp', 'tensor')
Inputs may be any that keep to these rules, and one draw needn't show every extreme that they name: hash_table gives each token id one expert.
All inputs are finite; a program needn't handle non-finite values.
Results may differ from a plain program's by a relative error of at most 0.018.
Values may be sent and summed in bfloat16 or wider, within the bound.
A program may use at most 192 MiB of HBM per device.

v0:
```python
import jax
import jax.numpy as jnp
from jax import lax
from jax.sharding import PartitionSpec as P

LEN = 1024


EPSILON = 1e-05
SCORE_SCALE = 0.125
MASKED = -1e30


def normalize(values, norm_gain, norm_shift):
    center = jnp.mean(values, axis=-1, keepdims=True)
    centered = values - center
    inv_scale = lax.rsqrt(jnp.mean(centered * centered, axis=-1, keepdims=True) + EPSILON)
    unit_rows = centered * inv_scale
    return (unit_rows * norm_gain + norm_shift, unit_rows, inv_scale)


def norm_back(grad_rows, unit_rows, inv_scale, norm_gain):
    scaled = grad_rows * norm_gain
    mean_plain = jnp.mean(scaled, axis=-1, keepdims=True)
    mean_unit = jnp.mean(scaled * unit_rows, axis=-1, keepdims=True)
    return inv_scale * (scaled - mean_plain - unit_rows * mean_unit)


def smooth(values):
    return jax.nn.gelu(values, approximate=True)


def causal_scores(query_rows, key_rows):
    length = query_rows.shape[0]
    scores = (
        jnp.einsum("qhd,khd->hqk", query_rows, key_rows, preferred_element_type=jnp.float32)
        * SCORE_SCALE
    )
    causal = lax.broadcasted_iota(jnp.int32, (length, length), 0) >= lax.broadcasted_iota(
        jnp.int32, (length, length), 1
    )
    return jnp.where(causal[None], scores, MASKED)


def attend(seq_block):
    scores = causal_scores(seq_block[:, :, 0], seq_block[:, :, 1])
    row_max = jnp.max(scores, axis=-1, keepdims=True)
    exp_scores = jnp.exp(scores - row_max)
    denominator = jnp.sum(exp_scores, axis=-1, keepdims=True)
    probabilities = (exp_scores / denominator).astype(jnp.bfloat16)
    mixed_heads = jnp.einsum(
        "hqk,khd->qhd", probabilities, seq_block[:, :, 2], preferred_element_type=jnp.float32
    )
    return (mixed_heads.astype(jnp.bfloat16), (row_max + jnp.log(denominator))[:, :, 0])


def attend_back(inputs):
    seq_block, mixed_grad, log_total = inputs
    query_rows = seq_block[:, :, 0]
    key_rows = seq_block[:, :, 1]
    value_rows = seq_block[:, :, 2]
    probabilities = jnp.exp(causal_scores(query_rows, key_rows) - log_total[:, :, None])
    prob_grad = jnp.einsum(
        "qhd,khd->hqk", mixed_grad, value_rows, preferred_element_type=jnp.float32
    )
    row_inner = jnp.sum(probabilities * prob_grad, axis=-1, keepdims=True)
    score_grad = (probabilities * (prob_grad - row_inner)).astype(jnp.bfloat16)
    value_grad = jnp.einsum(
        "hqk,qhd->khd",
        probabilities.astype(jnp.bfloat16),
        mixed_grad,
        preferred_element_type=jnp.float32,
    )
    query_grad = (
        jnp.einsum("hqk,khd->qhd", score_grad, key_rows, preferred_element_type=jnp.float32)
        * SCORE_SCALE
    )
    key_grad = (
        jnp.einsum("hqk,qhd->khd", score_grad, query_rows, preferred_element_type=jnp.float32)
        * SCORE_SCALE
    )
    return jnp.stack([query_grad, key_grad, value_grad], axis=2).astype(jnp.bfloat16)


def expert_back(shaped, hidden, activated, grad_rows, weight_out):
    act_grad = jnp.einsum(
        "secd,efd->secf", grad_rows, weight_out, preferred_element_type=jnp.float32
    )
    out_wgrad = jnp.einsum(
        "secf,secd->efd", activated, grad_rows, preferred_element_type=jnp.float32
    )
    unused, pull = jax.vjp(smooth, hidden)
    hidden_grad = pull(act_grad)[0].astype(jnp.bfloat16)
    in_wgrad = jnp.einsum("secd,secf->edf", shaped, hidden_grad, preferred_element_type=jnp.float32)
    return (hidden_grad, in_wgrad, out_wgrad)


def on_device(
    tokens,
    token_ids,
    hash_table,
    ln1_gain,
    ln1_bias,
    w_qkv,
    w_out,
    ln2_gain,
    ln2_bias,
    expert_in,
    expert_out,
    cotangent,
):
    row_count = tokens.shape[0]
    model_width = tokens.shape[1]
    local_experts = expert_in.shape[0]
    dp_count = lax.axis_size("dp")
    qkv_weight, out_weight = (
        lax.all_gather(w_qkv.astype(jnp.bfloat16), "dp", axis=0, tiled=True),
        lax.all_gather(w_out.astype(jnp.bfloat16), "dp", axis=1, tiled=True),
    )
    qkv_flat = qkv_weight.reshape(model_width, -1)
    heads_here = qkv_weight.shape[1]
    head_dim = qkv_weight.shape[2] // 3
    residual = tokens.astype(jnp.float32)
    first_norm, unit_one, scale_one = normalize(residual, ln1_gain, ln1_bias)
    first_all = lax.all_gather(first_norm.astype(jnp.bfloat16), "tensor", axis=0, tiled=True)
    group_rows = first_all.shape[0]
    projected = jnp.dot(first_all, qkv_flat, preferred_element_type=jnp.float32).astype(
        jnp.bfloat16
    )
    seq_blocks = projected.reshape(group_rows // LEN, LEN, heads_here, 3, head_dim)
    mixed_heads, log_total = lax.map(attend, seq_blocks)
    mixed_flat = mixed_heads.reshape(group_rows, heads_here * head_dim)
    attention = lax.psum_scatter(
        jnp.dot(mixed_flat, out_weight, preferred_element_type=jnp.float32).astype(jnp.bfloat16),
        "tensor",
        scatter_dimension=0,
        tiled=True,
    ).astype(jnp.float32)
    middle = residual + attention
    second_norm, unit_two, scale_two = normalize(middle, ln2_gain, ln2_bias)
    experts_total = dp_count * local_experts
    capacity = 2 * row_count // experts_total
    slot_count = experts_total * capacity
    expert_of = jnp.take(hash_table, token_ids)
    one_hot = (expert_of[:, None] == jnp.arange(experts_total, dtype=jnp.int32)[None, :]).astype(
        jnp.int32
    )
    slot_rank = jnp.sum((jnp.cumsum(one_hot, axis=0) - 1) * one_hot, axis=1)
    kept_rows = slot_rank < capacity
    target = jnp.where(kept_rows, expert_of * capacity + slot_rank, slot_count)
    source_row = jnp.minimum(target, slot_count - 1)

    def dispatch_rows(values):
        return (
            jnp.zeros((slot_count, model_width), jnp.bfloat16).at[target].set(values, mode="drop")
        )

    def collect_rows(values):
        return jnp.where(
            kept_rows[:, None], jnp.take(values, source_row, axis=0).astype(jnp.float32), 0.0
        )

    out_grad = cotangent.astype(jnp.float32)
    received = lax.all_to_all(
        dispatch_rows(second_norm.astype(jnp.bfloat16)),
        "dp",
        split_axis=0,
        concat_axis=0,
        tiled=True,
    )
    grad_sent = lax.all_to_all(
        dispatch_rows(cotangent), "dp", split_axis=0, concat_axis=0, tiled=True
    )
    weight_in, weight_out = (
        lax.all_gather(expert_in.astype(jnp.bfloat16), "tensor", axis=2, tiled=True),
        lax.all_gather(expert_out.astype(jnp.bfloat16), "tensor", axis=1, tiled=True),
    )
    shaped = received.reshape(dp_count, local_experts, capacity, model_width)
    hidden = jnp.einsum("secd,edf->secf", shaped, weight_in, preferred_element_type=jnp.float32)
    activated = smooth(hidden).astype(jnp.bfloat16)
    expert_result = jnp.einsum(
        "secf,efd->secd", activated, weight_out, preferred_element_type=jnp.float32
    )
    expert_result = expert_result.astype(jnp.bfloat16).reshape(slot_count, model_width)
    grad_rows = grad_sent.reshape(dp_count, local_experts, capacity, model_width)
    hidden_grad, in_wgrad, out_wgrad = expert_back(shaped, hidden, activated, grad_rows, weight_out)
    row_grad = jnp.einsum(
        "secf,edf->secd", hidden_grad, weight_in, preferred_element_type=jnp.float32
    )
    row_grad = row_grad.astype(jnp.bfloat16).reshape(slot_count, model_width)
    grad_expert_in, grad_expert_out = (
        lax.psum_scatter(
            in_wgrad.astype(jnp.bfloat16), "tensor", scatter_dimension=2, tiled=True
        ).astype(jnp.float32),
        lax.psum_scatter(
            out_wgrad.astype(jnp.bfloat16), "tensor", scatter_dimension=1, tiled=True
        ).astype(jnp.float32),
    )
    returned = lax.all_to_all(expert_result, "dp", split_axis=0, concat_axis=0, tiled=True)
    mixed_out = middle + collect_rows(returned)
    row_back = lax.all_to_all(row_grad, "dp", split_axis=0, concat_axis=0, tiled=True)
    second_grad = collect_rows(row_back)
    gain_two_grad = jnp.sum(second_grad * unit_two, axis=0)
    bias_two_grad = jnp.sum(second_grad, axis=0)
    middle_grad = out_grad + norm_back(second_grad, unit_two, scale_two, ln2_gain)
    middle_all = lax.all_gather(middle_grad.astype(jnp.bfloat16), "tensor", axis=0, tiled=True)
    out_wgrad_local = jnp.einsum(
        "tk,td->kd", mixed_flat, middle_all, preferred_element_type=jnp.float32
    )
    mixed_grad = jnp.einsum(
        "td,kd->tk", middle_all, out_weight, preferred_element_type=jnp.float32
    ).astype(jnp.bfloat16)
    mixed_grad = mixed_grad.reshape(group_rows // LEN, LEN, heads_here, head_dim)
    qkv_grad = lax.map(attend_back, (seq_blocks, mixed_grad, log_total)).reshape(group_rows, -1)
    qkv_wgrad = jnp.einsum(
        "td,tk->dk", first_all, qkv_grad, preferred_element_type=jnp.float32
    ).reshape(qkv_weight.shape)
    first_grad = lax.psum_scatter(
        jnp.einsum("tk,dk->td", qkv_grad, qkv_flat, preferred_element_type=jnp.float32).astype(
            jnp.bfloat16
        ),
        "tensor",
        scatter_dimension=0,
        tiled=True,
    ).astype(jnp.float32)
    gain_one_grad = jnp.sum(first_grad * unit_one, axis=0)
    bias_one_grad = jnp.sum(first_grad, axis=0)
    input_grad = middle_grad + norm_back(first_grad, unit_one, scale_one, ln1_gain)
    qkv_total, out_total = (
        lax.psum_scatter(
            qkv_wgrad.astype(jnp.bfloat16), "dp", scatter_dimension=0, tiled=True
        ).astype(jnp.float32),
        lax.psum_scatter(
            out_wgrad_local.astype(jnp.bfloat16), "dp", scatter_dimension=1, tiled=True
        ).astype(jnp.float32),
    )
    norm_sums = lax.psum(
        (gain_one_grad, bias_one_grad, gain_two_grad, bias_two_grad), ("dp", "tensor")
    )
    return (
        mixed_out.astype(jnp.bfloat16),
        input_grad.astype(jnp.bfloat16),
        norm_sums[0],
        norm_sums[1],
        qkv_total,
        out_total,
        norm_sums[2],
        norm_sums[3],
        grad_expert_in,
        grad_expert_out,
    )


def solution(mesh):
    placed = (
        P(("dp", "tensor"), None),
        P(("dp", "tensor")),
        P(),
        P(),
        P(),
        P("dp", "tensor", None),
        P("tensor", "dp"),
        P(),
        P(),
        P("dp", None, "tensor"),
        P("dp", "tensor", None),
        P(("dp", "tensor"), None),
    )
    return jax.shard_map(
        on_device,
        mesh=mesh,
        in_specs=placed,
        out_specs=(
            P(("dp", "tensor"), None),
            P(("dp", "tensor"), None),
            P(),
            P(),
            P("dp", "tensor", None),
            P("tensor", "dp"),
            P(),
            P(),
            P("dp", None, "tensor"),
            P("dp", "tensor", None),
        ),
        check_vma=False,
    )
```

profile of v0, /device:TPU:0, one launch (start us, length us, event | category | flops | bytes accessed | tf_op | source)
XLA Modules:
  0.0 1204.0 jit_solution(15293700236437319940)
XLA Ops:
  13.0 14.6 %all_gather.19 = bf16[768,3,192]{2,1,0:T(4,128)(2,1)S(1)} all-gather(bf16[96,3,192]{2,1,0:T(4,128)(2,1)S(1)} %copy.72), channel_id=1, replica_groups=mesh['dp'=8,'tensor'=4] {'dp'}, dimensions={0}, use_global_device_ids=true | all-gather | bytes 995328 | tf_op jit(solution)/shard_map/all_gather | solution.py:117
  28.5 9.6 all_gather.20
  38.1 40.8 %all-gather.5.cloned.1.call-done = bf16[2048,768]{1,0:T(8,128)(2,1)} async-done(((bf16[512,768]{1,0:T(8,128)(2,1)}), bf16[2048,768]{1,0:T(8,128)(2,1)}) %all-gather.5.cloned.1.call-update) | async-done | bytes 3145744 | tf_op jit(solution)/shard_map/all_gather | solution.py:125
  79.0 5.3 convolution_convert_fusion.2
  84.3 5.9 reshape.233
  92.3 29.1 %while.22 = (s32[]{:T(128)}, bf16[2,1024,3,64]{1,3,2,0:T(8,128)(2,1)}, f32[2,3,1024]{2,1,0:T(4,128)S(1)}, bf16[2,1024,3,3,64]{1,4,2,3,0:T(8,128)(2,1)}, s32[]{:T(128)}) while((s32[]{:T(128)}, bf16[2,1024,3,64]{1,3,2,0:T(8,128)(2,1)}, f32[2,3,1024]{2,1,0:T(4,128)S(1)}, bf16[2,1024,3,3,64]{1,4,2,3,0:T(8,128)(2,1)}, s32[]{:T(128)}) %tuple.61), condition=%wide.region_5.6_spmd, body=%wide.region_2.5_spmd.sunk | while | flops 844297216 | bytes 54898824 | solution.py:131
  97.1 3.9 fusion.134
  100.9 5.9 fusion.135
  111.6 3.9 fusion.134
  115.5 5.9 fusion.135
  127.3 4.0 convert_element_type.136
  131.4 4.4 convert_element_type.138
  141.1 45.2 %reduce-scatter.9.cloned.1.call-done = bf16[512,768]{1,0:T(8,128)(2,1)} async-done(((bf16[2048,768]{1,0:T(8,128)(2,1)}), bf16[512,768]{1,0:T(8,128)(2,1)}) %reduce-scatter.9.cloned.1.call-update) | async-done | bytes 786448 | tf_op jit(solution)/shard_map/reduce_scatter | solution.py:133
  189.4 4.1 scatter_custom_fusion
  197.2 4.5 scatter_custom_fusion.1
  201.7 16.5 %all-to-all-done = bf16[8,128,768]{2,1,0:T(8,128)(2,1)S(1)} async-done(((bf16[8,128,768]{2,1,0:T(8,128)(2,1)}), bf16[8,128,768]{2,1,0:T(8,128)(2,1)S(1)}, u32[]{:S(2)}, u32[]{:S(2)}) %all-to-all-start) | async-done | bytes 1572896 | tf_op jit(solution)/shard_map/all_to_all | solution.py:164
  218.2 4.3 all-to-all-start.2
  222.5 132.8 %all-gather.7.cloned.1.call-done = bf16[2,768,3072]{2,1,0:T(8,128)(2,1)} async-done(((bf16[2,768,768]{2,1,0:T(8,128)(2,1)}), bf16[2,768,3072]{2,1,0:T(8,128)(2,1)}) %all-gather.7.cloned.1.call-update) | async-done | bytes 9437200 | tf_op jit(solution)/shard_map/all_gather | solution.py:175
  355.3 12.2 %fusion.46 = f32[2,8,64,3072]{3,2,1,0:T(8,128)} fusion(bf16[2,768,3072]{2,1,0:T(8,128)(2,1)} %all-gather.7.cloned.1.call-done, bf16[8,2,64,768]{3,2,1,0:T(8,128)(2,1)S(1)} %bitcast.236), kind=kOutput, calls=%fused_computation.74 | convolution fusion | flops 4831838208 | bytes 23592960 | tf_op jit(solution)/shard_map/secd,edf->secf/dot_general | solution.py:179
  367.5 154.3 %all-gather.9.cloned.1.call-done = bf16[2,3072,768]{2,1,0:T(8,128)(2,1)} async-done(((bf16[2,768,768]{2,1,0:T(8,128)(2,1)}), bf16[2,3072,768]{2,1,0:T(8,128)(2,1)}) %all-gather.9.cloned.1.call-update) | async-done | bytes 9437200 | tf_op jit(solution)/shard_map/all_gather | solution.py:176
  521.7 11.5 fusion.89
  534.5 3.9 all-to-all-start.1
  538.4 17.5 %fusion.39 = bf16[8,2,64,3072]{3,2,0,1:T(8,128)(2,1)} fusion(f32[2,8,64,3072]{3,2,1,0:T(8,128)} %fusion.46, bf16[2,3072,768]{2,1,0:T(8,128)(2,1)} %all-gather.9.cloned.1.call-done, bf16[8,2,64,768]{3,2,1,0:T(8,128)(2,1)} %bitcast.33), kind=kOutput, calls=%fused_computation.64 | convolution fusion | flops 4894752768 | bytes 29884416 | tf_op jit(solution)/shard_map/secd,efd->secf/dot_general | solution.py:86
  555.8 9.9 fusion.86
  567.1 4.3 all-to-all-start.3
  574.2 18.2 %all-to-all-done.3 = bf16[8,128,768]{2,1,0:T(8,128)(2,1)} async-done(((bf16[8,128,768]{2,1,0:T(8,128)(2,1)}), bf16[8,128,768]{2,1,0:T(8,128)(2,1)}, u32[]{:S(2)}, u32[]{:S(2)}) %all-to-all-start.3) | async-done | bytes 1572896 | tf_op jit(solution)/shard_map/all_to_all | solution.py:201
  592.4 4.0 gather_fusion.2
  598.3 4.9 fusion.106
  603.5 59.8 %all-gather.11.cloned.1.call-done = bf16[2048,768]{1,0:T(8,128)(2,1)} async-done(((bf16[512,768]{1,0:T(8,128)(2,1)}), bf16[2048,768]{1,0:T(8,128)(2,1)}) %all-gather.11.cloned.1.call-update) | async-done | bytes 3145744 | tf_op jit(solution)/shard_map/all_gather | solution.py:206
  667.2 52.4 %while.23 = (s32[]{:T(128)}, bf16[2,1024,3,3,64]{1,4,2,3,0:T(8,128)(2,1)}, bf16[2,1024,3,3,64]{1,4,2,3,0:T(8,128)(2,1)}, f32[2,3,1024]{2,1,0:T(4,128)S(1)}, bf16[2,1024,3,64]{1,3,2,0:T(8,128)(2,1)S(1)}, /*index=5*/s32[]{:T(128)}) while((s32[]{:T(128)}, bf16[2,1024,3,3,64]{1,4,2,3,0:T(8,128)(2,1)}, bf16[2,1024,3,3,64]{1,4,2,3,0:T(8,128)(2,1)}, ...), condition=%wide.region_18.20_spmd, body=%wide.region_16.19_spmd.sunk | while | flops 2066019328 | bytes 126185616 | solution.py:214
  670.8 3.7 fusion.141
  674.5 7.1 multiply_reduce_fusion.5
  681.6 6.8 multiply_convert_fusion.2
  696.8 3.7 fusion.141
  700.5 7.1 multiply_reduce_fusion.5
  707.6 6.8 multiply_convert_fusion.2
  719.6 4.1 copy.84
  727.6 5.7 fusion.83
  733.4 4.1 convolution_convert_fusion
  738.8 10.4 bitcast_convert_fusion.1
  749.3 12.3 %bitcast_convert_fusion = bf16[2,3072,768]{2,1,0:T(8,128)(2,1)} fusion(bf16[8,2,64,768]{3,2,1,0:T(8,128)(2,1)} %bitcast.33, f32[2,8,64,3072]{3,2,1,0:T(8,128)} %fusion.46), kind=kOutput, calls=%fused_computation.54 | convolution fusion | flops 4864868352 | bytes 23592960 | tf_op jit(solution)/shard_map/secf,secd->efd/dot_general | solution.py:89
  763.5 36.7 %reduce-scatter.13.cloned.1.call-done = bf16[96,3,192]{2,0,1:T(8,128)(2,1)} async-done(((bf16[768,3,192]{2,0,1:T(8,128)(2,1)}), bf16[96,3,192]{2,0,1:T(8,128)(2,1)}) %reduce-scatter.13.cloned.1.call-update) | async-done | bytes 110608 | tf_op jit(solution)/shard_map/reduce_scatter | solution.py:230
  801.8 61.6 %reduce-scatter.11.cloned.1.call-done = bf16[512,768]{1,0:T(8,128)(2,1)} async-done(((bf16[2048,768]{1,0:T(8,128)(2,1)}), bf16[512,768]{1,0:T(8,128)(2,1)}) %reduce-scatter.11.cloned.1.call-update) | async-done | bytes 786448 | tf_op jit(solution)/shard_map/reduce_scatter | solution.py:218
  865.4 44.4 %all-reduce = (f32[768]{0:T(1024)}, f32[768]{0:T(1024)}, f32[768]{0:T(1024)}, f32[768]{0:T(1024)}) all-reduce(f32[768]{0:T(1024)S(1)} %get-tuple-element.102, f32[768]{0:T(1024)S(1)} %get-tuple-element.107, f32[768]{0:T(1024)S(1)} %copy-done.27, f32[768]{0:T(1024)S(1)} %copy-done.28), channel_id=1, replica_groups=mesh['dp'=8,'tensor'=4] {'dp','tensor'}, use_global_device_ids=true, to_apply=%region_23.25 | all-reduce | flops 3072 | bytes 24576 | tf_op jit(solution)/shard_map/psum | solution.py:237
  912.4 115.8 %reduce-scatter.15.cloned.1.call-done = bf16[2,768,768]{2,1,0:T(8,128)(2,1)} async-done(((bf16[2,768,3072]{2,1,0:T(8,128)(2,1)}), bf16[2,768,768]{2,1,0:T(8,128)(2,1)}) %reduce-scatter.15.cloned.1.call-update) | async-done | bytes 2359312 | tf_op jit(solution)/shard_map/reduce_scatter | solution.py:192
  1028.2 4.3 convert_element_type.158
  1032.5 160.2 %reduce-scatter.17.cloned.1.call-done = bf16[2,768,768]{2,1,0:T(8,128)(2,1)} async-done(((bf16[2,3072,768]{2,1,0:T(8,128)(2,1)}), bf16[2,768,768]{2,1,0:T(8,128)(2,1)}) %reduce-scatter.17.cloned.1.call-update) | async-done | bytes 2359312 | tf_op jit(solution)/shard_map/reduce_scatter | solution.py:195
  1192.7 4.2 convert_element_type.160
  (167 shorter events, 77.4 us)
Async XLA Ops:
  7.2 128.7 %copy-start = (s32[50257]{0:T(1024)S(1)}, s32[50257]{0:T(1024)}, u32[]{:S(2)}) copy-start(s32[50257]{0:T(1024)} %param.20) | copy-start | bytes 603088
  7.2 5.5 copy-start.20
  7.2 5.6 copy-start.19
  7.2 71.7 %all-gather.5.cloned.1.call-start = ((), (), s32[]{:S(2)}) async-start(), calls=%async_computation.10 | async-start | bytes 3932160 | tf_op jit(solution)/shard_map/all_gather | solution.py:125
  8.7 4.2 copy-start.21
  10.2 2.6 copy-start.25
  12.6 173.7 %reduce-scatter.9.cloned.1.call-start = ((), (), s32[]{:S(2)}) async-start(), calls=%async_computation.11 | async-start | bytes 3932160 | tf_op jit(solution)/shard_map/reduce_scatter | solution.py:133
  28.5 50.5 %copy-start.17 = (bf16[768,3,192]{0,2,1:T(8,128)(2,1)}, bf16[768,3,192]{0,2,1:T(8,128)(2,1)S(1)}, u32[]{:S(2)}) copy-start(bf16[768,3,192]{0,2,1:T(8,128)(2,1)S(1)} %copy.73) | copy-start | bytes 2654212
  92.6 4.4 copy-start.2
  94.4 2.7 copy-start.5
  107.2 4.4 copy-start.2
  108.9 2.6 copy-start.5
  121.4 3.1 copy-start.11
  127.3 228.1 %all-gather.7.cloned.1.call-start = ((), (), s32[]{:S(2)}) async-start(), calls=%async_computation.12 | async-start | bytes 11796480 | tf_op jit(solution)/shard_map/all_gather | solution.py:175
  131.3 4.5 copy-start.29
  131.3 390.4 %all-gather.9.cloned.1.call-start = ((), (), s32[]{:S(2)}) async-start(), calls=%async_computation.13 | async-start | bytes 11796480 | tf_op jit(solution)/shard_map/all_gather | solution.py:176
  135.8 50.6 %copy-start.3 = (bf16[512,768]{1,0:T(8,128)(2,1)S(1)}, bf16[512,768]{1,0:T(8,128)(2,1)}, u32[]{:S(2)}) copy-start(bf16[512,768]{1,0:T(8,128)(2,1)} %param.18) | copy-start | bytes 2359300
  135.8 53.6 %copy-start.23 = (f32[768]{0:T(1024)S(1)}, f32[768]{0:T(1024)}, u32[]{:S(2)}) copy-start(f32[768]{0:T(1024)} %param.25) | copy-start | bytes 9220
  135.8 53.6 %copy-start.30 = (f32[768]{0:T(1024)S(1)}, f32[768]{0:T(1024)}, u32[]{:S(2)}) copy-start(f32[768]{0:T(1024)} %param.26) | copy-start | bytes 9220
  186.3 3.1 copy-start.6
  193.5 24.7 %all-to-all-start = ((bf16[8,128,768]{2,1,0:T(8,128)(2,1)}), bf16[8,128,768]{2,1,0:T(8,128)(2,1)S(1)}, u32[]{:S(2)}, u32[]{:S(2)}) async-start(bf16[8,128,768]{2,1,0:T(8,128)(2,1)} %bitcast.22), calls=%async_computation.1 | async-start | bytes 3145728 | tf_op jit(solution)/shard_map/all_to_all | solution.py:164
  218.2 149.3 %copy-start.15 = (bf16[8,128,768]{2,1,0:T(8,128)(2,1)}, bf16[8,128,768]{2,1,0:T(8,128)(2,1)S(1)}, u32[]{:S(2)}) copy-start(bf16[8,128,768]{2,1,0:T(8,128)(2,1)S(1)} %all-to-all-done) | copy-start | bytes 4718596
  218.2 316.3 %all-to-all-start.2 = ((bf16[8,128,768]{2,1,0:T(8,128)(2,1)}), bf16[8,128,768]{2,1,0:T(8,128)(2,1)}, u32[]{:S(2)}, u32[]{:S(2)}) async-start(bf16[8,128,768]{2,1,0:T(8,128)(2,1)} %bitcast.32), calls=%async_computation.3 | async-start | bytes 3145728 | tf_op jit(solution)/shard_map/all_to_all | solution.py:171
  534.5 32.6 %all-to-all-start.1 = ((bf16[8,128,768]{2,1,0:T(8,128)(2,1)}), bf16[8,128,768]{2,1,0:T(8,128)(2,1)S(1)}, u32[]{:S(2)}, u32[]{:S(2)}) async-start(bf16[8,128,768]{2,1,0:T(8,128)(2,1)} %bitcast.232), calls=%async_computation.2 | async-start | bytes 3145728 | tf_op jit(solution)/shard_map/all_to_all | solution.py:199
  567.1 25.4 %all-to-all-start.3 = ((bf16[8,128,768]{2,1,0:T(8,128)(2,1)}), bf16[8,128,768]{2,1,0:T(8,128)(2,1)}, u32[]{:S(2)}, u32[]{:S(2)}) async-start(bf16[8,128,768]{2,1,0:T(8,128)(2,1)} %bitcast.231), calls=%async_computation.4 | async-start | bytes 3145728 | tf_op jit(solution)/shard_map/all_to_all | solution.py:201
  571.4 91.9 %all-gather.11.cloned.1.call-start = ((), (), s32[]{:S(2)}) async-start(), calls=%async_computation.14 | async-start | bytes 3932160 | tf_op jit(solution)/shard_map/all_gather | solution.py:206
  598.3 65.0 %copy-start.12 = (bf16[192,768]{0,1:T(8,128)(2,1)S(1)}, bf16[192,768]{0,1:T(8,128)(2,1)}, u32[]{:S(2)}) copy-start(bf16[192,768]{0,1:T(8,128)(2,1)} %all_gather.20) | copy-start | bytes 884740
  603.3 158.5 %reduce-scatter.19.cloned.1.call-start = ((), (), s32[]{:S(2)}) async-start(), calls=%async_computation.19 | async-start | bytes 442368
  689.6 2.0 copy-start.13
  691.8 1.4 copy-start.14
  715.6 2.0 copy-start.13
  717.8 1.4 copy-start.14
  723.7 1.9 copy-start.7
  723.7 2.1 copy-start.9
  727.5 72.6 %reduce-scatter.13.cloned.1.call-start = ((), (), s32[]{:S(2)}) async-start(), calls=%async_computation.16 | async-start | bytes 1327104 | tf_op jit(solution)/shard_map/reduce_scatter | solution.py:230
  727.6 5.8 copy-start.18
  733.3 130.1 %reduce-scatter.11.cloned.1.call-start = ((), (), s32[]{:S(2)}) async-start(), calls=%async_computation.15 | async-start | bytes 3932160 | tf_op jit(solution)/shard_map/reduce_scatter | solution.py:218
  737.4 1.4 copy-start.16
  737.4 290.8 %reduce-scatter.15.cloned.1.call-start = ((), (), s32[]{:S(2)}) async-start(), calls=%async_computation.17 | async-start | bytes 11796480 | tf_op jit(solution)/shard_map/reduce_scatter | solution.py:192
  749.3 443.4 %reduce-scatter.17.cloned.1.call-start = ((), (), s32[]{:S(2)}) async-start(), calls=%async_computation.18 | async-start | bytes 11796480 | tf_op jit(solution)/shard_map/reduce_scatter | solution.py:195
  761.6 101.8 %copy-start.4 = (bf16[512,768]{1,0:T(8,128)(2,1)S(1)}, bf16[512,768]{1,0:T(8,128)(2,1)}, u32[]{:S(2)}) copy-start(bf16[512,768]{1,0:T(8,128)(2,1)} %param.18) | copy-start | bytes 2359300
  761.6 101.8 %copy-start.22 = (f32[512]{0:T(512)S(1)}, f32[512]{0:T(512)}, u32[]{:S(2)}) copy-start(f32[512]{0:T(512)} %copy-done.21) | copy-start | bytes 6148
  761.6 101.8 %copy-start.24 = (f32[768]{0:T(1024)S(1)}, f32[768]{0:T(1024)}, u32[]{:S(2)}) copy-start(f32[768]{0:T(1024)} %param.21) | copy-start | bytes 9220
  761.6 101.8 %copy-start.26 = (f32[512]{0:T(512)S(1)}, f32[512]{0:T(512)}, u32[]{:S(2)}) copy-start(f32[512]{0:T(512)} %copy-done.25) | copy-start | bytes 6148
  761.7 103.8 %copy-start.27 = (f32[768]{0:T(1024)S(1)}, f32[768]{0:T(1024)}, u32[]{:S(2)}) copy-start(f32[768]{0:T(1024)} %get-tuple-element.100) | copy-start | bytes 9220
  761.7 103.8 %copy-start.28 = (f32[768]{0:T(1024)S(1)}, f32[768]{0:T(1024)}, u32[]{:S(2)}) copy-start(f32[768]{0:T(1024)} %get-tuple-element.106) | copy-start | bytes 9220
  761.7 148.1 %copy-start.10 = (f32[512,768]{1,0:T(8,128)S(1)}, f32[512,768]{1,0:T(8,128)}, u32[]{:S(2)}) copy-start(f32[512,768]{1,0:T(8,128)} %get-tuple-element.131) | copy-start | bytes 4718596
  1028.2 168.7 %copy-start.1 = (s32[50257]{0:T(1024)S(1)}, s32[50257]{0:T(1024)}, u32[]{:S(2)}) copy-start(s32[50257]{0:T(1024)} %param.20) | copy-start | bytes 603088
  (1 other events, 0.9 us)
Sparse Core Ops, SparseCore 0:
  12.7 66.1 all-gather.4
  127.4 58.8 reduce-scatter.8
  188.5 166.7 all-gather.6
  356.7 164.9 all-gather.8
  603.4 59.8 all-gather.10
  727.7 32.4 reduce-scatter.18
  763.4 36.7 reduce-scatter.12
  803.2 60.2 reduce-scatter.10
  865.9 162.2 reduce-scatter.14
  1030.6 162.1 reduce-scatter.16
where the time goes:
time: 1210 us; the launch traced here: 1200 us
  waiting for transfers between devices  842 us (70%)
  matrix products  144 us (12%)
  blocking collectives  68.6 us (6%)
  other arithmetic  67.2 us (6%)
  local copies, waits for them, and re-layouts  49.4 us (4%)
  starting transfers between devices  16.8 us (1%)
  between operations  14.9 us (1%)
    reduce_scatter x1, waiting for transfers between devices, on_device(): lax.psum_scatter(out_wgrad.astype(jnp.bfloat16), 'tensor', scatter_dimens...  160 us
    all_gather x1, waiting for transfers between devices, on_device(): lax.all_gather(expert_out.astype(jnp.bfloat16), 'tensor', axis=1, tiled=T...  154 us
    all_gather x1, waiting for transfers between devices, on_device(): lax.all_gather(expert_in.astype(jnp.bfloat16), 'tensor', axis=2, tiled=True)  133 us
    reduce_scatter x1, waiting for transfers between devices, on_device(): lax.psum_scatter(in_wgrad.astype(jnp.bfloat16), 'tensor', scatter_dimensi...  116 us
    reduce_scatter x1, waiting for transfers between devices, on_device(): lax.psum_scatter(jnp.einsum('tk,dk->td', qkv_grad, qkv_flat, preferred_el...  61.6 us
    all_gather x1, waiting for transfers between devices, on_device(): lax.all_gather(middle_grad.astype(jnp.bfloat16), 'tensor', axis=0, tiled=...  59.8 us
    reduce_scatter x1, waiting for transfers between devices, on_device(): lax.psum_scatter(jnp.dot(mixed_flat, out_weight, preferred_element_type=j...  45.2 us
    psum x1, blocking collectives, on_device(): lax.psum((gain_one_grad, bias_one_grad, gain_two_grad, bias_two_grad), ('...  44.4 us
  transfers between devices with their start and end apart: 14, of which 11 were waited for; matrix products, arithmetic and copies ran while one was open for 11% of the time, Pallas kernels for 0%

commit v1 on v0

--- a/solution.py
+++ b/solution.py
@@ -145,7 +145,12 @@
     one_hot = (expert_of[:, None] == jnp.arange(experts_total, dtype=jnp.int32)[None, :]).astype(
         jnp.int32
     )
-    slot_rank = jnp.sum((jnp.cumsum(one_hot, axis=0) - 1) * one_hot, axis=1)
+    before = (
+        lax.broadcasted_iota(jnp.int32, (row_count, row_count), 0)
+        > lax.broadcasted_iota(jnp.int32, (row_count, row_count), 1)
+    ).astype(jnp.bfloat16)
+    earlier = jnp.dot(before, one_hot.astype(jnp.bfloat16), preferred_element_type=jnp.float32)
+    slot_rank = jnp.sum(earlier.astype(jnp.int32) * one_hot, axis=1)
     kept_rows = slot_rank < capacity
     target = jnp.where(kept_rows, expert_of * capacity + slot_rank, slot_count)
     source_row = jnp.minimum(target, slot_count - 1)

time: 1210 us -> 1210 us (level)
  transfers between devices with their start and end apart: 14 -> 14, of which waited for: 11 -> 11; matrix products, arithmetic and copies ran while one was open for 11% -> 10% of each run, Pallas kernels for 0% -> 0%
where the time goes in v1:
time: 1210 us; the launch traced here: 1200 us
  waiting for transfers between devices  844 us (70%)
  matrix products  144 us (12%)
  blocking collectives  68.6 us (6%)
  other arithmetic  65.9 us (5%)
  local copies, waits for them, and re-layouts  49.2 us (4%)
  starting transfers between devices  16.7 us (1%)
  between operations  14.9 us (1%)
    reduce_scatter x1, waiting for transfers between devices, on_device(): lax.psum_scatter(out_wgrad.astype(jnp.bfloat16), 'tensor', scatter_dimens...  160 us
    all_gather x1, waiting for transfers between devices, on_device(): lax.all_gather(expert_out.astype(jnp.bfloat16), 'tensor', axis=1, tiled=T...  154 us
    all_gather x1, waiting for transfers between devices, on_device(): lax.all_gather(expert_in.astype(jnp.bfloat16), 'tensor', axis=2, tiled=True)  133 us
    reduce_scatter x1, waiting for transfers between devices, on_device(): lax.psum_scatter(in_wgrad.astype(jnp.bfloat16), 'tensor', scatter_dimensi...  116 us
    reduce_scatter x1, waiting for transfers between devices, on_device(): lax.psum_scatter(jnp.einsum('tk,dk->td', qkv_grad, qkv_flat, preferred_el...  61.6 us
    all_gather x1, waiting for transfers between devices, on_device(): lax.all_gather(middle_grad.astype(jnp.bfloat16), 'tensor', axis=0, tiled=...  59.8 us
    reduce_scatter x1, waiting for transfers between devices, on_device(): lax.psum_scatter(jnp.dot(mixed_flat, out_weight, preferred_element_type=j...  46.5 us
    psum x1, blocking collectives, on_device(): lax.psum((gain_one_grad, bias_one_grad, gain_two_grad, bias_two_grad), ('...  44.4 us
  transfers between devices with their start and end apart: 14, of which 11 were waited for; matrix products, arithmetic and copies ran while one was open for 10% of the time, Pallas kernels for 0%

profile of v1, /device:TPU:0, one launch (start us, length us, event | category | flops | bytes accessed | tf_op | source)
XLA Modules:
  0.0 1204.0 jit_solution(7400843623638007741)
XLA Ops:
  13.0 14.6 %all_gather.19 = bf16[768,3,192]{2,1,0:T(4,128)(2,1)S(1)} all-gather(bf16[96,3,192]{2,1,0:T(4,128)(2,1)S(1)} %copy.70), channel_id=1, replica_groups=mesh['dp'=8,'tensor'=4] {'dp'}, dimensions={0}, use_global_device_ids=true | all-gather | bytes 995328 | tf_op jit(solution)/shard_map/all_gather | solution.py:117
  28.5 9.7 all_gather.20
  38.1 40.8 %all-gather.5.cloned.1.call-done = bf16[2048,768]{1,0:T(8,128)(2,1)} async-done(((bf16[512,768]{1,0:T(8,128)(2,1)}), bf16[2048,768]{1,0:T(8,128)(2,1)}) %all-gather.5.cloned.1.call-update) | async-done | bytes 3145744 | tf_op jit(solution)/shard_map/all_gather | solution.py:125
  79.0 5.3 convolution_convert_fusion.2
  84.3 5.9 reshape.214
  92.3 29.1 %while.22 = (s32[]{:T(128)}, bf16[2,1024,3,64]{1,3,2,0:T(8,128)(2,1)}, f32[2,3,1024]{2,1,0:T(4,128)S(1)}, bf16[2,1024,3,3,64]{1,4,2,3,0:T(8,128)(2,1)}, s32[]{:T(128)}) while((s32[]{:T(128)}, bf16[2,1024,3,64]{1,3,2,0:T(8,128)(2,1)}, f32[2,3,1024]{2,1,0:T(4,128)S(1)}, bf16[2,1024,3,3,64]{1,4,2,3,0:T(8,128)(2,1)}, s32[]{:T(128)}) %tuple.61), condition=%wide.region_5.6_spmd, body=%wide.region_2.5_spmd.sunk | while | flops 844297216 | bytes 54898824 | solution.py:131
  97.1 3.9 fusion.134
  100.9 5.9 fusion.135
  111.6 3.9 fusion.134
  115.5 5.9 fusion.135
  127.3 4.0 convert_element_type.143
  131.4 4.4 convert_element_type.145
  139.8 46.5 %reduce-scatter.9.cloned.1.call-done = bf16[512,768]{1,0:T(8,128)(2,1)} async-done(((bf16[2048,768]{1,0:T(8,128)(2,1)}), bf16[512,768]{1,0:T(8,128)(2,1)}) %reduce-scatter.9.cloned.1.call-update) | async-done | bytes 786448 | tf_op jit(solution)/shard_map/reduce_scatter | solution.py:133
  189.4 4.1 scatter_custom_fusion
  197.2 4.5 scatter_custom_fusion.1
  201.7 16.5 %all-to-all-done = bf16[8,128,768]{2,1,0:T(8,128)(2,1)S(1)} async-done(((bf16[8,128,768]{2,1,0:T(8,128)(2,1)}), bf16[8,128,768]{2,1,0:T(8,128)(2,1)S(1)}, u32[]{:S(2)}, u32[]{:S(2)}) %all-to-all-start) | async-done | bytes 1572896 | tf_op jit(solution)/shard_map/all_to_all | solution.py:169
  218.2 4.3 all-to-all-start.2
  222.5 132.8 %all-gather.7.cloned.1.call-done = bf16[2,768,3072]{2,1,0:T(8,128)(2,1)} async-done(((bf16[2,768,768]{2,1,0:T(8,128)(2,1)}), bf16[2,768,3072]{2,1,0:T(8,128)(2,1)}) %all-gather.7.cloned.1.call-update) | async-done | bytes 9437200 | tf_op jit(solution)/shard_map/all_gather | solution.py:180
  355.3 12.2 %fusion.46 = f32[2,8,64,3072]{3,2,1,0:T(8,128)} fusion(bf16[2,768,3072]{2,1,0:T(8,128)(2,1)} %all-gather.7.cloned.1.call-done, bf16[8,2,64,768]{3,2,1,0:T(8,128)(2,1)S(1)} %bitcast.220), kind=kOutput, calls=%fused_computation.74 | convolution fusion | flops 4831838208 | bytes 23592960 | tf_op jit(solution)/shard_map/secd,edf->secf/dot_general | solution.py:184
  367.5 154.2 %all-gather.9.cloned.1.call-done = bf16[2,3072,768]{2,1,0:T(8,128)(2,1)} async-done(((bf16[2,768,768]{2,1,0:T(8,128)(2,1)}), bf16[2,3072,768]{2,1,0:T(8,128)(2,1)}) %all-gather.9.cloned.1.call-update) | async-done | bytes 9437200 | tf_op jit(solution)/shard_map/all_gather | solution.py:181
  521.7 11.5 fusion.89
  534.5 3.8 all-to-all-start.1
  538.3 17.5 %fusion.39 = bf16[8,2,64,3072]{3,2,0,1:T(8,128)(2,1)} fusion(f32[2,8,64,3072]{3,2,1,0:T(8,128)} %fusion.46, bf16[2,3072,768]{2,1,0:T(8,128)(2,1)} %all-gather.9.cloned.1.call-done, bf16[8,2,64,768]{3,2,1,0:T(8,128)(2,1)} %bitcast.31), kind=kOutput, calls=%fused_computation.64 | convolution fusion | flops 4894752768 | bytes 29884416 | tf_op jit(solution)/shard_map/secd,efd->secf/dot_general | solution.py:86
  555.8 9.9 fusion.86
  567.1 4.3 all-to-all-start.3
  574.2 18.2 %all-to-all-done.3 = bf16[8,128,768]{2,1,0:T(8,128)(2,1)} async-done(((bf16[8,128,768]{2,1,0:T(8,128)(2,1)}), bf16[8,128,768]{2,1,0:T(8,128)(2,1)}, u32[]{:S(2)}, u32[]{:S(2)}) %all-to-all-start.3) | async-done | bytes 1572896 | tf_op jit(solution)/shard_map/all_to_all | solution.py:206
  592.4 4.0 gather_fusion.2
  598.3 4.9 fusion.106
  603.5 59.8 %all-gather.11.cloned.1.call-done = bf16[2048,768]{1,0:T(8,128)(2,1)} async-done(((bf16[512,768]{1,0:T(8,128)(2,1)}), bf16[2048,768]{1,0:T(8,128)(2,1)}) %all-gather.11.cloned.1.call-update) | async-done | bytes 3145744 | tf_op jit(solution)/shard_map/all_gather | solution.py:211
  667.2 52.4 %while.23 = (s32[]{:T(128)}, bf16[2,1024,3,3,64]{1,4,2,3,0:T(8,128)(2,1)}, bf16[2,1024,3,3,64]{1,4,2,3,0:T(8,128)(2,1)}, f32[2,3,1024]{2,1,0:T(4,128)S(1)}, bf16[2,1024,3,64]{1,3,2,0:T(8,128)(2,1)S(1)}, /*index=5*/s32[]{:T(128)}) while((s32[]{:T(128)}, bf16[2,1024,3,3,64]{1,4,2,3,0:T(8,128)(2,1)}, bf16[2,1024,3,3,64]{1,4,2,3,0:T(8,128)(2,1)}, ...), condition=%wide.region_16.18_spmd, body=%wide.region_14.17_spmd.sunk | while | flops 2066019328 | bytes 126185616 | solution.py:219
  670.8 3.7 fusion.141
  674.5 7.1 multiply_reduce_fusion.5
  681.6 6.8 multiply_convert_fusion.2
  696.8 3.7 fusion.141
  700.5 7.1 multiply_reduce_fusion.5
  707.6 6.8 multiply_convert_fusion.2
  719.6 4.1 copy.81
  727.6 5.7 fusion.83
  733.4 4.0 convolution_convert_fusion
  738.9 10.4 bitcast_convert_fusion.1
  749.3 12.3 %bitcast_convert_fusion = bf16[2,3072,768]{2,1,0:T(8,128)(2,1)} fusion(bf16[8,2,64,768]{3,2,1,0:T(8,128)(2,1)} %bitcast.31, f32[2,8,64,3072]{3,2,1,0:T(8,128)} %fusion.46), kind=kOutput, calls=%fused_computation.54 | convolution fusion | flops 4864868352 | bytes 23592960 | tf_op jit(solution)/shard_map/secf,secd->efd/dot_general | solution.py:89
  763.4 36.8 %reduce-scatter.13.cloned.1.call-done = bf16[96,3,192]{2,0,1:T(8,128)(2,1)} async-done(((bf16[768,3,192]{2,0,1:T(8,128)(2,1)}), bf16[96,3,192]{2,0,1:T(8,128)(2,1)}) %reduce-scatter.13.cloned.1.call-update) | async-done | bytes 110608 | tf_op jit(solution)/shard_map/reduce_scatter | solution.py:235
  801.8 61.6 %reduce-scatter.11.cloned.1.call-done = bf16[512,768]{1,0:T(8,128)(2,1)} async-done(((bf16[2048,768]{1,0:T(8,128)(2,1)}), bf16[512,768]{1,0:T(8,128)(2,1)}) %reduce-scatter.11.cloned.1.call-update) | async-done | bytes 786448 | tf_op jit(solution)/shard_map/reduce_scatter | solution.py:223
  865.5 44.4 %all-reduce = (f32[768]{0:T(1024)}, f32[768]{0:T(1024)}, f32[768]{0:T(1024)}, f32[768]{0:T(1024)}) all-reduce(f32[768]{0:T(1024)S(1)} %get-tuple-element.102, f32[768]{0:T(1024)S(1)} %get-tuple-element.107, f32[768]{0:T(1024)S(1)} %copy-done.27, f32[768]{0:T(1024)S(1)} %copy-done.28), channel_id=1, replica_groups=mesh['dp'=8,'tensor'=4] {'dp','tensor'}, use_global_device_ids=true, to_apply=%region_21.23 | all-reduce | flops 3072 | bytes 24576 | tf_op jit(solution)/shard_map/psum | solution.py:242
  912.5 115.8 %reduce-scatter.15.cloned.1.call-done = bf16[2,768,768]{2,1,0:T(8,128)(2,1)} async-done(((bf16[2,768,3072]{2,1,0:T(8,128)(2,1)}), bf16[2,768,768]{2,1,0:T(8,128)(2,1)}) %reduce-scatter.15.cloned.1.call-update) | async-done | bytes 2359312 | tf_op jit(solution)/shard_map/reduce_scatter | solution.py:197
  1028.2 4.3 convert_element_type.165
  1032.5 160.2 %reduce-scatter.17.cloned.1.call-done = bf16[2,768,768]{2,1,0:T(8,128)(2,1)} async-done(((bf16[2,3072,768]{2,1,0:T(8,128)(2,1)}), bf16[2,768,768]{2,1,0:T(8,128)(2,1)}) %reduce-scatter.17.cloned.1.call-update) | async-done | bytes 2359312 | tf_op jit(solution)/shard_map/reduce_scatter | solution.py:200
  1192.7 4.2 convert_element_type.167
  (162 shorter events, 76.1 us)
Async XLA Ops:
  7.2 128.7 %copy-start = (s32[50257]{0:T(1024)S(1)}, s32[50257]{0:T(1024)}, u32[]{:S(2)}) copy-start(s32[50257]{0:T(1024)} %param.20) | copy-start | bytes 603088
  7.2 5.5 copy-start.20
  7.2 5.6 copy-start.19
  7.2 71.7 %all-gather.5.cloned.1.call-start = ((), (), s32[]{:S(2)}) async-start(), calls=%async_computation.10 | async-start | bytes 3932160 | tf_op jit(solution)/shard_map/all_gather | solution.py:125
  8.7 4.2 copy-start.21
  10.2 2.6 copy-start.25
  12.6 173.7 %reduce-scatter.9.cloned.1.call-start = ((), (), s32[]{:S(2)}) async-start(), calls=%async_computation.11 | async-start | bytes 3932160 | tf_op jit(solution)/shard_map/reduce_scatter | solution.py:133
  28.5 50.5 %copy-start.17 = (bf16[768,3,192]{0,2,1:T(8,128)(2,1)}, bf16[768,3,192]{0,2,1:T(8,128)(2,1)S(1)}, u32[]{:S(2)}) copy-start(bf16[768,3,192]{0,2,1:T(8,128)(2,1)S(1)} %copy.71) | copy-start | bytes 2654212
  92.6 4.4 copy-start.2
  94.4 2.6 copy-start.5
  107.1 4.4 copy-start.2
  108.9 2.6 copy-start.5
  121.4 3.1 copy-start.11
  127.2 228.1 %all-gather.7.cloned.1.call-start = ((), (), s32[]{:S(2)}) async-start(), calls=%async_computation.12 | async-start | bytes 11796480 | tf_op jit(solution)/shard_map/all_gather | solution.py:180
  131.3 4.5 copy-start.29
  131.3 390.4 %all-gather.9.cloned.1.call-start = ((), (), s32[]{:S(2)}) async-start(), calls=%async_computation.13 | async-start | bytes 11796480 | tf_op jit(solution)/shard_map/all_gather | solution.py:181
  135.8 50.6 %copy-start.3 = (bf16[512,768]{1,0:T(8,128)(2,1)S(1)}, bf16[512,768]{1,0:T(8,128)(2,1)}, u32[]{:S(2)}) copy-start(bf16[512,768]{1,0:T(8,128)(2,1)} %param.18) | copy-start | bytes 2359300
  135.8 53.6 %copy-start.23 = (f32[768]{0:T(1024)S(1)}, f32[768]{0:T(1024)}, u32[]{:S(2)}) copy-start(f32[768]{0:T(1024)} %param.25) | copy-start | bytes 9220
  135.8 53.6 %copy-start.30 = (f32[768]{0:T(1024)S(1)}, f32[768]{0:T(1024)}, u32[]{:S(2)}) copy-start(f32[768]{0:T(1024)} %param.26) | copy-start | bytes 9220
  186.3 3.1 copy-start.6
  193.5 24.7 %all-to-all-start = ((bf16[8,128,768]{2,1,0:T(8,128)(2,1)}), bf16[8,128,768]{2,1,0:T(8,128)(2,1)S(1)}, u32[]{:S(2)}, u32[]{:S(2)}) async-start(bf16[8,128,768]{2,1,0:T(8,128)(2,1)} %bitcast.20), calls=%async_computation.1 | async-start | bytes 3145728 | tf_op jit(solution)/shard_map/all_to_all | solution.py:169
  218.2 149.3 %copy-start.15 = (bf16[8,128,768]{2,1,0:T(8,128)(2,1)}, bf16[8,128,768]{2,1,0:T(8,128)(2,1)S(1)}, u32[]{:S(2)}) copy-start(bf16[8,128,768]{2,1,0:T(8,128)(2,1)S(1)} %all-to-all-done) | copy-start | bytes 4718596
  218.2 316.3 %all-to-all-start.2 = ((bf16[8,128,768]{2,1,0:T(8,128)(2,1)}), bf16[8,128,768]{2,1,0:T(8,128)(2,1)}, u32[]{:S(2)}, u32[]{:S(2)}) async-start(bf16[8,128,768]{2,1,0:T(8,128)(2,1)} %bitcast.30), calls=%async_computation.3 | async-start | bytes 3145728 | tf_op jit(solution)/shard_map/all_to_all | solution.py:176
  534.5 32.6 %all-to-all-start.1 = ((bf16[8,128,768]{2,1,0:T(8,128)(2,1)}), bf16[8,128,768]{2,1,0:T(8,128)(2,1)S(1)}, u32[]{:S(2)}, u32[]{:S(2)}) async-start(bf16[8,128,768]{2,1,0:T(8,128)(2,1)} %bitcast.216), calls=%async_computation.2 | async-start | bytes 3145728 | tf_op jit(solution)/shard_map/all_to_all | solution.py:204
  567.1 25.3 %all-to-all-start.3 = ((bf16[8,128,768]{2,1,0:T(8,128)(2,1)}), bf16[8,128,768]{2,1,0:T(8,128)(2,1)}, u32[]{:S(2)}, u32[]{:S(2)}) async-start(bf16[8,128,768]{2,1,0:T(8,128)(2,1)} %bitcast.215), calls=%async_computation.4 | async-start | bytes 3145728 | tf_op jit(solution)/shard_map/all_to_all | solution.py:206
  571.4 91.9 %all-gather.11.cloned.1.call-start = ((), (), s32[]{:S(2)}) async-start(), calls=%async_computation.14 | async-start | bytes 3932160 | tf_op jit(solution)/shard_map/all_gather | solution.py:211
  598.3 65.0 %copy-start.12 = (bf16[192,768]{0,1:T(8,128)(2,1)S(1)}, bf16[192,768]{0,1:T(8,128)(2,1)}, u32[]{:S(2)}) copy-start(bf16[192,768]{0,1:T(8,128)(2,1)} %all_gather.20) | copy-start | bytes 884740
  603.2 158.4 %reduce-scatter.19.cloned.1.call-start = ((), (), s32[]{:S(2)}) async-start(), calls=%async_computation.19 | async-start | bytes 442368
  689.6 2.0 copy-start.13
  691.8 1.4 copy-start.14
  715.6 2.0 copy-start.13
  717.8 1.4 copy-start.14
  723.7 1.9 copy-start.7
  723.7 2.1 copy-start.9
  727.5 72.6 %reduce-scatter.13.cloned.1.call-start = ((), (), s32[]{:S(2)}) async-start(), calls=%async_computation.16 | async-start | bytes 1327104 | tf_op jit(solution)/shard_map/reduce_scatter | solution.py:235
  727.6 5.8 copy-start.18
  733.3 130.1 %reduce-scatter.11.cloned.1.call-start = ((), (), s32[]{:S(2)}) async-start(), calls=%async_computation.15 | async-start | bytes 3932160 | tf_op jit(solution)/shard_map/reduce_scatter | solution.py:223
  737.4 1.4 copy-start.16
  737.5 290.8 %reduce-scatter.15.cloned.1.call-start = ((), (), s32[]{:S(2)}) async-start(), calls=%async_computation.17 | async-start | bytes 11796480 | tf_op jit(solution)/shard_map/reduce_scatter | solution.py:197
  749.2 443.5 %reduce-scatter.17.cloned.1.call-start = ((), (), s32[]{:S(2)}) async-start(), calls=%async_computation.18 | async-start | bytes 11796480 | tf_op jit(solution)/shard_map/reduce_scatter | solution.py:200
  761.6 101.9 %copy-start.4 = (bf16[512,768]{1,0:T(8,128)(2,1)S(1)}, bf16[512,768]{1,0:T(8,128)(2,1)}, u32[]{:S(2)}) copy-start(bf16[512,768]{1,0:T(8,128)(2,1)} %param.18) | copy-start | bytes 2359300
  761.6 101.9 %copy-start.22 = (f32[512]{0:T(512)S(1)}, f32[512]{0:T(512)}, u32[]{:S(2)}) copy-start(f32[512]{0:T(512)} %copy-done.21) | copy-start | bytes 6148
  761.6 101.9 %copy-start.24 = (f32[768]{0:T(1024)S(1)}, f32[768]{0:T(1024)}, u32[]{:S(2)}) copy-start(f32[768]{0:T(1024)} %param.21) | copy-start | bytes 9220
  761.6 101.9 %copy-start.26 = (f32[512]{0:T(512)S(1)}, f32[512]{0:T(512)}, u32[]{:S(2)}) copy-start(f32[512]{0:T(512)} %copy-done.25) | copy-start | bytes 6148
  761.6 103.9 %copy-start.27 = (f32[768]{0:T(1024)S(1)}, f32[768]{0:T(1024)}, u32[]{:S(2)}) copy-start(f32[768]{0:T(1024)} %get-tuple-element.100) | copy-start | bytes 9220
  761.6 103.9 %copy-start.28 = (f32[768]{0:T(1024)S(1)}, f32[768]{0:T(1024)}, u32[]{:S(2)}) copy-start(f32[768]{0:T(1024)} %get-tuple-element.106) | copy-start | bytes 9220
  761.6 148.2 %copy-start.10 = (f32[512,768]{1,0:T(8,128)S(1)}, f32[512,768]{1,0:T(8,128)}, u32[]{:S(2)}) copy-start(f32[512,768]{1,0:T(8,128)} %get-tuple-element.131) | copy-start | bytes 4718596
  1028.2 168.7 %copy-start.1 = (s32[50257]{0:T(1024)S(1)}, s32[50257]{0:T(1024)}, u32[]{:S(2)}) copy-start(s32[50257]{0:T(1024)} %param.20) | copy-start | bytes 603088
  (1 other events, 0.9 us)
Sparse Core Ops, SparseCore 0:
  12.7 66.1 all-gather.4
  127.4 58.8 reduce-scatter.8
  188.5 166.7 all-gather.6
  356.7 164.9 all-gather.8
  603.4 59.9 all-gather.10
  727.7 32.4 reduce-scatter.18
  763.4 36.7 reduce-scatter.12
  803.2 60.2 reduce-scatter.10
  865.9 162.2 reduce-scatter.14
  1030.6 162.1 reduce-scatter.16

commit v2 on v1

v2 whole, which is shorter than its diff:
```python
import jax
import jax.numpy as jnp
from jax import lax
from jax.sharding import PartitionSpec as P

LEN = 1024


EPSILON = 1e-05
SCORE_SCALE = 0.125
MASKED = -1e30


def normalize(values, norm_gain, norm_shift):
    center = jnp.mean(values, axis=-1, keepdims=True)
    centered = values - center
    inv_scale = lax.rsqrt(jnp.mean(centered * centered, axis=-1, keepdims=True) + EPSILON)
    unit_rows = centered * inv_scale
    return (unit_rows * norm_gain + norm_shift, unit_rows, inv_scale)


def norm_back(grad_rows, unit_rows, inv_scale, norm_gain):
    scaled = grad_rows * norm_gain
    mean_plain = jnp.mean(scaled, axis=-1, keepdims=True)
    mean_unit = jnp.mean(scaled * unit_rows, axis=-1, keepdims=True)
    return inv_scale * (scaled - mean_plain - unit_rows * mean_unit)


def smooth(values):
    return jax.nn.gelu(values, approximate=True)


def causal_scores(query_rows, key_rows):
    length = query_rows.shape[0]
    scores = (
        jnp.einsum("qhd,khd->hqk", query_rows, key_rows, preferred_element_type=jnp.float32)
        * SCORE_SCALE
    )
    causal = lax.broadcasted_iota(jnp.int32, (length, length), 0) >= lax.broadcasted_iota(
        jnp.int32, (length, length), 1
    )
    return jnp.where(causal[None], scores, MASKED)


def attend(seq_block):
    scores = causal_scores(seq_block[:, :, 0], seq_block[:, :, 1])
    row_max = jnp.max(scores, axis=-1, keepdims=True)
    exp_scores = jnp.exp(scores - row_max)
    denominator = jnp.sum(exp_scores, axis=-1, keepdims=True)
    probabilities = (exp_scores / denominator).astype(jnp.bfloat16)
    mixed_heads = jnp.einsum(
        "hqk,khd->qhd", probabilities, seq_block[:, :, 2], preferred_element_type=jnp.float32
    )
    return (mixed_heads.astype(jnp.bfloat16), (row_max + jnp.log(denominator))[:, :, 0])


def attend_back(seq_block, mixed_grad, log_total):
    query_rows = seq_block[:, :, 0]
    key_rows = seq_block[:, :, 1]
    value_rows = seq_block[:, :, 2]
    probabilities = jnp.exp(causal_scores(query_rows, key_rows) - log_total[:, :, None])
    prob_grad = jnp.einsum(
        "qhd,khd->hqk", mixed_grad, value_rows, preferred_element_type=jnp.float32
    )
    row_inner = jnp.sum(probabilities * prob_grad, axis=-1, keepdims=True)
    score_grad = (probabilities * (prob_grad - row_inner)).astype(jnp.bfloat16)
    value_grad = jnp.einsum(
        "hqk,qhd->khd",
        probabilities.astype(jnp.bfloat16),
        mixed_grad,
        preferred_element_type=jnp.float32,
    )
    query_grad = (
        jnp.einsum("hqk,khd->qhd", score_grad, key_rows, preferred_element_type=jnp.float32)
        * SCORE_SCALE
    )
    key_grad = (
        jnp.einsum("hqk,qhd->khd", score_grad, query_rows, preferred_element_type=jnp.float32)
        * SCORE_SCALE
    )
    return jnp.stack([query_grad, key_grad, value_grad], axis=2).astype(jnp.bfloat16)


def product(spec, left, right):
    return jnp.einsum(spec, left, right, preferred_element_type=jnp.float32)


def on_device(
    tokens,
    token_ids,
    hash_table,
    ln1_gain,
    ln1_bias,
    w_qkv,
    w_out,
    ln2_gain,
    ln2_bias,
    expert_in,
    expert_out,
    cotangent,
):
    low = jnp.bfloat16
    row_count, model_width = tokens.shape
    local_experts = expert_in.shape[0]
    dp_count = lax.axis_size("dp")
    line = lax.axis_size("tensor")
    shares = LEN // row_count
    place = lax.axis_index("tensor")
    part = place % shares
    swap = [(t, t ^ 1) for t in range(line)]
    hop = [(t, t ^ 2) for t in range(line)]
    head_dim = w_qkv.shape[2] // 3
    heads_shard = w_qkv.shape[1]

    def swapped(values):
        return lax.ppermute(values, "tensor", swap)

    def joined(own, other):
        both = jnp.stack([own, other])
        return jnp.where(part == 0, both, both[::-1]).reshape((-1,) + own.shape[1:])

    def halves(both):
        pair = both.reshape((shares, -1) + both.shape[1:])
        return (
            lax.dynamic_index_in_dim(pair, part, 0, False),
            lax.dynamic_index_in_dim(pair, 1 - part, 0, False),
        )

    experts_total = dp_count * local_experts
    capacity = 2 * row_count // experts_total
    slot_count = experts_total * capacity
    expert_of = jnp.take(hash_table, token_ids)
    one_hot = (expert_of[:, None] == jnp.arange(experts_total, dtype=jnp.int32)[None, :]).astype(
        jnp.int32
    )
    before = (
        lax.broadcasted_iota(jnp.int32, (row_count, row_count), 0)
        > lax.broadcasted_iota(jnp.int32, (row_count, row_count), 1)
    ).astype(low)
    earlier = jnp.dot(before, one_hot.astype(low), preferred_element_type=jnp.float32)
    slot_rank = jnp.sum(earlier.astype(jnp.int32) * one_hot, axis=1)
    target = jnp.where(slot_rank < capacity, expert_of * capacity + slot_rank, slot_count)
    targets = lax.all_gather(target, "tensor", axis=0)
    route = (targets[:, None, :] == jnp.arange(slot_count, dtype=jnp.int32)[None, :, None]).astype(
        low
    )

    def dispatch(values):
        rows = lax.all_gather(values, "tensor", axis=0)
        slots = product("bsr,brd->bsd", route, rows).astype(low)
        slots = slots.reshape(line, dp_count, local_experts, capacity, model_width)
        slots = slots.transpose(1, 2, 0, 3, 4)
        slots = slots.reshape(dp_count, local_experts, line * capacity, model_width)
        return lax.all_to_all(slots, "dp", split_axis=0, concat_axis=0, tiled=True)

    def collect(values):
        back = lax.all_to_all(values, "dp", split_axis=0, concat_axis=0, tiled=True)
        back = back.reshape(dp_count, local_experts, line, capacity, model_width)
        back = back.transpose(2, 0, 1, 3, 4).reshape(line, slot_count, model_width)
        rows = product("bsr,bsd->brd", route, back).astype(low)
        rows = rows.reshape(line * row_count, model_width)
        return lax.psum_scatter(rows, "tensor", scatter_dimension=0, tiled=True).astype(
            jnp.float32
        )

    qkv_own = w_qkv.astype(low)
    qkv_pair = jnp.stack([qkv_own, lax.ppermute(qkv_own, "tensor", hop)], axis=1)
    qkv_flat = lax.all_gather(qkv_pair, "dp", axis=0, tiled=True).reshape(model_width, -1)
    out_rows = lax.all_gather(w_out.astype(low), "tensor", axis=0)
    out_weight = lax.all_gather(out_rows, "dp", axis=2, tiled=True)

    def picked(shards):
        own = lax.dynamic_index_in_dim(shards, place, 0, False)
        far = lax.dynamic_index_in_dim(shards, place ^ 2, 0, False)
        return jnp.concatenate([own, far])

    def picked_other(shards):
        own = lax.dynamic_index_in_dim(shards, place ^ 1, 0, False)
        far = lax.dynamic_index_in_dim(shards, place ^ 3, 0, False)
        return jnp.concatenate([own, far])

    out_mine = picked(out_weight)
    out_other = picked_other(out_weight)

    residual = tokens.astype(jnp.float32)
    first_norm, unit_one, scale_one = normalize(residual, ln1_gain, ln1_bias)
    first_low = first_norm.astype(low)
    first_all = joined(first_low, swapped(first_low))
    projected = jnp.dot(first_all, qkv_flat, preferred_element_type=jnp.float32).astype(low)
    heads_here = 2 * heads_shard
    seq_block = projected.reshape(LEN, heads_here, 3, head_dim)
    mixed_heads, log_total = attend(seq_block)
    mixed_own, mixed_sent = halves(mixed_heads.reshape(LEN, heads_here * head_dim))
    mixed_other = swapped(mixed_sent)
    attention = product("tk,kd->td", mixed_own, out_mine) + product(
        "tk,kd->td", mixed_other, out_other
    )
    middle = residual + attention
    second_norm, unit_two, scale_two = normalize(middle, ln2_gain, ln2_bias)

    out_grad = cotangent.astype(jnp.float32)
    grad_rows = dispatch(cotangent)
    shaped = dispatch(second_norm.astype(low))
    weight_in = expert_in.astype(low)
    weight_out = expert_out.astype(low)
    hidden = product("secd,edf->secf", shaped, weight_in)
    activated, pull = jax.vjp(smooth, hidden)
    activated = activated.astype(low)
    expert_result = product("secf,efd->secd", activated, weight_out).astype(low)
    act_grad = product("secd,efd->secf", grad_rows, weight_out)
    hidden_grad = pull(act_grad)[0].astype(low)
    row_grad = product("secf,edf->secd", hidden_grad, weight_in).astype(low)
    grad_expert_out = product("secf,secd->efd", activated, grad_rows)
    grad_expert_in = product("secd,secf->edf", shaped, hidden_grad)

    second_grad = collect(row_grad)
    mixed_out = middle + collect(expert_result)
    gain_two_grad = jnp.sum(second_grad * unit_two, axis=0)
    bias_two_grad = jnp.sum(second_grad, axis=0)
    middle_grad = out_grad + norm_back(second_grad, unit_two, scale_two, ln2_gain)
    middle_low = middle_grad.astype(low)
    grad_mine = product("td,kd->tk", middle_low, out_mine).astype(low)
    grad_sent = product("td,kd->tk", middle_low, out_other).astype(low)
    mixed_grad = joined(grad_mine, swapped(grad_sent)).reshape(LEN, heads_here, head_dim)
    wgrad_mine = product("tk,td->kd", mixed_own, middle_low).reshape(2, -1, model_width)
    wgrad_other = product("tk,td->kd", mixed_other, middle_low).reshape(2, -1, model_width)
    out_wgrad = jnp.stack([wgrad_mine[0], wgrad_other[0], wgrad_mine[1], wgrad_other[1]])
    out_part = lax.psum_scatter(out_wgrad.astype(low), "dp", scatter_dimension=2, tiled=True)
    out_total = out_part[0].astype(jnp.float32)
    for i in range(1, line):
        sent = lax.ppermute(out_part[i], "tensor", [(t, t ^ i) for t in range(line)])
        out_total = out_total + sent.astype(jnp.float32)

    qkv_grad = attend_back(seq_block, mixed_grad, log_total).reshape(LEN, -1)
    qkv_wgrad = product("td,tk->dk", first_all, qkv_grad).astype(low)
    qkv_part = lax.psum_scatter(qkv_wgrad, "dp", scatter_dimension=0, tiled=True)
    qkv_part = qkv_part.reshape((-1, 2) + w_qkv.shape[1:])
    qkv_total = qkv_part[:, 0].astype(jnp.float32) + lax.ppermute(
        qkv_part[:, 1], "tensor", hop
    ).astype(jnp.float32)
    first_own, first_sent = halves(product("tk,dk->td", qkv_grad, qkv_flat))
    first_grad = first_own + swapped(first_sent.astype(low)).astype(jnp.float32)
    gain_one_grad = jnp.sum(first_grad * unit_one, axis=0)
    bias_one_grad = jnp.sum(first_grad, axis=0)
    input_grad = middle_grad + norm_back(first_grad, unit_one, scale_one, ln1_gain)
    norm_sums = lax.psum(
        (gain_one_grad, bias_one_grad, gain_two_grad, bias_two_grad), ("dp", "tensor")
    )
    return (
        mixed_out.astype(low),
        input_grad.astype(low),
        norm_sums[0],
        norm_sums[1],
        qkv_total,
        out_total,
        norm_sums[2],
        norm_sums[3],
        grad_expert_in,
        grad_expert_out,
    )


def solution(mesh):
    rows = P(("dp", "tensor"), None)
    weights = (P("dp", "tensor", None), P("tensor", "dp"))
    experts = (P("dp", None, "tensor"), P("dp", "tensor", None))
    return jax.shard_map(
        on_device,
        mesh=mesh,
        in_specs=(rows, P(("dp", "tensor")), P(), P(), P(), *weights, P(), P(), *experts, rows),
        out_specs=(rows, rows, P(), P(), *weights, P(), P(), *experts),
        check_vma=False,
    )
```

time: 1210 us -> 794 us (0.66)
  waiting for transfers between devices: 844 us -> 356 us
  matrix products: 144 us -> 178 us
  local copies, waits for them, and re-layouts: 49.2 us -> 69 us
  other arithmetic: 65.9 us -> 49 us
  starting transfers between devices: 16.7 us -> 33.1 us
  blocking collectives: 68.6 us -> 81.7 us
    reduce_scatter x5 -> x3, waiting for transfers between devices: 421 us -> 37.6 us  [the longest x2 37.6 us: collect(): lax.psum_scatter(rows, 'tensor', scatter_dimension=0, tiled=True)]
    all_gather x4, waiting for transfers between devices: 388 us -> 112 us  [the longest x2 112 us: dispatch(): rows = lax.all_gather(values, 'tensor', axis=0)]
    all_to_all x4, waiting for transfers between devices: 34.7 us -> 182 us  [the longest x2 122 us: collect(): back = lax.all_to_all(values, 'dp', split_axis=0, concat_axis=0, tiled=True)]
    ppermute x0 -> x9, waiting for transfers between devices: none -> 24.1 us  [the longest x4 10.7 us: swapped(): return lax.ppermute(values, 'tensor', swap)]
    dot_general x13 -> x20, matrix products: 95.6 us -> 119 us  [the longest x18 113 us: product(): return jnp.einsum(spec, left, right, preferred_element_type=jnp.float32)]
    convert_element_type x10 -> x6, other arithmetic: 29.1 us -> 8.98 us  [the longest x1 3.47 us: on_device(): middle_low = middle_grad.astype(low)]
    all_gather x2, blocking collectives: 24.3 us -> 40.8 us  [the longest x1 28.6 us: on_device(): out_rows = lax.all_gather(w_out.astype(low), 'tensor', axis=0)]
    ppermute x0 -> x9, starting transfers between devices: none -> 13 us  [the longest x3 4.45 us: on_device(): lax.ppermute(out_part[i], 'tensor', [(t, t ^ i) for t in range(line)])]
  transfers between devices with their start and end apart: 14 -> 21, of which waited for: 11 -> 12; matrix products, arithmetic and copies ran while one was open for 10% -> 31% of each run, Pallas kernels for 0% -> 0%
where the time goes in v2:
time: 794 us; the launch traced here: 783 us
  waiting for transfers between devices  356 us (45%)
  matrix products  178 us (22%)
  blocking collectives  81.7 us (10%)
  local copies, waits for them, and re-layouts  69 us (9%)
  other arithmetic  49 us (6%)
  starting transfers between devices  33.1 us (4%)
  between operations  15.3 us (2%)
    all_to_all x2, waiting for transfers between devices, collect(): back = lax.all_to_all(values, 'dp', split_axis=0, concat_axis=0, tiled=True)  122 us
    dot_general x18, matrix products, product(): return jnp.einsum(spec, left, right, preferred_element_type=jnp.float32)  113 us
    all_gather x2, waiting for transfers between devices, dispatch(): rows = lax.all_gather(values, 'tensor', axis=0)  112 us
    all_to_all x2, waiting for transfers between devices, dispatch(): return lax.all_to_all(slots, 'dp', split_axis=0, concat_axis=0, tiled=True)  60.4 us
    psum x1, blocking collectives, on_device(): lax.psum((gain_one_grad, bias_one_grad, gain_two_grad, bias_two_grad), ('...  41 us
    reduce_scatter x2, waiting for transfers between devices, collect(): lax.psum_scatter(rows, 'tensor', scatter_dimension=0, tiled=True)  37.6 us
    all_gather x1, blocking collectives, on_device(): out_rows = lax.all_gather(w_out.astype(low), 'tensor', axis=0)  28.6 us
    unnamed x75, local copies, waits for them, and re-layouts  18.6 us
  transfers between devices with their start and end apart: 21, of which 12 were waited for; matrix products, arithmetic and copies ran while one was open for 31% of the time, Pallas kernels for 0%

profile of v2, /device:TPU:0, one launch (start us, length us, event | category | flops | bytes accessed | tf_op | source)
XLA Modules:
  0.0 783.1 jit_solution(6894556946211187529)
XLA Ops:
  8.3 4.1 collective-permute-start.1
  13.4 6.0 collective-permute-done.1
  23.5 28.6 %all-gather = bf16[768,96]{1,0:T(8,128)(2,1)S(1)} all-gather(bf16[192,96]{1,0:T(8,128)(2,1)S(1)} %convert_element_type.169), channel_id=2, replica_groups=mesh['dp'=8,'tensor'=4] {'tensor'}, dimensions={0}, use_global_device_ids=true | all-gather | bytes 184320 | tf_op jit(solution)/shard_map/all_gather | solution.py:169
  56.4 5.6 copy.103
  63.3 5.1 convolution_convert_fusion
  71.2 12.1 %fusion.105 = (f32[6,1024]{1,0:T(8,128)S(1)}, f32[6,1024,1024]{1,2,0:T(8,128)}) fusion(bf16[1024,6,3,64]{0,3,2,1:T(8,128)(2,1)S(1)} %bitcast.199, pred[1024,1024]{0,1:T(8,128)(4,1)} %iota_compare_fusion.5), kind=kOutput, calls=%fused_computation.174 | convolution fusion | flops 824174592 | bytes 27811840 | tf_op jit(solution)/shard_map/qhd,khd->hqk/dot_general | solution.py:36
  83.3 10.2 %fusion = f32[6,1024]{1,0:T(8,128)S(1)} fusion(f32[6,1024,1024]{1,2,0:T(8,128)} %get-tuple-element.71, f32[6,1024]{1,0:T(8,128)S(1)} %get-tuple-element.70), kind=kLoop, calls=%fused_computation.7 | loop fusion | flops 12576768 | bytes 25214976 | tf_op jit(solution)/shard_map/reduce_sum | solution.py:49
  94.2 11.3 %fusion.80 = bf16[1024,6,64]{0,2,1:T(8,128)(2,1)} fusion(f32[6,1024,1024]{1,2,0:T(8,128)} %get-tuple-element.71, f32[6,1024]{1,0:T(8,128)S(1)} %fusion, f32[6,1024]{1,0:T(8,128)S(1)} %get-tuple-element.70, bf16[1024,6,3,64]{0,3,2,1:T(8,128)(2,1)S(1)} %bitcast.200), kind=kOutput, calls=%fused_computation.109 | convolution fusion | flops 824573952 | bytes 26804224 | tf_op jit(solution)/shard_map/hqk,khd->qhd/dot_general | solution.py:51
  111.6 7.7 constant_dynamic-slice_fusion.1
  133.2 3.1 gather_fusion
  136.6 12.1 %all-gather.4 = s32[4,1,512]{2,1,0:T(1,128)S(1)} all-gather(s32[1,1,512]{2,1,0:T(1,128)S(1)} %bitcast.233), channel_id=3, replica_groups=mesh['dp'=8,'tensor'=4] {'tensor'}, dimensions={0}, use_global_device_ids=true | all-gather | bytes 10240 | tf_op jit(solution)/shard_map/all_gather | solution.py:143
  148.7 48.1 %all-gather.14.cloned.1.call-done = bf16[2048,768]{1,0:T(8,128)(2,1)} async-done(((bf16[512,768]{1,0:T(8,128)(2,1)}), bf16[2048,768]{1,0:T(8,128)(2,1)}) %all-gather.14.cloned.1.call-update) | async-done | bytes 3145744 | tf_op jit(solution)/shard_map/all_gather | solution.py:149
  196.8 5.5 fusion.32
  202.3 3.1 copy.117
  205.4 4.7 all-to-all-start
  210.8 64.1 %all-gather.16.cloned.1.call-done = bf16[2048,768]{1,0:T(8,128)(2,1)} async-done(((bf16[512,768]{1,0:T(8,128)(2,1)}), bf16[2048,768]{1,0:T(8,128)(2,1)}) %all-gather.16.cloned.1.call-update) | async-done | bytes 3145744 | tf_op jit(solution)/shard_map/all_gather | solution.py:149
  274.9 5.5 fusion.33
  283.4 4.9 all-to-all-start.2
  288.3 11.3 %fusion.23 = f32[2,8,256,768]{3,2,1,0:T(8,128)} fusion(bf16[8,2,256,768]{3,2,1,0:T(8,128)(2,1)} %all-to-all-done, f32[2,768,768]{2,1,0:T(8,128)} %param.21), kind=kOutput, calls=%fused_computation.35 | convolution fusion | flops 4833017856 | bytes 23592960 | tf_op jit(solution)/shard_map/secd,edf->secf/dot_general | solution.py:85
  299.6 60.3 %all-to-all-done.2 = bf16[8,2,256,768]{3,2,1,0:T(8,128)(2,1)} async-done(((bf16[8,2,256,768]{3,2,1,0:T(8,128)(2,1)}), bf16[8,2,256,768]{3,2,1,0:T(8,128)(2,1)}, u32[]{:S(2)}, u32[]{:S(2)}) %all-to-all-start.2) | async-done | bytes 6291488 | tf_op jit(solution)/shard_map/all_to_all | solution.py:154
  359.9 16.7 %fusion.8 = bf16[8,2,256,768]{3,2,0,1:T(8,128)(2,1)S(1)} fusion(f32[2,8,256,768]{3,2,1,0:T(8,128)} %fusion.23, bf16[8,2,256,768]{3,2,1,0:T(8,128)(2,1)} %all-to-all-done.2, f32[2,768,768]{2,1,0:T(8,128)} %param.22), kind=kOutput, calls=%fused_computation.17 | convolution fusion | flops 4895932416 | bytes 29884416 | tf_op jit(solution)/shard_map/secd,efd->secf/dot_general | solution.py:85
  376.6 10.0 %convert_bitcast_fusion = bf16[8,2,256,768]{3,2,0,1:T(8,128)(2,1)S(1)} fusion(bf16[8,2,256,768]{3,2,0,1:T(8,128)(2,1)S(1)} %fusion.8, f32[2,768,768]{2,1,0:T(8,128)} %param.21), kind=kOutput, calls=%fused_computation.37 | convolution fusion | flops 4836163584 | bytes 17301504 | tf_op jit(solution)/shard_map/secf,edf->secd/dot_general | solution.py:85
  386.6 3.1 copy.124
  389.7 5.0 all-to-all-start.3
  394.7 10.4 %convert_bitcast_fusion.1 = bf16[8,2,256,768]{3,2,0,1:T(8,128)(2,1)S(1)} fusion(f32[2,768,768]{2,1,0:T(8,128)} %param.22, f32[2,8,256,768]{3,2,1,0:T(8,128)} %fusion.23), kind=kOutput, calls=%fused_computation.38 | convolution fusion | flops 4864475136 | bytes 23592960 | tf_op jit(solution)/shard_map/secf,efd->secd/dot_general | solution.py:85
  408.1 58.1 %all-to-all-done.3 = bf16[8,2,256,768]{3,2,1,0:T(8,128)(2,1)} async-done(((bf16[8,2,256,768]{3,2,1,0:T(8,128)(2,1)}), bf16[8,2,256,768]{3,2,1,0:T(8,128)(2,1)}, u32[]{:S(2)}, u32[]{:S(2)}) %all-to-all-start.3) | async-done | bytes 6291488 | tf_op jit(solution)/shard_map/all_to_all | solution.py:157
  466.3 4.7 all-to-all-start.1
  471.1 3.2 copy.125
  474.3 4.9 fusion.47
  479.2 63.4 %all-to-all-done.1 = bf16[8,2,256,768]{3,2,1,0:T(8,128)(2,1)} async-done(((bf16[8,2,256,768]{3,2,1,0:T(8,128)(2,1)}), bf16[8,2,256,768]{3,2,1,0:T(8,128)(2,1)}, u32[]{:S(2)}, u32[]{:S(2)}) %all-to-all-start.1) | async-done | bytes 6291488 | tf_op jit(solution)/shard_map/all_to_all | solution.py:157
  542.6 3.2 copy.120
  545.8 4.9 fusion.46
  551.5 16.9 %fusion.43 = f32[2,768,768]{2,1,0:T(8,128)} fusion(bf16[8,2,256,768]{3,2,1,0:T(8,128)(2,1)} %all-to-all-done.2, f32[2,8,256,768]{3,2,1,0:T(8,128)} %fusion.23), kind=kOutput, calls=%fused_computation.66 | convolution fusion | flops 4860149760 | bytes 23592960 | tf_op jit(solution)/shard_map/secf,secd->efd/dot_general | solution.py:85
  570.4 37.6 %reduce-scatter.7.cloned.1.call-done = bf16[512,768]{1,0:T(8,128)(2,1)} async-done(((bf16[2048,768]{1,0:T(8,128)(2,1)}), bf16[512,768]{1,0:T(8,128)(2,1)}) %reduce-scatter.7.cloned.1.call-update) | async-done | bytes 786448 | tf_op jit(solution)/shard_map/reduce_scatter | solution.py:162
  608.0 3.5 fusion.102
  620.2 4.3 collective-permute-done.3
  627.2 16.5 %multiply_reduce_fusion = (f32[6,1024]{1,0:T(8,128)S(1)}, f32[6,1024,1024]{1,2,0:T(8,128)}) fusion(f32[6,1024,1024]{1,2,0:T(8,128)} %get-tuple-element.71, f32[6,1024]{1,0:T(8,128)S(1)} %log_add_fusion, bf16[1024,6,64]{0,2,1:T(8,128)(2,1)S(1)} %reshape_reshape.7, bf16[1024,6,3,64]{0,3,2,1:T(8,128)(2,1)} %bitcast.201), kind=kOutput, calls=%fused_computation.2 | convolution fusion | flops 824174592 | bytes 51953664 | tf_op jit(solution)/shard_map/qhd,khd->hqk/dot_general | solution.py:62
  643.7 17.1 %multiply_convert_fusion = bf16[6,1024,1024]{1,2,0:T(8,128)(2,1)S(1)} fusion(f32[6,1024,1024]{1,2,0:T(8,128)} %get-tuple-element.75, f32[6,1024,1024]{1,2,0:T(8,128)} %get-tuple-element.71, f32[6,1024]{1,0:T(8,128)S(1)} %get-tuple-element.74, f32[6,1024]{1,0:T(8,128)S(1)} %log_add_fusion), kind=kLoop, calls=%fused_computation.1 | loop fusion | flops 25165824 | bytes 62963712 | tf_op jit(solution)/shard_map/convert_element_type | solution.py:66
  660.8 5.1 fusion.79
  665.9 4.4 fusion.78
  670.2 10.3 %fusion.75 = bf16[1024,6,1,64]{0,3,1,2:T(8,128)(2,1)S(1)} fusion(bf16[1024,6,64]{0,2,1:T(8,128)(2,1)S(1)} %reshape_reshape.7, f32[6,1024,1024]{1,2,0:T(8,128)} %get-tuple-element.71, f32[6,1024]{1,0:T(8,128)S(1)} %log_add_fusion), kind=kOutput, calls=%fused_computation.106 | convolution fusion | flops 818282496 | bytes 26763264 | tf_op jit(solution)/shard_map/hqk,qhd->khd/dot_general | solution.py:67
  682.1 3.1 convert_element_type.195
  685.3 4.9 convolution_convert_fusion.1
  690.2 4.5 fusion.38
  696.4 10.8 %fusion.40 = f32[2,768,768]{2,1,0:T(8,128)} fusion(bf16[8,2,256,768]{3,2,1,0:T(8,128)(2,1)} %all-to-all-done, bf16[8,2,256,768]{3,2,0,1:T(8,128)(2,1)} %copy-done.29), kind=kOutput, calls=%fused_computation.65 | convolution fusion | flops 4831838208 | bytes 17301504 | tf_op jit(solution)/shard_map/secd,secf->edf/dot_general | solution.py:85
  707.2 6.4 collective-permute-done.4
  714.6 41.0 %all-reduce = (f32[768]{0:T(1024)}, f32[768]{0:T(1024)}, f32[768]{0:T(1024)}, f32[768]{0:T(1024)}) all-reduce(f32[768]{0:T(1024)S(1)} %get-tuple-element.42, f32[768]{0:T(1024)S(1)} %get-tuple-element.45, f32[768]{0:T(1024)S(1)} %get-tuple-element.40, f32[768]{0:T(1024)S(1)} %get-tuple-element.47), channel_id=1, replica_groups=mesh['dp'=8,'tensor'=4] {'dp','tensor'}, use_global_device_ids=true, to_apply=%region_15.16 | all-reduce | flops 3072 | bytes 24576 | tf_op jit(solution)/shard_map/psum | solution.py:246
  768.6 6.3 collective-permute-done.5
  (167 shorter events, 73.8 us)
Async XLA Ops:
  7.2 126.0 %copy-start = (s32[50257]{0:T(1024)S(1)}, s32[50257]{0:T(1024)}, u32[]{:S(2)}) copy-start(s32[50257]{0:T(1024)} %param.14) | copy-start | bytes 603088
  7.2 14.7 %copy-start.2 = (bf16[512,768]{1,0:T(8,128)(2,1)S(1)}, bf16[512,768]{1,0:T(8,128)(2,1)}, u32[]{:S(2)}) copy-start(bf16[512,768]{1,0:T(8,128)(2,1)} %param.12) | copy-start | bytes 2359300
  7.2 15.1 %copy-start.19 = (f32[768]{0:T(1024)S(1)}, f32[768]{0:T(1024)}, u32[]{:S(2)}) copy-start(f32[768]{0:T(1024)} %param.15) | copy-start | bytes 9220
  7.2 15.1 %copy-start.26 = (f32[768]{0:T(1024)S(1)}, f32[768]{0:T(1024)}, u32[]{:S(2)}) copy-start(f32[768]{0:T(1024)} %param.16) | copy-start | bytes 9220
  7.2 16.3 %copy-start.16 = (f32[192,96]{1,0:T(8,128)S(1)}, f32[192,96]{1,0:T(8,128)}, u32[]{:S(2)}) copy-start(f32[192,96]{1,0:T(8,128)} %param.18) | copy-start | bytes 221188
  7.2 49.2 %all-gather.10.cloned.1.call-start = ((), (), s32[]{:S(2)}) async-start(), calls=%async_computation.8 | async-start | bytes 2654208 | tf_op jit(solution)/shard_map/all_gather | solution.py:168
  8.3 11.1 %collective-permute-start.1 = (bf16[96,3,192]{2,0,1:T(8,128)(2,1)S(1)}, bf16[96,3,192]{2,0,1:T(8,128)(2,1)S(1)}, u32[]{:S(2)}, u32[]{:S(2)}) collective-permute-start(bf16[96,3,192]{2,0,1:T(8,128)(2,1)S(1)} %convert_element_type.164), channel_id=1, source_target_pairs={{0,2},{1,3},{2,0},{3,1},{4,6},{5,7},{6,4},{7,5},{8,10},{9,11},{10,... | collective-permute-start | bytes 331784 | tf_op jit(solution)/shard_map/ppermute | solution.py:167
  20.6 91.0 %all-gather.12.cloned.1.call-start = ((), (), s32[]{:S(2)}) async-start(), calls=%async_computation.9 | async-start | bytes 1769472 | tf_op jit(solution)/shard_map/all_gather | solution.py:170
  21.9 33.0 %copy-start.17 = (f32[512]{0:T(512)}, f32[512]{0:T(512)S(1)}, u32[]{:S(2)}) copy-start(f32[512]{0:T(512)S(1)} %broadcast_multiply_fusion.5) | copy-start | bytes 6148
  22.3 32.6 %copy-start.21 = (f32[512]{0:T(512)}, f32[512]{0:T(512)S(1)}, u32[]{:S(2)}) copy-start(f32[512]{0:T(512)S(1)} %add_rsqrt_fusion.1) | copy-start | bytes 6148
  22.7 32.0 %collective-permute-start = (bf16[512,768]{1,0:T(8,128)(2,1)S(1)}, bf16[512,768]{1,0:T(8,128)(2,1)S(1)}, u32[]{:S(2)}, u32[]{:S(2)}) collective-permute-start(bf16[512,768]{1,0:T(8,128)(2,1)S(1)} %fusion.58), channel_id=1, source_target_pairs={{0,1},{1,0},{2,3},{3,2},{4,5},{5,4},{6,7},{7,6},{8,9},{9,8},{10,11... | collective-permute-start | bytes 2359304 | tf_op jit(solution)/shard_map/ppermute | solution.py:116
  53.0 143.8 %all-gather.14.cloned.1.call-start = ((), (), s32[]{:S(2)}) async-start(), calls=%async_computation.13 | async-start | bytes 3932160 | tf_op jit(solution)/shard_map/all_gather | solution.py:149
  62.0 1.3 copy-start.6
  71.2 22.3 %copy-start.4 = (bf16[1024,1152]{0,1:T(8,128)(2,1)}, bf16[1024,1152]{0,1:T(8,128)(2,1)S(1)}, u32[]{:S(2)}) copy-start(bf16[1024,1152]{0,1:T(8,128)(2,1)S(1)} %copy.104) | copy-start | bytes 7077892
  83.3 10.2 %copy-start.12 = (f32[6,1024]{1,0:T(8,128)}, f32[6,1024]{1,0:T(8,128)S(1)}, u32[]{:S(2)}) copy-start(f32[6,1024]{1,0:T(8,128)S(1)} %get-tuple-element.70) | copy-start | bytes 73732
  111.3 17.9 %collective-permute-start.2 = (bf16[512,384]{1,0:T(8,128)(2,1)}, bf16[512,384]{1,0:T(8,128)(2,1)}, u32[]{:S(2)}, u32[]{:S(2)}) collective-permute-start(bf16[512,384]{1,0:T(8,128)(2,1)} %bitcast.15), channel_id=1, source_target_pairs={{0,1},{1,0},{2,3},{3,2},{4,5},{5,4},{6,7},{7,6},{8,9},{9,8},{10,11... | collective-permute-start | bytes 1179656 | tf_op jit(solution)/shard_map/ppermute | solution.py:116
  126.6 2.7 copy-start.9
  129.3 2.6 copy-start.23
  129.3 2.6 copy-start.28
  131.0 2.1 copy-start.27
  205.4 77.9 %all-to-all-start = ((bf16[8,2,256,768]{3,2,1,0:T(8,128)(2,1)}), bf16[8,2,256,768]{3,2,1,0:T(8,128)(2,1)}, u32[]{:S(2)}, u32[]{:S(2)}) async-start(bf16[8,2,256,768]{3,2,1,0:T(8,128)(2,1)} %bitcast.197), calls=%async_computation | async-start | bytes 12582912 | tf_op jit(solution)/shard_map/all_to_all | solution.py:154
  210.2 64.7 %all-gather.16.cloned.1.call-start = ((), (), s32[]{:S(2)}) async-start(), calls=%async_computation.14 | async-start | bytes 3932160 | tf_op jit(solution)/shard_map/all_gather | solution.py:149
  283.4 76.5 %all-to-all-start.2 = ((bf16[8,2,256,768]{3,2,1,0:T(8,128)(2,1)}), bf16[8,2,256,768]{3,2,1,0:T(8,128)(2,1)}, u32[]{:S(2)}, u32[]{:S(2)}) async-start(bf16[8,2,256,768]{3,2,1,0:T(8,128)(2,1)} %bitcast.198), calls=%async_computation.3 | async-start | bytes 12582912 | tf_op jit(solution)/shard_map/all_to_all | solution.py:154
  376.6 10.0 %copy-start.29 = (bf16[8,2,256,768]{3,2,0,1:T(8,128)(2,1)}, bf16[8,2,256,768]{3,2,0,1:T(8,128)(2,1)S(1)}, u32[]{:S(2)}) copy-start(bf16[8,2,256,768]{3,2,0,1:T(8,128)(2,1)S(1)} %fusion.8) | copy-start | bytes 18874372
  389.7 76.6 %all-to-all-start.3 = ((bf16[8,2,256,768]{3,2,1,0:T(8,128)(2,1)}), bf16[8,2,256,768]{3,2,1,0:T(8,128)(2,1)}, u32[]{:S(2)}, u32[]{:S(2)}) async-start(bf16[8,2,256,768]{3,2,1,0:T(8,128)(2,1)} %copy.124), calls=%async_computation.4 | async-start | bytes 12582912 | tf_op jit(solution)/shard_map/all_to_all | solution.py:157
  466.3 76.3 %all-to-all-start.1 = ((bf16[8,2,256,768]{3,2,1,0:T(8,128)(2,1)}), bf16[8,2,256,768]{3,2,1,0:T(8,128)(2,1)}, u32[]{:S(2)}, u32[]{:S(2)}) async-start(bf16[8,2,256,768]{3,2,1,0:T(8,128)(2,1)} %copy.119), calls=%async_computation.1 | async-start | bytes 12582912 | tf_op jit(solution)/shard_map/all_to_all | solution.py:157
  471.0 97.5 %reduce-scatter.9.cloned.1.call-start = ((), (), s32[]{:S(2)}) async-start(), calls=%async_computation.11 | async-start | bytes 3932160 | tf_op jit(solution)/shard_map/reduce_scatter | solution.py:162
  479.2 128.9 %reduce-scatter.7.cloned.1.call-start = ((), (), s32[]{:S(2)}) async-start(), calls=%async_computation.10 | async-start | bytes 3932160 | tf_op jit(solution)/shard_map/reduce_scatter | solution.py:162
  550.7 0.8 copy-start.15
  550.8 207.7 %reduce-scatter.13.cloned.1.call-start = ((), (), s32[]{:S(2)}) async-start(), calls=%async_computation.15 | async-start | bytes 1327104
  551.5 17.0 %copy-start.25 = (f32[512]{0:T(512)S(1)}, f32[512]{0:T(512)}, u32[]{:S(2)}) copy-start(f32[512]{0:T(512)} %copy-done.24) | copy-start | bytes 6148
  551.5 56.5 %copy-start.5 = (bf16[512,768]{1,0:T(8,128)(2,1)S(1)}, bf16[512,768]{1,0:T(8,128)(2,1)}, u32[]{:S(2)}) copy-start(bf16[512,768]{1,0:T(8,128)(2,1)} %param.23) | copy-start | bytes 2359300
  611.5 4.5 copy-start.10
  613.4 11.1 %collective-permute-start.3 = (bf16[512,384]{1,0:T(8,128)(2,1)}, bf16[512,384]{1,0:T(8,128)(2,1)}, u32[]{:S(2)}, u32[]{:S(2)}) collective-permute-start(bf16[512,384]{1,0:T(8,128)(2,1)} %convolution_convert_fusion.4), channel_id=1, source_target_pairs={{0,1},{1,0},{2,3},{3,2},{4,5},{5,4},{6,7},{7,6},{8,9},{9,8},{10,11... | collective-permute-start | bytes 1179656 | tf_op jit(solution)/shard_map/ppermute | solution.py:116
  616.2 3.4 copy-start.7
  616.2 3.4 copy-start.8
  617.2 2.4 copy-start.11
  619.5 145.4 %reduce-scatter.11.cloned.1.call-start = ((), (), s32[]{:S(2)}) async-start(), calls=%async_computation.12 | async-start | bytes 1990656 | tf_op jit(solution)/shard_map/reduce_scatter | solution.py:236
  694.9 18.8 %copy-start.3 = (bf16[512,768]{1,0:T(8,128)(2,1)S(1)}, bf16[512,768]{1,0:T(8,128)(2,1)}, u32[]{:S(2)}) copy-start(bf16[512,768]{1,0:T(8,128)(2,1)} %param.12) | copy-start | bytes 2359300
  694.9 18.8 %copy-start.18 = (f32[512]{0:T(512)S(1)}, f32[512]{0:T(512)}, u32[]{:S(2)}) copy-start(f32[512]{0:T(512)} %copy-done.17) | copy-start | bytes 6148
  694.9 18.8 %copy-start.20 = (f32[768]{0:T(1024)S(1)}, f32[768]{0:T(1024)}, u32[]{:S(2)}) copy-start(f32[768]{0:T(1024)} %param.15) | copy-start | bytes 9220
  694.9 18.8 %copy-start.22 = (f32[512]{0:T(512)S(1)}, f32[512]{0:T(512)}, u32[]{:S(2)}) copy-start(f32[512]{0:T(512)} %copy-done.21) | copy-start | bytes 6148
  694.9 18.7 %collective-permute-start.4 = (bf16[512,768]{1,0:T(8,128)(2,1)S(1)}, bf16[512,768]{1,0:T(8,128)(2,1)S(1)}, u32[]{:S(2)}, u32[]{:S(2)}) collective-permute-start(bf16[512,768]{1,0:T(8,128)(2,1)S(1)} %fusion.88), channel_id=1, source_target_pairs={{0,1},{1,0},{2,3},{3,2},{4,5},{5,4},{6,7},{7,6},{8,9},{9,8},{10,11... | collective-permute-start | bytes 2359304 | tf_op jit(solution)/shard_map/ppermute | solution.py:116
  755.6 20.3 %copy-start.1 = (s32[50257]{0:T(1024)S(1)}, s32[50257]{0:T(1024)}, u32[]{:S(2)}) copy-start(s32[50257]{0:T(1024)} %param.14) | copy-start | bytes 603088
  760.4 6.5 collective-permute-start.8
  762.8 4.5 collective-permute-start.6
  762.8 5.2 collective-permute-start.7
  766.1 8.9 %collective-permute-start.5 = (bf16[96,3,192]{0,2,1:T(8,128)(2,1)S(1)}, bf16[96,3,192]{0,2,1:T(8,128)(2,1)S(1)}, u32[]{:S(2)}, u32[]{:S(2)}) collective-permute-start(bf16[96,3,192]{0,2,1:T(8,128)(2,1)S(1)} %slice_bitcast_fusion.13), channel_id=1, source_target_pairs={{0,2},{1,3},{2,0},{3,1},{4,6},{5,7},{6,4},{7,5},{8,10},{9,11},{10,... | collective-permute-start | bytes 331784 | tf_op jit(solution)/shard_map/ppermute | solution.py:238
  (3 other events, 1.9 us)
Sparse Core Ops, SparseCore 0:
  20.7 30.1 all-gather.9
  53.4 25.6 all-gather.11
  133.2 63.5 all-gather.13
  212.3 62.5 all-gather.15
  479.3 59.2 reduce-scatter.8
  550.9 57.1 reduce-scatter.6
  619.6 37.2 reduce-scatter.12
  690.4 39.9 reduce-scatter.10

commit v3 on v2

v3 whole, which is shorter than its diff:
```python
import functools

import jax
import jax.numpy as jnp
from jax import lax
from jax.experimental import pallas as pl
from jax.experimental.pallas import tpu as pltpu
from jax.sharding import PartitionSpec as P

LEN = 1024


EPSILON = 1e-05
SCORE_SCALE = 0.125
MASKED = -1e30
MESH = pl.DeviceIdType.MESH


def normalize(values, norm_gain, norm_shift):
    center = jnp.mean(values, axis=-1, keepdims=True)
    centered = values - center
    inv_scale = lax.rsqrt(jnp.mean(centered * centered, axis=-1, keepdims=True) + EPSILON)
    unit_rows = centered * inv_scale
    return (unit_rows * norm_gain + norm_shift, unit_rows, inv_scale)


def norm_back(grad_rows, unit_rows, inv_scale, norm_gain):
    scaled = grad_rows * norm_gain
    mean_plain = jnp.mean(scaled, axis=-1, keepdims=True)
    mean_unit = jnp.mean(scaled * unit_rows, axis=-1, keepdims=True)
    return inv_scale * (scaled - mean_plain - unit_rows * mean_unit)


def smooth(values):
    return jax.nn.gelu(values, approximate=True)


def lanes_of(values, mask):
    return jnp.where(mask, values, 0.0).astype(jnp.bfloat16)


def dot_rows(left, right):
    return lax.dot_general(left, right, (((1,), (1,)), ((), ())), preferred_element_type=jnp.float32)


def dot_columns(left, right):
    return lax.dot_general(left, right, (((0,), (0,)), ((), ())), preferred_element_type=jnp.float32)


def dot_plain(left, right):
    return jnp.dot(left, right, preferred_element_type=jnp.float32)


def masked_scores(query, key, first):
    scores = dot_rows(query, key)
    rows, columns = scores.shape
    row = lax.broadcasted_iota(jnp.int32, (rows, rows), 0)
    column = lax.broadcasted_iota(jnp.int32, (rows, rows), 1)
    edge = jnp.where(row >= column, scores[:, first:], MASKED)
    return edge if first == 0 else jnp.concatenate([scores[:, :first], edge], axis=1)


def attend_back_kernel(head_dim, block, q_ref, k_ref, v_ref, log_ref, grad_ref, dq_ref, dk_sum, dv_sum):
    length, width = q_ref.shape
    lane = lax.broadcasted_iota(jnp.int32, (block, width), 1)
    for first in reversed(range(0, length, block)):
        rows = pl.ds(first, block)
        seen = pl.ds(0, first + block)
        lanes_seen = lax.broadcasted_iota(jnp.int32, (first + block, width), 1)
        wide_query = q_ref[rows, :].astype(jnp.float32) * SCORE_SCALE
        key, value, grad = k_ref[seen, :], v_ref[seen, :], grad_ref[rows, :]
        query, wide_grad = wide_query.astype(jnp.bfloat16), grad.astype(jnp.float32)
        dq = jnp.zeros((block, width), jnp.float32)
        dk = jnp.zeros((first + block, width), jnp.float32)
        dv = jnp.zeros((first + block, width), jnp.float32)
        for head in range(width // head_dim):
            mine = lane // head_dim == head
            there = lanes_seen // head_dim == head
            scores = masked_scores(lanes_of(wide_query, mine), key, first)
            log_total = log_ref[rows, pl.ds(head * head_dim, 1)]
            probs = jnp.exp(scores - log_total)
            prob_grad = dot_rows(lanes_of(wide_grad, mine), value)
            inner = jnp.sum(probs * prob_grad, axis=-1, keepdims=True)
            score_grad = (probs * (prob_grad - inner)).astype(jnp.bfloat16)
            dq = jnp.where(mine, dot_plain(score_grad, key), dq)
            dk = jnp.where(there, dot_columns(score_grad, query), dk)
            dv = jnp.where(there, dot_columns(probs.astype(jnp.bfloat16), grad), dv)
        dq_ref[rows, :] = dq * SCORE_SCALE
        if first + block == length:
            dk_sum[...] = dk
            dv_sum[...] = dv
        else:
            dk_sum[seen, :] += dk
            dv_sum[seen, :] += dv


PAIR = 128
BLOCK = 256


def attend_back(projected, log_total, mixed_grad, head_dim):
    length, columns = projected.shape
    wide = columns // 3
    pairs = wide // PAIR

    def kind(which):
        return pl.BlockSpec((length, PAIR), lambda p: (0, which * pairs + p))

    return pl.pallas_call(
        functools.partial(attend_back_kernel, head_dim, BLOCK),
        grid=(pairs,),
        in_specs=[kind(0), kind(1), kind(2), kind(0), kind(0)],
        out_specs=[pl.BlockSpec((length, PAIR), lambda p: (0, p))] * 3,
        out_shape=[jax.ShapeDtypeStruct((length, wide), jnp.float32)] * 3,
        compiler_params=pltpu.CompilerParams(vmem_limit_bytes=32 << 20),
        cost_estimate=pl.CostEstimate(
            flops=40 * length * length * wide // 5,
            bytes_accessed=18 * length * wide,
            transcendentals=length * length * wide // head_dim,
        ),
        name="attend_back",
    )(projected, projected, projected, log_total, mixed_grad)


def block_order(place):
    half = place // 2
    return (place, 1 + 4 * half - place, 2 - half, 3 - 3 * half)


def greet(dp_count, line):
    me, place = lax.axis_index("dp"), lax.axis_index("tensor")
    barrier = pltpu.get_barrier_semaphore()

    def plane(i, carry):
        pl.semaphore_signal(
            barrier, 1, device_id={"dp": lax.rem(me + i, dp_count)}, device_id_type=MESH
        )
        return carry

    lax.fori_loop(1, dp_count, plane, 0)
    for i in range(1, line):
        pl.semaphore_signal(
            barrier, 1, device_id={"tensor": lax.rem(place + i, line)}, device_id_type=MESH
        )
    pl.semaphore_wait(barrier, dp_count + line - 2)


class Line:
    def __init__(self, own, held, send_sem, recv_sem):
        self.own, self.held, self.send_sem, self.recv_sem = own, held, send_sem, recv_sem
        self.place = lax.axis_index("tensor")
        self.order = block_order(self.place)
        self.last = held.shape[0] - 1

    def copy(self, source, block, index, to):
        return pltpu.make_async_remote_copy(
            src_ref=source,
            dst_ref=self.held.at[block],
            send_sem=self.send_sem.at[index],
            recv_sem=self.recv_sem.at[block],
            device_id={"tensor": to},
            device_id_type=MESH,
        )

    def left(self):
        return self.copy(self.own, self.place, 0, self.place - 1)

    def right(self):
        return self.copy(self.own, self.place, self.last + 1, self.place + 1)

    def onward(self, step):
        block = self.order[step]
        up = self.copy(self.held.at[block], block, step, self.place + 1)
        down = self.copy(self.held.at[block], block, step, self.place - 1)
        return (
            (jnp.logical_and(block < self.place, self.place < self.last), up),
            (jnp.logical_and(block > self.place, self.place > 0), down),
        )

    def start(self):
        pl.when(self.place > 0)(lambda: self.left().start())
        pl.when(self.place < self.last)(lambda: self.right().start())

    def take(self, step):
        block = self.order[step]
        self.copy(self.held.at[block], block, step, block).wait_recv()
        for needed, copy in self.onward(step):
            pl.when(needed)(copy.start)

    def finish(self):
        pl.when(self.place > 0)(lambda: self.left().wait_send())
        pl.when(self.place < self.last)(lambda: self.right().wait_send())
        for step in range(1, self.last + 1):
            for needed, copy in self.onward(step):
                pl.when(needed)(copy.wait_send)


def slot_matrix(target_ref, block, first, count):
    target = target_ref[block, 0:1, :]
    slot = lax.broadcasted_iota(jnp.int32, (count, target.shape[1]), 0) + first
    return jnp.where(slot == target, 1.0, 0.0).astype(jnp.bfloat16)


class Plane:
    def __init__(self, piece, place_of, send_sem, recv_sem, local_sem, dp_count):
        self.piece, self.place_of = piece, place_of
        self.send_sem, self.recv_sem, self.local_sem = send_sem, recv_sem, local_sem
        self.me, self.dp_count = lax.axis_index("dp"), dp_count

    def copy(self, step, i):
        to = lax.rem(self.me + i, self.dp_count)
        return pltpu.make_async_remote_copy(
            src_ref=self.piece(step, to),
            dst_ref=self.place_of(step, self.me),
            send_sem=self.send_sem.at[step, i],
            recv_sem=self.recv_sem.at[step, i],
            device_id={"dp": to},
            device_id_type=MESH,
        )

    def own(self, step):
        return pltpu.make_async_copy(
            self.piece(step, self.me), self.place_of(step, self.me), self.local_sem.at[step]
        )

    def start(self, step):
        def one(i, carry):
            self.copy(step, i).start()
            return carry

        lax.fori_loop(1, self.dp_count, one, 0)
        self.own(step).start()

    def wait_recv(self, step):
        def one(i, carry):
            here = lax.rem(self.me + self.dp_count - i, self.dp_count)
            pltpu.make_async_remote_copy(
                src_ref=self.piece(step, self.me),
                dst_ref=self.place_of(step, here),
                send_sem=self.send_sem.at[step, i],
                recv_sem=self.recv_sem.at[step, i],
                device_id={"dp": here},
                device_id_type=MESH,
            ).wait_recv()
            return carry

        lax.fori_loop(1, self.dp_count, one, 0)
        self.own(step).wait()

    def wait_send(self, step):
        def one(i, carry):
            self.copy(step, i).wait_send()
            return carry

        lax.fori_loop(1, self.dp_count, one, 0)


def dispatch_block(rows, target_ref, block, slots, step, per):
    groups = slots.shape[1]
    chunk = 256 // per

    def one(i, carry):
        chosen = slot_matrix(target_ref, block, i * 256, 256)
        values = dot_plain(chosen, rows[...]).astype(jnp.bfloat16)
        slots[step, pl.ds(i * chunk, chunk)] = values.reshape((chunk, per) + values.shape[1:])
        return carry

    lax.fori_loop(0, groups // chunk, one, 0)


def collect_block(slots, target_ref, block, step, per):
    groups = slots.shape[1]
    chunk = 256 // per
    total = None
    for i in range(groups // chunk):
        chosen = slot_matrix(target_ref, block, i * 256, 256)
        values = slots[step, pl.ds(i * chunk, chunk)]
        term = dot_columns(chosen, values.reshape((256,) + values.shape[2:]))
        total = term if total is None else total + term
    return total


GELU_SCALE = 0.7978845608028654
GELU_CUBE = 0.044715


def expert_kernel(
    dp_count,
    rows_ref,
    target_ref,
    grads_ref,
    w_in_ref,
    w_out_ref,
    back_ref,
    result_ref,
    d_in_ref,
    d_out_ref,
    held,
    slots,
    arrived,
    grads,
    active,
    hidden_grad,
    sent_back,
    returned,
    far,
    line_send,
    line_recv,
    send_sem,
    recv_sem,
    back_send,
    back_recv,
    local_sem,
    back_local,
    grad_sem,
    far_send,
    far_recv,
    out_sem,
):
    line = held.shape[0]
    experts, _, _, per, width = arrived.shape
    place, me = lax.axis_index("tensor"), lax.axis_index("dp")
    order = block_order(place)
    rows_of = dp_count * per
    greet(dp_count, line)
    along = Line(rows_ref, held, line_send, line_recv)
    along.start()
    out_plane = Plane(
        lambda step, to: slots.at[step, pl.ds(to * experts, experts)],
        lambda step, at: arrived.at[:, step, at],
        send_sem,
        recv_sem,
        local_sem,
        dp_count,
    )
    back_plane = Plane(
        lambda step, to: sent_back.at[:, step, to],
        lambda step, at: returned.at[step, pl.ds(at * experts, experts)],
        back_send,
        back_recv,
        back_local,
        dp_count,
    )

    def grad_copy(step):
        return pltpu.make_async_copy(
            grads_ref.at[:, step], grads.at[:, step % 2], grad_sem.at[step]
        )

    def dispatch(step):
        if step:
            along.take(step)
        source = rows_ref if step == 0 else held.at[order[step]]
        dispatch_block(source, target_ref, order[step], slots, step, per)
        out_plane.start(step)

    half = dp_count // 2

    def forward(step):
        grad_copy(step).wait()
        for expert in range(experts):

            def one(i, carry):
                part = pl.ds(i * half, half)
                x = arrived[expert, step, part].reshape(half * per, width)
                g = grads[expert, step % 2, part].reshape(half * per, width)
                hidden = dot_plain(x, w_in_ref[expert])
                inner = GELU_SCALE * (hidden + GELU_CUBE * hidden * hidden * hidden)
                bend = jnp.tanh(inner)
                gate = 0.5 * (1.0 + bend)
                active[expert, part] = (
                    (hidden * gate).astype(jnp.bfloat16).reshape(half, per, -1)
                )
                slope = gate + 0.5 * hidden * (1.0 - bend * bend) * (
                    GELU_SCALE * (1.0 + 3.0 * GELU_CUBE * hidden * hidden)
                )
                change = (dot_rows(g, w_out_ref[expert]) * slope).astype(jnp.bfloat16)
                hidden_grad[expert, part] = change.reshape(half, per, -1)
                row_grad = dot_rows(change, w_in_ref[expert]).astype(jnp.bfloat16)
                sent_back[expert, step, part] = row_grad.reshape(half, per, width)
                return carry

            lax.fori_loop(0, 2, one, 0)
        back_plane.start(step)

    def result_copy(step, expert):
        return pltpu.make_async_copy(
            slots.at[step, pl.ds(expert * dp_count, dp_count)],
            result_ref.at[expert, order[step]],
            out_sem.at[step, expert],
        )

    def later(step):
        out_plane.wait_send(step)
        for expert in range(experts):
            a = active[expert].reshape(rows_of, -1)
            result = dot_plain(a, w_out_ref[expert]).astype(jnp.bfloat16)
            slots[step, pl.ds(expert * dp_count, dp_count)] = result.reshape(
                dp_count, per, width
            )
            result_copy(step, expert).start()
            g = grads[expert, step % 2].reshape(rows_of, width)
            x = arrived[expert, step].reshape(rows_of, width)
            change = hidden_grad[expert].reshape(rows_of, -1)
            if step == 0:
                d_out_ref[expert] = dot_columns(a, g)
                d_in_ref[expert] = dot_columns(x, change)
            else:
                d_out_ref[expert] += dot_columns(a, g)
                d_in_ref[expert] += dot_columns(x, change)

    mine = lax.rem(place, 2)
    mate = order[1]
    rows_half = rows_ref.shape[0] // 2
    kept = pl.ds(mine * rows_half, rows_half)
    passed = pl.ds((1 - mine) * rows_half, rows_half)

    def mate_copy():
        return pltpu.make_async_remote_copy(
            src_ref=held.at[1],
            dst_ref=far.at[0],
            send_sem=far_send.at[0],
            recv_sem=far_recv.at[0],
            device_id={"tensor": mate},
            device_id_type=MESH,
        )

    def half_copy(step):
        return pltpu.make_async_remote_copy(
            src_ref=held.at[step, passed],
            dst_ref=far.at[step, passed],
            send_sem=far_send.at[step - 1],
            recv_sem=far_recv.at[step - 1],
            device_id={"tensor": mate},
            device_id_type=MESH,
        )

    def owner_copy(step, part, at):
        return pltpu.make_async_remote_copy(
            src_ref=held.at[step, part],
            dst_ref=far.at[1, part],
            send_sem=far_send.at[step + 1],
            recv_sem=far_recv.at[3 + at],
            device_id={"tensor": order[step]},
            device_id_type=MESH,
        )

    grad_copy(0).start()
    grad_copy(1).start()
    dispatch(0)
    for step in range(line):
        if step + 1 < line:
            dispatch(step + 1)
        out_plane.wait_recv(step)
        forward(step)
        later(step)
        if step + 2 < line:
            grad_copy(step + 2).start()
    along.finish()
    back_plane.wait_recv(0)
    back_ref[...] = collect_block(returned, target_ref, order[0], 0, per)
    for step in range(1, line):
        back_plane.wait_recv(step)
        held[step] = collect_block(returned, target_ref, order[step], step, per).astype(
            jnp.bfloat16
        )
        if step == 1:
            mate_copy().start()
            continue
        half_copy(step).start()
        pltpu.make_async_remote_copy(
            src_ref=held.at[step, kept],
            dst_ref=far.at[step, kept],
            send_sem=far_send.at[step - 1],
            recv_sem=far_recv.at[step - 1],
            device_id={"tensor": mate},
            device_id_type=MESH,
        ).wait_recv()
        held[step, kept] = (
            held[step, kept].astype(jnp.float32) + far[step, kept].astype(jnp.float32)
        ).astype(jnp.bfloat16)
        owner_copy(step, kept, mine).start()
    mate_copy().wait()
    owner_copy(2, pl.ds(0, rows_half), 0).wait_recv()
    owner_copy(2, pl.ds(rows_half, rows_half), 1).wait_recv()
    back_ref[...] += far[0].astype(jnp.float32) + far[1].astype(jnp.float32)
    for step in range(line):
        back_plane.wait_send(step)
        for expert in range(experts):
            result_copy(step, expert).wait()
    for step in (2, 3):
        half_copy(step).wait_send()
        owner_copy(step, kept, mine).wait_send()


def run_experts(rows, targets, grads, w_in, w_out, dp_count, line):
    experts, _, _, per, width = grads.shape
    units = w_in.shape[2]
    low, dma = jnp.bfloat16, pltpu.SemaphoreType.DMA
    whole, far = pl.BlockSpec(memory_space=pltpu.VMEM), pl.BlockSpec(memory_space=pl.ANY)
    groups = dp_count * experts
    return pl.pallas_call(
        functools.partial(expert_kernel, dp_count),
        in_specs=[whole, whole, far, whole, whole],
        out_specs=[whole, far, whole, whole],
        out_shape=[
            jax.ShapeDtypeStruct(rows.shape, jnp.float32),
            jax.ShapeDtypeStruct(grads.shape, low),
            jax.ShapeDtypeStruct((experts, width, units), jnp.float32),
            jax.ShapeDtypeStruct((experts, units, width), jnp.float32),
        ],
        scratch_shapes=[
            pltpu.VMEM((line,) + rows.shape, low),
            pltpu.VMEM((line, groups, per, width), low),
            pltpu.VMEM(grads.shape, low),
            pltpu.VMEM((experts, 2, dp_count, per, width), low),
            pltpu.VMEM((experts, dp_count, per, units), low),
            pltpu.VMEM((experts, dp_count, per, units), low),
            pltpu.VMEM(grads.shape, low),
            pltpu.VMEM((line, groups, per, width), low),
            pltpu.VMEM((line,) + rows.shape, low),
            dma((line + 1,)),
            dma((line,)),
            dma((line, dp_count)),
            dma((line, dp_count)),
            dma((line, dp_count)),
            dma((line, dp_count)),
            dma((line,)),
            dma((line,)),
            dma((line,)),
            dma((line + 1,)),
            dma((line + 1,)),
            dma((line, experts)),
        ],
        compiler_params=pltpu.CompilerParams(
            collective_id=0, has_side_effects=True, vmem_limit_bytes=61 << 20
        ),
        cost_estimate=pl.CostEstimate(
            flops=12 * experts * line * dp_count * per * width * units,
            bytes_accessed=8 * grads.size,
            transcendentals=grads.size,
        ),
        name="experts",
    )(rows, targets, grads, w_in, w_out)


def norm_stats(values):
    center = jnp.mean(values, axis=-1, keepdims=True)
    centered = values - center
    inv_scale = lax.rsqrt(jnp.mean(centered * centered, axis=-1, keepdims=True) + EPSILON)
    return centered * inv_scale, inv_scale


def attend_pair(proj_ref, mixed_ref, log_ref, pair, head_dim):
    length = proj_ref.shape[0]
    wide = proj_ref.shape[1] // 3
    here = pl.ds(pair * PAIR, PAIR)
    lane = lax.broadcasted_iota(jnp.int32, (BLOCK, PAIR), 1)
    for first in range(0, length, BLOCK):
        rows, seen = pl.ds(first, BLOCK), pl.ds(0, first + BLOCK)
        wide_query = proj_ref[rows, here].astype(jnp.float32) * SCORE_SCALE
        key = proj_ref[seen, pl.ds(wide + pair * PAIR, PAIR)]
        value = proj_ref[seen, pl.ds(2 * wide + pair * PAIR, PAIR)]
        mixed = jnp.zeros((BLOCK, PAIR), jnp.float32)
        logs = jnp.zeros((BLOCK, PAIR), jnp.float32)
        for head in range(PAIR // head_dim):
            mine = lane // head_dim == head
            scores = masked_scores(lanes_of(wide_query, mine), key, first)
            top = jnp.max(scores, axis=-1, keepdims=True)
            powers = jnp.exp(scores - top)
            total = jnp.sum(powers, axis=-1, keepdims=True)
            probs = (powers * (1.0 / total)).astype(jnp.bfloat16)
            mixed = jnp.where(mine, dot_plain(probs, value), mixed)
            logs = jnp.where(mine, top + jnp.log(total), logs)
        mixed_ref[rows, here] = mixed.astype(jnp.bfloat16)
        log_ref[rows, here] = logs


def send(source, there, send_sem, recv_sem, **to):
    return pltpu.make_async_remote_copy(
        src_ref=source,
        dst_ref=there,
        send_sem=send_sem,
        recv_sem=recv_sem,
        device_id=to,
        device_id_type=MESH,
    )


class Share:
    def __init__(self, held, sems, dp_count):
        self.held, self.steps = held, dp_count // 2
        self.sems, self.dp_count = sems, dp_count
        self.me = lax.axis_index("dp")
        self.other = self.me + 1 - 2 * lax.rem(self.me, 2)

    def block(self, of, i):
        return lax.rem(of + self.dp_count - 2 * i, self.dp_count)

    def across(self, i):
        to = lax.rem(self.me + 2 * i, self.dp_count)
        mine = self.held.at[self.me]
        return send(mine, mine, self.sems.at[0, i], self.sems.at[1, i], dp=to)

    def within(self, i):
        piece = self.held.at[self.block(self.me, i)]
        return send(piece, piece, self.sems.at[2, i], self.sems.at[3, i], dp=self.other)

    def start(self):
        for i in range(1, self.steps):
            self.across(i).start()
        self.within(0).start()

    def relay(self):
        for i in range(1, self.steps):
            at = self.block(self.me, i)
            piece = self.held.at[at]
            send(piece, piece, self.sems.at[0, i], self.sems.at[1, i], dp=at).wait_recv()
            self.within(i).start()

    def finish(self):
        for i in range(self.steps):
            piece = self.held.at[self.block(self.other, i)]
            send(piece, piece, self.sems.at[2, i], self.sems.at[3, i], dp=self.other).wait_recv()

    def drain(self):
        for i in range(self.steps):
            if i:
                self.across(i).wait_send()
            self.within(i).wait_send()


def front_kernel(
    dp_count,
    head_dim,
    tokens_ref,
    cot_ref,
    own_target_ref,
    qkv_a_ref,
    qkv_b_ref,
    out_a_ref,
    out_b_ref,
    gains_ref,
    grads_ref,
    target_ref,
    wq_ref,
    wo_ref,
    first_ref,
    proj_ref,
    log_ref,
    mixed_ref,
    middle_ref,
    second_ref,
    held,
    slots,
    hop,
    out_parts,
    mixed_all,
    line_send,
    line_recv,
    send_sem,
    recv_sem,
    local_sem,
    target_send,
    target_recv,
    near_send,
    near_recv,
    mix_send,
    mix_recv,
    q_sems,
    o_sems,
):
    line = held.shape[0]
    experts, _, _, per, _ = grads_ref.shape
    rows = tokens_ref.shape[0]
    me, place = lax.axis_index("dp"), lax.axis_index("tensor")
    order = block_order(place)
    mate, across, last = order[1], lax.rem(place + 2, line), line - 1 - place
    part = lax.rem(place, 2)
    wide = proj_ref.shape[1] // 3
    greet(dp_count, line)

    near = [
        send(qkv_b_ref, hop, near_send.at[0], near_recv.at[0], tensor=across),
        send(out_a_ref, out_parts.at[1], near_send.at[1], near_recv.at[1], tensor=mate),
        send(out_b_ref, out_parts.at[0], near_send.at[2], near_recv.at[2], tensor=across),
        send(out_b_ref, out_parts.at[2], near_send.at[3], near_recv.at[3], tensor=last),
    ]
    for copy in near:
        copy.start()
    target_ref[place] = own_target_ref[...]

    def target_copy(i, at, to):
        return send(
            target_ref.at[at], target_ref.at[at], target_send.at[i], target_recv.at[i], tensor=to
        )

    for i in range(1, line):
        target_copy(i, place, lax.rem(place + i, line)).start()

    def first_rows(i, carry):
        values = tokens_ref[pl.ds(i * 128, 128), :].astype(jnp.float32)
        unit, _ = norm_stats(values)
        unit = unit * gains_ref[0:1, :] + gains_ref[1:2, :]
        first_ref[part, pl.ds(i * 128, 128), :] = unit.astype(jnp.bfloat16)
        return carry

    lax.fori_loop(0, rows // 128, first_rows, 0)
    first_copy = send(
        first_ref.at[part], first_ref.at[part], near_send.at[4], near_recv.at[4], tensor=mate
    )
    first_copy.start()
    along = Line(cot_ref, held, line_send, line_recv)
    along.start()
    near[0].wait_recv()
    for kind in range(3):
        base = kind * wide
        wq_ref[me, :, base : base + PAIR] = qkv_a_ref[:, base : base + PAIR]
        wq_ref[me, :, base + PAIR : base + wide] = (
            qkv_a_ref[:, base + PAIR : base + wide].astype(jnp.float32)
            + hop[kind].astype(jnp.float32)
        ).astype(jnp.bfloat16)
    share_q = Share(wq_ref, q_sems, dp_count)
    share_q.start()
    for copy in near[1:]:
        copy.wait_recv()
    for group, (a, b) in enumerate(((out_a_ref[...], 0), (out_parts[1], 2))):
        base = group * wide
        a = a.astype(jnp.float32)
        b = out_parts[b].astype(jnp.float32)
        wo_ref[me, :, base : base + PAIR] = a[:, :PAIR].astype(jnp.bfloat16)
        wo_ref[me, :, base + PAIR : base + 2 * PAIR] = (a[:, PAIR:] + b[:, :PAIR]).astype(
            jnp.bfloat16
        )
        wo_ref[me, :, base + 2 * PAIR : base + wide] = b[:, PAIR:].astype(jnp.bfloat16)
    share_o = Share(wo_ref, o_sems, dp_count)
    share_o.start()
    share_q.relay()

    plane = Plane(
        lambda step, to: slots.at[step, pl.ds(to * experts, experts)],
        lambda step, at: grads_ref.at[:, step, at],
        send_sem,
        recv_sem,
        local_sem,
        dp_count,
    )

    def dispatch(step):
        if step:
            along.take(step)
        source = cot_ref if step == 0 else held.at[order[step]]
        dispatch_block(source, target_ref, order[step], slots, step, per)
        plane.start(step)

    dispatch(0)
    share_o.relay()
    share_q.finish()
    send(
        first_ref.at[1 - part], first_ref.at[1 - part], near_send.at[4], near_recv.at[4], tensor=mate
    ).wait_recv()

    def project(i, carry):
        values = first_ref[i // 2, pl.ds(lax.rem(i, 2) * (rows // 2), rows // 2), :]
        weights = wq_ref[...].reshape(-1, 3 * wide)
        proj_ref[pl.ds(i * (rows // 2), rows // 2), :] = dot_plain(values, weights).astype(
            jnp.bfloat16
        )
        return carry

    lax.fori_loop(0, 4, project, 0)
    for i in range(1, line):
        target_copy(i, lax.rem(place + line - i, line), lax.rem(place + line - i, line)).wait_recv()

    def mix_copy(pair):
        here = pl.ds(pair * PAIR, PAIR)
        return send(
            mixed_all.at[pl.ds((1 - part) * rows, rows), here],
            mixed_ref.at[1, :, here],
            mix_send.at[pair],
            mix_recv.at[pair],
            tensor=mate,
        )

    for pair in range(wide // PAIR):
        dispatch(pair + 1)
        attend_pair(proj_ref, mixed_all, log_ref, pair, head_dim)
        mix_copy(pair).start()
    mixed_ref[0] = mixed_all[pl.ds(part * rows, rows), :]
    share_o.finish()
    for pair in range(wide // PAIR):
        mix_copy(pair).wait_recv()

    def finish_rows(i, carry):
        here = pl.ds(i * 128, 128)
        total = tokens_ref[here, :].astype(jnp.float32)
        total += dot_rows(mixed_ref[0, here, :], wo_ref[:, :, :wide].reshape(-1, wide)) + dot_rows(
            mixed_ref[1, here, :], wo_ref[:, :, wide:].reshape(-1, wide)
        )
        middle_ref[here, :] = total
        unit, _ = norm_stats(total)
        second_ref[here, :] = (unit * gains_ref[2:3, :] + gains_ref[3:4, :]).astype(jnp.bfloat16)
        return carry

    lax.fori_loop(0, rows // 128, finish_rows, 0)
    along.finish()
    share_q.drain()
    share_o.drain()
    for copy in near:
        copy.wait_send()
    first_copy.wait_send()
    for i in range(1, line):
        target_copy(i, place, lax.rem(place + i, line)).wait_send()
    for pair in range(wide // PAIR):
        mix_copy(pair).wait_send()
    for step in range(line):
        plane.wait_recv(step)
        plane.wait_send(step)


def run_front(tokens, cotangent, target, weights, gains, sizes):
    dp_count, line, experts, per, head_dim = sizes
    rows, width = tokens.shape
    qkv_a, qkv_b, out_a, out_b = weights
    share, columns = qkv_a.shape
    wide = columns // 3
    low, dma = jnp.bfloat16, pltpu.SemaphoreType.DMA
    whole, far = pl.BlockSpec(memory_space=pltpu.VMEM), pl.BlockSpec(memory_space=pl.ANY)
    shape = jax.ShapeDtypeStruct
    return pl.pallas_call(
        functools.partial(front_kernel, dp_count, head_dim),
        in_specs=[whole] * 8,
        out_specs=[far] + [whole] * 9,
        out_shape=[
            shape((experts, line, dp_count, per, width), low),
            shape((line,) + target.shape, jnp.int32),
            shape((dp_count, share, columns), low),
            shape((dp_count, share, 2 * wide), low),
            shape((2, rows, width), low),
            shape((2 * rows, columns), low),
            shape((2 * rows, wide), jnp.float32),
            shape((2, rows, wide), low),
            shape((rows, width), jnp.float32),
            shape((rows, width), low),
        ],
        scratch_shapes=[
            pltpu.VMEM((line, rows, width), low),
            pltpu.VMEM((line, dp_count * experts, per, width), low),
            pltpu.VMEM(qkv_b.shape, low),
            pltpu.VMEM((3,) + out_b.shape, low),
            pltpu.VMEM((2 * rows, wide), low),
            dma((line + 1,)),
            dma((line,)),
            dma((line, dp_count)),
            dma((line, dp_count)),
            dma((line,)),
            dma((line,)),
            dma((line,)),
            dma((5,)),
            dma((5,)),
            dma((wide // PAIR,)),
            dma((wide // PAIR,)),
            dma((4, dp_count // 2)),
            dma((4, dp_count // 2)),
        ],
        compiler_params=pltpu.CompilerParams(
            collective_id=1, has_side_effects=True, vmem_limit_bytes=56 << 20
        ),
        name="front",
    )(tokens, cotangent, target, *weights, gains)


def product(spec, left, right):
    return jnp.einsum(spec, left, right, preferred_element_type=jnp.float32)


def on_device(
    tokens,
    token_ids,
    hash_table,
    ln1_gain,
    ln1_bias,
    w_qkv,
    w_out,
    ln2_gain,
    ln2_bias,
    expert_in,
    expert_out,
    cotangent,
):
    low = jnp.bfloat16
    row_count, model_width = tokens.shape
    local_experts = expert_in.shape[0]
    dp_count = lax.axis_size("dp")
    line = lax.axis_size("tensor")
    shares = LEN // row_count
    place = lax.axis_index("tensor")
    part = place % shares
    swap = [(t, t ^ 1) for t in range(line)]
    hop = [(t, t ^ 2) for t in range(line)]
    head_dim = w_qkv.shape[2] // 3
    heads_shard = w_qkv.shape[1]

    def swapped(values):
        return lax.ppermute(values, "tensor", swap)

    def joined(own, other):
        both = jnp.stack([own, other])
        return jnp.where(part == 0, both, both[::-1]).reshape((-1,) + own.shape[1:])

    def halves(both):
        pair = both.reshape((shares, -1) + both.shape[1:])
        return (
            lax.dynamic_index_in_dim(pair, part, 0, False),
            lax.dynamic_index_in_dim(pair, 1 - part, 0, False),
        )

    experts_total = dp_count * local_experts
    capacity = 2 * row_count // experts_total
    slot_count = experts_total * capacity
    expert_of = jnp.take(hash_table, token_ids)
    one_hot = (expert_of[:, None] == jnp.arange(experts_total, dtype=jnp.int32)[None, :]).astype(
        jnp.int32
    )
    before = (
        lax.broadcasted_iota(jnp.int32, (row_count, row_count), 0)
        > lax.broadcasted_iota(jnp.int32, (row_count, row_count), 1)
    ).astype(low)
    earlier = jnp.dot(before, one_hot.astype(low), preferred_element_type=jnp.float32)
    slot_rank = jnp.sum(earlier.astype(jnp.int32) * one_hot, axis=1)
    target = jnp.where(slot_rank < capacity, expert_of * capacity + slot_rank, slot_count)
    own_target = jnp.broadcast_to(target[None, :], (8, row_count))

    share = w_qkv.shape[0]
    wide = 2 * heads_shard * head_dim
    by_kind = w_qkv.astype(low).reshape(share, heads_shard, 3, head_dim).transpose(0, 2, 1, 3)
    qkv_a = jnp.pad(by_kind.reshape(share, 3, -1), ((0, 0), (0, 0), (0, wide // 2)))
    qkv_b = jnp.concatenate([by_kind[:, :, -1:], by_kind[:, :, :-1]], axis=2).reshape(share, 3, -1)
    qkv_b = jnp.pad(qkv_b, ((0, 0), (0, 0), (head_dim, 0))).transpose(1, 0, 2)
    out_rows = w_out.astype(low).T
    out_a = jnp.pad(out_rows, ((0, 0), (0, head_dim)))
    out_b = jnp.concatenate([out_rows[:, -head_dim:], out_rows[:, :-head_dim]], axis=1)
    out_b = jnp.pad(out_b, ((0, 0), (head_dim, 0)))
    gains = jnp.stack([ln1_gain, ln1_bias, ln2_gain, ln2_bias])
    sizes = (dp_count, line, local_experts, capacity, head_dim)
    (
        grad_rows,
        targets,
        qkv_weight,
        out_weight,
        first_all,
        projected,
        log_total,
        mixed_pair,
        middle,
        second_low,
    ) = run_front(
        tokens,
        cotangent,
        own_target,
        (qkv_a.reshape(share, -1), qkv_b, out_a, out_b),
        jnp.pad(gains, ((0, 4), (0, 0))),
        sizes,
    )
    qkv_flat = qkv_weight.reshape(model_width, -1)
    out_weight = out_weight.reshape(model_width, -1)
    first_all = first_all.reshape(LEN, model_width)
    residual = tokens.astype(jnp.float32)
    _, unit_one, scale_one = normalize(residual, ln1_gain, ln1_bias)
    _, unit_two, scale_two = normalize(middle, ln2_gain, ln2_bias)

    out_grad = cotangent.astype(jnp.float32)
    second_grad, result, grad_expert_in, grad_expert_out = run_experts(
        second_low,
        targets,
        grad_rows,
        expert_in.astype(low),
        expert_out.astype(low),
        dp_count,
        line,
    )
    gain_two_grad = jnp.sum(second_grad * unit_two, axis=0)
    bias_two_grad = jnp.sum(second_grad, axis=0)
    middle_grad = out_grad + norm_back(second_grad, unit_two, scale_two, ln2_gain)
    middle_low = middle_grad.astype(low)
    mixed_both = product("td,dk->tk", middle_low, out_weight).astype(low)
    mixed_grad = joined(mixed_both[:, :wide], swapped(mixed_both[:, wide:]))
    result, mixed_grad = lax.optimization_barrier((result, mixed_grad))
    result = lax.all_to_all(result.transpose(2, 0, 1, 3, 4), "dp", split_axis=0, concat_axis=0)
    result = result.transpose(2, 0, 1, 3, 4).reshape(line, slot_count, model_width)
    chosen = (
        jnp.arange(slot_count, dtype=jnp.int32)[None, :, None] == targets[:, :1, :]
    ).astype(low)
    rows = product("bsr,bsd->brd", chosen, result).astype(low)
    rows = rows.reshape(line * row_count, model_width)
    rows = lax.psum_scatter(rows, "tensor", scatter_dimension=0, tiled=True)
    mixed_out = middle + rows.astype(jnp.float32)
    out_wgrad = product("td,ptk->dpk", middle_low, mixed_pair).reshape(model_width, -1).astype(low)
    out_part = lax.psum_scatter(out_wgrad, "dp", scatter_dimension=0, tiled=True)
    half = wide // 2

    def swap_last(values):
        return jnp.concatenate([values[:, head_dim:], values[:, :head_dim]], axis=1)

    pieces = (
        out_part[:, :half],
        out_part[:, wide : wide + half],
        swap_last(out_part[:, half:wide]),
        swap_last(out_part[:, wide + half :]),
    )
    out_total = pieces[0].astype(jnp.float32)
    for i in range(1, line):
        sent = lax.ppermute(pieces[i], "tensor", [(t, t ^ i) for t in range(line)])
        out_total = out_total + sent.astype(jnp.float32)
    out_total = out_total.T

    qkv_grad = jnp.concatenate(attend_back(projected, log_total, mixed_grad, head_dim), axis=1).astype(low)
    qkv_wgrad = product("td,tk->dk", first_all, qkv_grad).astype(low)
    qkv_part = lax.psum_scatter(qkv_wgrad, "dp", scatter_dimension=0, tiled=True)
    qkv_part = qkv_part.reshape(share, 3, wide)
    qkv_far = qkv_part[:, :, half:]
    qkv_far = jnp.concatenate([qkv_far[:, :, head_dim:], qkv_far[:, :, :head_dim]], axis=2)
    qkv_far = lax.ppermute(qkv_far, "tensor", hop)
    qkv_total = qkv_part[:, :, :half].astype(jnp.float32) + qkv_far.astype(jnp.float32)
    qkv_total = qkv_total.reshape(share, 3, heads_shard, head_dim).transpose(0, 2, 1, 3)
    qkv_total = qkv_total.reshape(w_qkv.shape)
    first_own, first_sent = halves(product("tk,dk->td", qkv_grad, qkv_flat))
    first_grad = first_own + swapped(first_sent.astype(low)).astype(jnp.float32)
    gain_one_grad = jnp.sum(first_grad * unit_one, axis=0)
    bias_one_grad = jnp.sum(first_grad, axis=0)
    input_grad = middle_grad + norm_back(first_grad, unit_one, scale_one, ln1_gain)
    norm_sums = lax.psum(
        (gain_one_grad, bias_one_grad, gain_two_grad, bias_two_grad), ("dp", "tensor")
    )
    return (
        mixed_out.astype(low),
        input_grad.astype(low),
        norm_sums[0],
        norm_sums[1],
        qkv_total,
        out_total,
        norm_sums[2],
        norm_sums[3],
        grad_expert_in,
        grad_expert_out,
    )


def solution(mesh):
    rows = P(("dp", "tensor"), None)
    weights = (P("dp", "tensor", None), P("tensor", "dp"))
    experts = (P("dp", None, "tensor"), P("dp", "tensor", None))
    return jax.shard_map(
        on_device,
        mesh=mesh,
        in_specs=(rows, P(("dp", "tensor")), P(), P(), P(), *weights, P(), P(), *experts, rows),
        out_specs=(rows, rows, P(), P(), *weights, P(), P(), *experts),
        check_vma=False,
    )
```

time: 794 us -> 562 us (0.71)
  Pallas kernels: 0 us -> 322 us
  waiting for transfers between devices: 356 us -> 79.8 us
  matrix products: 178 us -> 15.5 us
  blocking collectives: 81.7 us -> 46.2 us
  local copies, waits for them, and re-layouts: 69 us -> 40.1 us
  other arithmetic: 49 us -> 22.7 us
  starting transfers between devices: 33.1 us -> 13.1 us
    pallas_call x0 -> x3, Pallas kernels: none -> 322 us  [the longest x1 186 us: run_experts(): pl.pallas_call(functools.partial(expert_kernel, dp_count), in_specs=[whol...]
    all_to_all x4 -> x1, waiting for transfers between devices: 182 us -> 47.3 us  [on_device(): lax.all_to_all(result.transpose(2, 0, 1, 3, 4), 'dp', split_axis=0, conca...]
    all_gather x4 -> x0, waiting for transfers between devices: 112 us -> none  [the longest x2 112 us: dispatch(): rows = lax.all_gather(values, 'tensor', axis=0)]
    dot_general x18 -> x5, matrix products: 113 us -> 15.2 us  [product(): return jnp.einsum(spec, left, right, preferred_element_type=jnp.float32)]
    dot_general x7 -> x0, matrix products: 64.7 us -> none  [the longest x1 16.5 us: attend_back(): jnp.einsum('qhd,khd->hqk', mixed_grad, value_rows, preferred_element_type...]
    all_gather x2 -> x0, blocking collectives: 40.8 us -> none  [the longest x1 28.6 us: on_device(): out_rows = lax.all_gather(w_out.astype(low), 'tensor', axis=0)]
    reduce_scatter x2 -> x1, waiting for transfers between devices: 37.6 us -> 0.01 us  [on_device(): rows = lax.psum_scatter(rows, 'tensor', scatter_dimension=0, tiled=True)]
    convert_element_type x6 -> x3, other arithmetic: 23.1 us -> 8.13 us  [the longest x1 4.12 us: on_device(): expert_in.astype(low)]
  transfers between devices with their start and end apart: 21 -> 10, of which waited for: 12 -> 6; matrix products, arithmetic and copies ran while one was open for 31% -> 6% of each run, Pallas kernels for 0% -> 3%
where the time goes in v3:
time: 562 us; the launch traced here: 554 us
  Pallas kernels  322 us (57%)
  waiting for transfers between devices  79.8 us (14%)
  blocking collectives  46.2 us (8%)
  local copies, waits for them, and re-layouts  40.1 us (7%)
  other arithmetic  22.7 us (4%)
  matrix products  15.5 us (3%)
  between operations  14.8 us (3%)
  starting transfers between devices  13.1 us (2%)
    pallas_call x1, Pallas kernels, run_experts(): pl.pallas_call(functools.partial(expert_kernel, dp_count), in_specs=[whol...  186 us
    pallas_call x1, Pallas kernels, run_front(): pl.pallas_call(functools.partial(front_kernel, dp_count, head_dim), in_sp...  118 us
    all_to_all x1, waiting for transfers between devices, on_device(): lax.all_to_all(result.transpose(2, 0, 1, 3, 4), 'dp', split_axis=0, conca...  47.3 us
    psum x1, blocking collectives, on_device(): lax.psum((gain_one_grad, bias_one_grad, gain_two_grad, bias_two_grad), ('...  46.2 us
    ppermute x2, waiting for transfers between devices, swapped(): return lax.ppermute(values, 'tensor', swap)  24 us
    unnamed x63, local copies, waits for them, and re-layouts  19.5 us
    pallas_call x1, Pallas kernels, attend_back(): pl.pallas_call(functools.partial(attend_back_kernel, head_dim, BLOCK), gr...  17.7 us
    dot_general x5, matrix products, product(): return jnp.einsum(spec, left, right, preferred_element_type=jnp.float32)  15.2 us
  transfers between devices with their start and end apart: 10, of which 6 were waited for; matrix products, arithmetic and copies ran while one was open for 6% of the time, Pallas kernels for 3%

profile of v3, /device:TPU:0, one launch (start us, length us, event | category | flops | bytes accessed | tf_op | source)
XLA Modules:
  0.0 553.8 jit_solution(7317443933092557204)
XLA Ops:
  7.2 1.2 copy.50
  8.4 1.0 copy.55
  9.6 0.8 pad_bitcast_fusion.qkv_b_ref
  11.1 0.9 copy.66.qkv_a_ref
  12.0 3.1 gather_fusion
  15.6 4.1 convert_element_type.100.w_in_ref
  19.7 1.6 convert_element_type.101.w_out_ref
  21.3 0.7 fusion.34.out_b_ref
  23.3 117.8 %front.1 = (bf16[2,4,8,64,768]{4,3,2,1,0:T(8,128)(2,1)}, s32[4,8,512]{2,1,0:T(8,128)}, bf16[8,96,1152]{2,1,0:T(8,128)(2,1)}, bf16[8,96,768]{2,1,0:T(8,128)(2,1)}...) custom-call(bf16[512,768]{1,0:T(8,128)(2,1)} %tokens_ref.1, ...), custom_call_target="tpu_custom_call" | custom-call | tf_op jit(solution)/shard_map/front/pallas_call | solution.py:830
  141.1 1.7 reduce_sum.118
  143.2 186.1 %experts.1 = (f32[512,768]{1,0:T(8,128)}, bf16[2,4,8,64,768]{4,3,2,1,0:T(8,128)(2,1)}, f32[2,768,768]{2,1,0:T(8,128)}, f32[2,768,768]{2,1,0:T(8,128)}) custom-call(bf16[512,768]{1,0:T(8,128)(2,1)} %get-tuple-element.31.rows_ref, s32[4,8,512]{2,1,0:T(8,128)} %get-tuple-element.30.target_ref, bf16[2,4,8,64,768]{4,3,2,1,0:T(8,128)(2,1)} %get-tuple-element.32.grads_ref, ...), custom_call_target="tpu_custom_call" | custom-call | flops 28991029248 | bytes 25165824 | tf_op jit(solution)/shard_map/experts/pallas_call | solution.py:502
  329.4 2.3 multiply_reduce_fusion
  332.3 0.7 copy-done.21
  333.0 0.8 convolution_convert_fusion.2
  333.9 0.8 collective-permute-start
  334.6 9.7 %collective-permute-done = bf16[512,384]{1,0:T(8,128)(2,1)S(1)} collective-permute-done((bf16[512,384]{1,0:T(8,128)(2,1)S(1)}, bf16[512,384]{1,0:T(8,128)(2,1)S(1)}, u32[]{:S(2)}, u32[]{:S(2)}) %collective-permute-start) | collective-permute-done | bytes 393248 | tf_op jit(solution)/shard_map/ppermute | solution.py:905
  344.6 6.2 %copy.56 = bf16[8,2,4,64,768]{4,3,2,1,0:T(8,128)(2,1)} copy(bf16[8,2,4,64,768]{4,3,0,2,1:T(8,128)(2,1)} %bitcast.53) | data formatting | bytes 12582912 | tf_op jit(solution)/shard_map/transpose | solution.py:989
  350.8 6.4 %all-to-all-start = ((bf16[8,2,4,64,768]{4,3,2,1,0:T(8,128)(2,1)}), bf16[8,2,4,64,768]{4,3,2,1,0:T(8,128)(2,1)}, u32[]{:S(2)}, u32[]{:S(2)}) async-start(bf16[8,2,4,64,768]{4,3,2,1,0:T(8,128)(2,1)} %copy.56), calls=%async_computation | async-start | bytes 12582912 | tf_op jit(solution)/shard_map/all_to_all | solution.py:989
  357.3 1.8 convolution_convert_fusion.1
  359.1 2.5 copy.67
  361.7 1.4 copy-done.3
  363.1 17.7 %attend_back.1 = (f32[1024,384]{1,0:T(8,128)S(1)}, f32[1024,384]{1,0:T(8,128)S(1)}, f32[1024,384]{1,0:T(8,128)S(1)}) custom-call(bf16[1024,1152]{1,0:T(8,128)(2,1)S(1)} %copy-done.2, bf16[1024,1152]{1,0:T(8,128)(2,1)S(1)} %copy-done.2, bf16[1024,1152]{1,0:T(8,128)(2,1)S(1)} %copy-done.2, f32[1024,384]{1,0:T(8,128)S(1)} %copy-done.3, ...), custom_call_target="tpu_custom_call" | custom-call | flops 3221225472 | bytes 7077888 | tf_op jit(solution)/shard_map/attend_back/pallas_call | solution.py:109
  381.1 1.3 copy-done.20
  382.4 3.5 convolution_convert_fusion
  386.0 0.8 slice.61
  386.9 47.3 %all-to-all-done = bf16[8,2,4,64,768]{4,3,2,1,0:T(8,128)(2,1)} async-done(((bf16[8,2,4,64,768]{4,3,2,1,0:T(8,128)(2,1)}), bf16[8,2,4,64,768]{4,3,2,1,0:T(8,128)(2,1)}, u32[]{:S(2)}, u32[]{:S(2)}) %all-to-all-start) | async-done | bytes 6291488 | tf_op jit(solution)/shard_map/all_to_all | solution.py:989
  434.2 3.3 copy.57
  437.5 5.1 fusion.13
  442.6 4.0 fusion.2
  446.6 1.7 copy-done.13
  448.5 1.0 copy-done.6
  450.0 14.3 %collective-permute-done.1 = bf16[512,768]{1,0:T(8,128)(2,1)} collective-permute-done((bf16[512,768]{1,0:T(8,128)(2,1)S(1)}, bf16[512,768]{1,0:T(8,128)(2,1)}, u32[]{:S(2)}, u32[]{:S(2)}) %collective-permute-start.1) | collective-permute-done | bytes 786464 | tf_op jit(solution)/shard_map/ppermute | solution.py:905
  464.3 3.6 fusion.24
  467.9 46.2 %all-reduce.5 = (f32[768]{0:T(1024)}, f32[768]{0:T(1024)}, f32[768]{0:T(1024)}, f32[768]{0:T(1024)}) all-reduce(f32[768]{0:T(1024)S(1)} %get-tuple-element.80, f32[768]{0:T(1024)S(1)} %get-tuple-element.85, f32[768]{0:T(1024)S(1)} %get-tuple-element.78, ...), channel_id=1, replica_groups=mesh['dp'=8,'tensor'=4] {'dp','tensor'}, use_global_device_ids=true, to_apply=%region_11.12 | all-reduce | flops 3072 | bytes 24576 | tf_op jit(solution)/shard_map/psum | solution.py:1032
  514.2 2.9 fusion.23
  517.0 0.8 fusion.39
  517.9 0.8 fusion.40
  518.9 1.2 collective-permute-start.4
  520.3 2.1 collective-permute-start.5
  522.4 0.8 fusion.38
  523.9 1.0 reshape.139
  525.2 2.1 collective-permute-start.2
  527.2 1.7 collective-permute-done.4
  530.0 6.3 %collective-permute-done.2 = bf16[96,3,192]{2,0,1:T(8,128)(2,1)S(1)} collective-permute-done((bf16[96,3,192]{2,0,1:T(8,128)(2,1)S(1)}, bf16[96,3,192]{2,0,1:T(8,128)(2,1)S(1)}, u32[]{:S(2)}, u32[]{:S(2)}) %collective-permute-start.2) | collective-permute-done | bytes 110624 | tf_op jit(solution)/shard_map/ppermute | solution.py:1023
  536.5 0.9 copy.64
  537.4 2.4 add_convert_fusion
  539.8 4.9 copy.84
  544.7 2.2 copy.85
  (115 shorter events, 7.7 us)
Async XLA Ops:
  7.2 4.8 copy-start
  8.4 3.6 copy-start.17
  11.1 4.4 copy-start.16
  11.1 4.4 copy-start.18
  11.1 4.4 copy-start.15
  11.1 4.4 copy-start.19
  15.6 4.1 copy-start.11
  141.0 1.9 copy-start.4
  329.4 2.3 copy-start.10
  329.4 2.3 copy-start.12
  331.7 1.3 copy-start.21
  332.3 1.5 copy-start.7
  333.9 10.5 %collective-permute-start = (bf16[512,384]{1,0:T(8,128)(2,1)S(1)}, bf16[512,384]{1,0:T(8,128)(2,1)S(1)}, u32[]{:S(2)}, u32[]{:S(2)}) collective-permute-start(bf16[512,384]{1,0:T(8,128)(2,1)S(1)} %get-tuple-element.92), channel_id=1, source_target_pairs={{0,1},{1,0},{2,3},{3,2},{4,5},{5,4},{6,7},{7,6},{8,9},{9,8},{10,11... | collective-permute-start | bytes 1179656 | tf_op jit(solution)/shard_map/ppermute | solution.py:905
  350.8 6.4 %copy-start.8 = (f32[512,768]{1,0:T(8,128)S(1)}, f32[512,768]{1,0:T(8,128)}, u32[]{:S(2)}) copy-start(f32[512,768]{1,0:T(8,128)} %copy-done.7) | copy-start | bytes 4718596
  350.8 6.4 %copy-start.14 = (bf16[2,512,384]{2,1,0:T(8,128)(2,1)S(1)}, bf16[2,512,384]{2,1,0:T(8,128)(2,1)}, u32[]{:S(2)}) copy-start(bf16[2,512,384]{2,1,0:T(8,128)(2,1)} %get-tuple-element.45) | copy-start | bytes 2359300
  350.8 83.4 %all-to-all-start = ((bf16[8,2,4,64,768]{4,3,2,1,0:T(8,128)(2,1)}), bf16[8,2,4,64,768]{4,3,2,1,0:T(8,128)(2,1)}, u32[]{:S(2)}, u32[]{:S(2)}) async-start(bf16[8,2,4,64,768]{4,3,2,1,0:T(8,128)(2,1)} %copy.56), calls=%async_computation | async-start | bytes 12582912 | tf_op jit(solution)/shard_map/all_to_all | solution.py:989
  357.2 159.8 %reduce-scatter.10.cloned.1.call-start = ((), (), s32[]{:S(2)}) async-start(), calls=%async_computation.6 | async-start | bytes 1327104
  359.1 2.6 copy-start.2
  361.7 162.2 %reduce-scatter.8.cloned.1.call-start = ((), (), s32[]{:S(2)}) async-start(), calls=%async_computation.5 | async-start | bytes 1990656 | tf_op jit(solution)/shard_map/reduce_scatter | solution.py:1019
  361.7 1.4 copy-start.3
  381.0 1.4 copy-start.20
  386.0 151.4 %reduce-scatter.6.cloned.1.call-start = ((), (), s32[]{:S(2)}) async-start(), calls=%async_computation.4 | async-start | bytes 3932160 | tf_op jit(solution)/shard_map/reduce_scatter | solution.py:996
  446.6 1.7 copy-start.13
  448.3 1.1 copy-start.6
  448.4 15.9 %collective-permute-start.1 = (bf16[512,768]{1,0:T(8,128)(2,1)S(1)}, bf16[512,768]{1,0:T(8,128)(2,1)}, u32[]{:S(2)}, u32[]{:S(2)}) collective-permute-start(bf16[512,768]{1,0:T(8,128)(2,1)S(1)} %fusion.28), channel_id=1, source_target_pairs={{0,1},{1,0},{2,3},{3,2},{4,5},{5,4},{6,7},{7,6},{8,9},{9,8},{10,11... | collective-permute-start | bytes 2359304 | tf_op jit(solution)/shard_map/ppermute | solution.py:905
  450.0 64.2 %copy-start.9 = (f32[512,768]{1,0:T(8,128)S(1)}, f32[512,768]{1,0:T(8,128)}, u32[]{:S(2)}) copy-start(f32[512,768]{1,0:T(8,128)} %copy-done.7) | copy-start | bytes 4718596
  518.9 10.0 %collective-permute-start.4 = (bf16[96,192]{0,1:T(8,128)(2,1)S(1)}, bf16[96,192]{0,1:T(8,128)(2,1)S(1)}, u32[]{:S(2)}, u32[]{:S(2)}) collective-permute-start(bf16[96,192]{0,1:T(8,128)(2,1)S(1)} %pad_maximum_fusion.3), channel_id=1, source_target_pairs={{0,2},{1,3},{2,0},{3,1},{4,6},{5,7},{6,4},{7,5},{8,10},{9,11},{10,... | collective-permute-start | bytes 110600 | tf_op jit(solution)/shard_map/ppermute | solution.py:1013
  520.3 8.6 %collective-permute-start.5 = (bf16[96,192]{0,1:T(8,128)(2,1)S(1)}, bf16[96,192]{0,1:T(8,128)(2,1)S(1)}, u32[]{:S(2)}, u32[]{:S(2)}) collective-permute-start(bf16[96,192]{0,1:T(8,128)(2,1)S(1)} %pad_maximum_fusion.4), channel_id=1, source_target_pairs={{0,3},{1,2},{2,1},{3,0},{4,7},{5,6},{6,5},{7,4},{8,11},{9,10},{10,... | collective-permute-start | bytes 110600 | tf_op jit(solution)/shard_map/ppermute | solution.py:1013
  523.3 6.0 %collective-permute-start.3 = (bf16[96,192]{0,1:T(8,128)(2,1)S(1)}, bf16[96,192]{0,1:T(8,128)(2,1)S(1)}, u32[]{:S(2)}, u32[]{:S(2)}) collective-permute-start(bf16[96,192]{0,1:T(8,128)(2,1)S(1)} %copy.74), channel_id=1, source_target_pairs={{0,1},{1,0},{2,3},{3,2},{4,5},{5,4},{6,7},{7,6},{8,9},{9,8},{10,11... | collective-permute-start | bytes 110600 | tf_op jit(solution)/shard_map/ppermute | solution.py:1013
  525.1 12.2 %copy-start.5 = (f32[512,768]{1,0:T(8,128)S(1)}, f32[512,768]{1,0:T(8,128)}, u32[]{:S(2)}) copy-start(f32[512,768]{1,0:T(8,128)} %get-tuple-element.29) | copy-start | bytes 4718596
  525.2 11.1 %collective-permute-start.2 = (bf16[96,3,192]{2,0,1:T(8,128)(2,1)S(1)}, bf16[96,3,192]{2,0,1:T(8,128)(2,1)S(1)}, u32[]{:S(2)}, u32[]{:S(2)}) collective-permute-start(bf16[96,3,192]{2,0,1:T(8,128)(2,1)S(1)} %pad_maximum_fusion.2), channel_id=1, source_target_pairs={{0,2},{1,3},{2,0},{3,1},{4,6},{5,7},{6,4},{7,5},{8,10},{9,11},{10,... | collective-permute-start | bytes 331784 | tf_op jit(solution)/shard_map/ppermute | solution.py:1023
  537.4 7.3 %slice-start = ((s8[4718592]{0:T(1024)(128)(4,1)}), s8[4194304]{0:T(1024)(128)(4,1)S(1)}, s32[]{:S(2)}) async-start(s8[4718592]{0:T(1024)(128)(4,1)} %bitcast.56), calls=%async_computation.7 | async-start | bytes 8388608
  539.8 4.9 slice-start.1
  544.7 2.2 copy-start.1
Sparse Core Ops, SparseCore 0:
  361.8 52.2 reduce-scatter.9
  417.8 44.3 reduce-scatter.7
  465.2 63.0 reduce-scatter.5

commit v4 on v3

--- a/solution.py
+++ b/solution.py
@@ -14,25 +14,6 @@
 SCORE_SCALE = 0.125
 MASKED = -1e30
 MESH = pl.DeviceIdType.MESH
-
-
-def normalize(values, norm_gain, norm_shift):
-    center = jnp.mean(values, axis=-1, keepdims=True)
-    centered = values - center
-    inv_scale = lax.rsqrt(jnp.mean(centered * centered, axis=-1, keepdims=True) + EPSILON)
-    unit_rows = centered * inv_scale
-    return (unit_rows * norm_gain + norm_shift, unit_rows, inv_scale)
-
-
-def norm_back(grad_rows, unit_rows, inv_scale, norm_gain):
-    scaled = grad_rows * norm_gain
-    mean_plain = jnp.mean(scaled, axis=-1, keepdims=True)
-    mean_unit = jnp.mean(scaled * unit_rows, axis=-1, keepdims=True)
-    return inv_scale * (scaled - mean_plain - unit_rows * mean_unit)
-
-
-def smooth(values):
-    return jax.nn.gelu(values, approximate=True)
 
 
 def lanes_of(values, mask):
@@ -60,66 +41,8 @@
     return edge if first == 0 else jnp.concatenate([scores[:, :first], edge], axis=1)
 
 
-def attend_back_kernel(head_dim, block, q_ref, k_ref, v_ref, log_ref, grad_ref, dq_ref, dk_sum, dv_sum):
-    length, width = q_ref.shape
-    lane = lax.broadcasted_iota(jnp.int32, (block, width), 1)
-    for first in reversed(range(0, length, block)):
-        rows = pl.ds(first, block)
-        seen = pl.ds(0, first + block)
-        lanes_seen = lax.broadcasted_iota(jnp.int32, (first + block, width), 1)
-        wide_query = q_ref[rows, :].astype(jnp.float32) * SCORE_SCALE
-        key, value, grad = k_ref[seen, :], v_ref[seen, :], grad_ref[rows, :]
-        query, wide_grad = wide_query.astype(jnp.bfloat16), grad.astype(jnp.float32)
-        dq = jnp.zeros((block, width), jnp.float32)
-        dk = jnp.zeros((first + block, width), jnp.float32)
-        dv = jnp.zeros((first + block, width), jnp.float32)
-        for head in range(width // head_dim):
-            mine = lane // head_dim == head
-            there = lanes_seen // head_dim == head
-            scores = masked_scores(lanes_of(wide_query, mine), key, first)
-            log_total = log_ref[rows, pl.ds(head * head_dim, 1)]
-            probs = jnp.exp(scores - log_total)
-            prob_grad = dot_rows(lanes_of(wide_grad, mine), value)
-            inner = jnp.sum(probs * prob_grad, axis=-1, keepdims=True)
-            score_grad = (probs * (prob_grad - inner)).astype(jnp.bfloat16)
-            dq = jnp.where(mine, dot_plain(score_grad, key), dq)
-            dk = jnp.where(there, dot_columns(score_grad, query), dk)
-            dv = jnp.where(there, dot_columns(probs.astype(jnp.bfloat16), grad), dv)
-        dq_ref[rows, :] = dq * SCORE_SCALE
-        if first + block == length:
-            dk_sum[...] = dk
-            dv_sum[...] = dv
-        else:
-            dk_sum[seen, :] += dk
-            dv_sum[seen, :] += dv
-
-
 PAIR = 128
 BLOCK = 256
-
-
-def attend_back(projected, log_total, mixed_grad, head_dim):
-    length, columns = projected.shape
-    wide = columns // 3
-    pairs = wide // PAIR
-
-    def kind(which):
-        return pl.BlockSpec((length, PAIR), lambda p: (0, which * pairs + p))
-
-    return pl.pallas_call(
-        functools.partial(attend_back_kernel, head_dim, BLOCK),
-        grid=(pairs,),
-        in_specs=[kind(0), kind(1), kind(2), kind(0), kind(0)],
-        out_specs=[pl.BlockSpec((length, PAIR), lambda p: (0, p))] * 3,
-        out_shape=[jax.ShapeDtypeStruct((length, wide), jnp.float32)] * 3,
-        compiler_params=pltpu.CompilerParams(vmem_limit_bytes=32 << 20),
-        cost_estimate=pl.CostEstimate(
-            flops=40 * length * length * wide // 5,
-            bytes_accessed=18 * length * wide,
-            transcendentals=length * length * wide // head_dim,
-        ),
-        name="attend_back",
-    )(projected, projected, projected, log_total, mixed_grad)
 
 
 def block_order(place):
@@ -278,6 +201,86 @@
         term = dot_columns(chosen, values.reshape((256,) + values.shape[2:]))
         total = term if total is None else total + term
     return total
+
+
+def send(source, there, send_sem, recv_sem, **to):
+    return pltpu.make_async_remote_copy(
+        src_ref=source,
+        dst_ref=there,
+        send_sem=send_sem,
+        recv_sem=recv_sem,
+        device_id=to,
+        device_id_type=MESH,
+    )
+
+
+class Return:
+    def __init__(self, plane, returned, target_ref, stage, far, far_send, far_recv, per):
+        self.plane, self.returned, self.target_ref = plane, returned, target_ref
+        self.stage, self.far, self.per = stage, far, per
+        self.far_send, self.far_recv = far_send, far_recv
+        self.place = lax.axis_index("tensor")
+        self.order = block_order(self.place)
+        self.mine = lax.rem(self.place, 2)
+        self.half = stage.shape[1] // 2
+        self.kept = pl.ds(self.mine * self.half, self.half)
+        self.passed = pl.ds((1 - self.mine) * self.half, self.half)
+
+    def mate_copy(self):
+        return send(
+            self.stage.at[1],
+            self.far.at[0],
+            self.far_send.at[0],
+            self.far_recv.at[0],
+            tensor=self.order[1],
+        )
+
+    def half_copy(self, step, part):
+        return send(
+            self.stage.at[step, part],
+            self.far.at[step, part],
+            self.far_send.at[step - 1],
+            self.far_recv.at[step - 1],
+            tensor=self.order[1],
+        )
+
+    def owner_copy(self, step, part, at):
+        return send(
+            self.stage.at[step, part],
+            self.far.at[1, part],
+            self.far_send.at[step + 1],
+            self.far_recv.at[3 + at],
+            tensor=self.order[step],
+        )
+
+    def collect(self, step):
+        return collect_block(self.returned, self.target_ref, self.order[step], step, self.per)
+
+    def step(self, step):
+        self.plane.wait_recv(step)
+        self.stage[step] = self.collect(step).astype(jnp.bfloat16)
+        if step == 1:
+            self.mate_copy().start()
+            return
+        self.half_copy(step, self.passed).start()
+        self.half_copy(step, self.kept).wait_recv()
+        self.stage[step, self.kept] = (
+            self.stage[step, self.kept].astype(jnp.float32)
+            + self.far[step, self.kept].astype(jnp.float32)
+        ).astype(jnp.bfloat16)
+        self.owner_copy(step, self.kept, self.mine).start()
+
+    def wait(self):
+        self.mate_copy().wait()
+        self.owner_copy(2, pl.ds(0, self.half), 0).wait_recv()
+        self.owner_copy(2, pl.ds(self.half, self.half), 1).wait_recv()
+
+    def drain(self):
+        for step in range(4):
+            self.plane.wait_send(step)
+        for step in (2, 3):
+            self.half_copy(step, self.passed).wait_send()
+            self.owner_copy(step, self.kept, self.mine).wait_send()
 
 
 GELU_SCALE = 0.7978845608028654
@@ -409,42 +412,7 @@
                 d_out_ref[expert] += dot_columns(a, g)
                 d_in_ref[expert] += dot_columns(x, change)
 
-    mine = lax.rem(place, 2)
-    mate = order[1]
-    rows_half = rows_ref.shape[0] // 2
-    kept = pl.ds(mine * rows_half, rows_half)
-    passed = pl.ds((1 - mine) * rows_half, rows_half)
-
-    def mate_copy():
-        return pltpu.make_async_remote_copy(
-            src_ref=held.at[1],
-            dst_ref=far.at[0],
-            send_sem=far_send.at[0],
-            recv_sem=far_recv.at[0],
-            device_id={"tensor": mate},
-            device_id_type=MESH,
-        )
-
-    def half_copy(step):
-        return pltpu.make_async_remote_copy(
-            src_ref=held.at[step, passed],
-            dst_ref=far.at[step, passed],
-            send_sem=far_send.at[step - 1],
-            recv_sem=far_recv.at[step - 1],
-            device_id={"tensor": mate},
-            device_id_type=MESH,
-        )
-
-    def owner_copy(step, part, at):
-        return pltpu.make_async_remote_copy(
-            src_ref=held.at[step, part],
-            dst_ref=far.at[1, part],
-            send_sem=far_send.at[step + 1],
-            recv_sem=far_recv.at[3 + at],
-            device_id={"tensor": order[step]},
-            device_id_type=MESH,
-        )
-
+    home = Return(back_plane, returned, target_ref, held, far, far_send, far_recv, per)
     grad_copy(0).start()
     grad_copy(1).start()
     dispatch(0)
@@ -458,39 +426,15 @@
             grad_copy(step + 2).start()
     along.finish()
     back_plane.wait_recv(0)
-    back_ref[...] = collect_block(returned, target_ref, order[0], 0, per)
+    back_ref[...] = home.collect(0)
     for step in range(1, line):
-        back_plane.wait_recv(step)
-        held[step] = collect_block(returned, target_ref, order[step], step, per).astype(
-            jnp.bfloat16
-        )
-        if step == 1:
-            mate_copy().start()
-            continue
-        half_copy(step).start()
-        pltpu.make_async_remote_copy(
-            src_ref=held.at[step, kept],
-            dst_ref=far.at[step, kept],
-            send_sem=far_send.at[step - 1],
-            recv_sem=far_recv.at[step - 1],
-            device_id={"tensor": mate},
-            device_id_type=MESH,
-        ).wait_recv()
-        held[step, kept] = (
-            held[step, kept].astype(jnp.float32) + far[step, kept].astype(jnp.float32)
-        ).astype(jnp.bfloat16)
-        owner_copy(step, kept, mine).start()
-    mate_copy().wait()
-    owner_copy(2, pl.ds(0, rows_half), 0).wait_recv()
-    owner_copy(2, pl.ds(rows_half, rows_half), 1).wait_recv()
+        home.step(step)
+    home.wait()
     back_ref[...] += far[0].astype(jnp.float32) + far[1].astype(jnp.float32)
+    home.drain()
     for step in range(line):
-        back_plane.wait_send(step)
         for expert in range(experts):
             result_copy(step, expert).wait()
-    for step in (2, 3):
-        half_copy(step).wait_send()
-        owner_copy(step, kept, mine).wait_send()
 
 
 def run_experts(rows, targets, grads, w_in, w_out, dp_count, line):
@@ -574,17 +518,6 @@
             logs = jnp.where(mine, top + jnp.log(total), logs)
         mixed_ref[rows, here] = mixed.astype(jnp.bfloat16)
         log_ref[rows, here] = logs
-
-
-def send(source, there, send_sem, recv_sem, **to):
-    return pltpu.make_async_remote_copy(
-        src_ref=source,
-        dst_ref=there,
-        send_sem=send_sem,
-        recv_sem=recv_sem,
-        device_id=to,
-        device_id_type=MESH,
-    )
 
 
 class Share:
@@ -870,8 +803,422 @@
     )(tokens, cotangent, target, *weights, gains)
 
 
-def product(spec, left, right):
-    return jnp.einsum(spec, left, right, preferred_element_type=jnp.float32)
+def attend_back_pair(proj_ref, log_ref, grad_ref, out_ref, dk_sum, dv_sum, pair, head_dim):
+    length, wide = proj_ref.shape[0], proj_ref.shape[1] // 3
+    here = pl.ds(pair * PAIR, PAIR)
+    key_at, value_at = pl.ds(wide + pair * PAIR, PAIR), pl.ds(2 * wide + pair * PAIR, PAIR)
+    lane = lax.broadcasted_iota(jnp.int32, (BLOCK, PAIR), 1)
+    for first in reversed(range(0, length, BLOCK)):
+        rows, seen = pl.ds(first, BLOCK), pl.ds(0, first + BLOCK)
+        lanes_seen = lax.broadcasted_iota(jnp.int32, (first + BLOCK, PAIR), 1)
+        wide_query = proj_ref[rows, here].astype(jnp.float32) * SCORE_SCALE
+        key, value, grad = proj_ref[seen, key_at], proj_ref[seen, value_at], grad_ref[rows, here]
+        query, wide_grad = wide_query.astype(jnp.bfloat16), grad.astype(jnp.float32)
+        dq = jnp.zeros((BLOCK, PAIR), jnp.float32)
+        dk = jnp.zeros((first + BLOCK, PAIR), jnp.float32)
+        dv = jnp.zeros((first + BLOCK, PAIR), jnp.float32)
+        for head in range(PAIR // head_dim):
+            mine = lane // head_dim == head
+            there = lanes_seen // head_dim == head
+            scores = masked_scores(lanes_of(wide_query, mine), key, first)
+            log_total = log_ref[rows, pl.ds(pair * PAIR + head * head_dim, 1)]
+            probs = jnp.exp(scores - log_total)
+            prob_grad = dot_rows(lanes_of(wide_grad, mine), value)
+            inner = jnp.sum(probs * prob_grad, axis=-1, keepdims=True)
+            score_grad = (probs * (prob_grad - inner)).astype(jnp.bfloat16)
+            dq = jnp.where(mine, dot_plain(score_grad, key), dq)
+            dk = jnp.where(there, dot_columns(score_grad, query), dk)
+            dv = jnp.where(there, dot_columns(probs.astype(jnp.bfloat16), grad), dv)
+        out_ref[rows, here] = (dq * SCORE_SCALE).astype(jnp.bfloat16)
+        if first + BLOCK == length:
+            dk_sum[...] = dk
+            dv_sum[...] = dv
+        else:
+            dk_sum[seen, :] += dk
+            dv_sum[seen, :] += dv
+    out_ref[:, key_at] = dk_sum[...].astype(jnp.bfloat16)
+    out_ref[:, value_at] = dv_sum[...].astype(jnp.bfloat16)
+
+
+class Pieces:
+    def __init__(self, source, held, sems, dp_count):
+        self.source, self.held, self.sems, self.dp_count = source, held, sems, dp_count
+        self.me = lax.axis_index("dp")
+
+    def copy(self, i, to):
+        return send(
+            self.source.at[to],
+            self.held.at[self.me],
+            self.sems.at[0, i],
+            self.sems.at[1, i],
+            dp=to,
+        )
+
+    def start(self):
+        def one(i, carry):
+            self.copy(i, lax.rem(self.me + i, self.dp_count)).start()
+            return carry
+
+        lax.fori_loop(1, self.dp_count, one, 0)
+
+    def total(self, sum_ref):
+        sum_ref[...] = self.source[self.me].astype(jnp.float32)
+
+        def one(i, carry):
+            at = lax.rem(self.me + self.dp_count - i, self.dp_count)
+            send(
+                self.source.at[self.me],
+                self.held.at[at],
+                self.sems.at[0, i],
+                self.sems.at[1, i],
+                dp=at,
+            ).wait_recv()
+            sum_ref[...] += self.held[at].astype(jnp.float32)
+            return carry
+
+        lax.fori_loop(1, self.dp_count, one, 0)
+
+    def drain(self):
+        def one(i, carry):
+            self.copy(i, lax.rem(self.me + i, self.dp_count)).wait_send()
+            return carry
+
+        lax.fori_loop(1, self.dp_count, one, 0)
+
+
+def norm_back_rows(grad, values, gain):
+    unit, inv_scale = norm_stats(values)
+    scaled = grad * gain
+    mean_plain = jnp.mean(scaled, axis=-1, keepdims=True)
+    mean_unit = jnp.mean(scaled * unit, axis=-1, keepdims=True)
+    change = inv_scale * (scaled - mean_plain - unit * mean_unit)
+    return (
+        change,
+        jnp.sum(grad * unit, axis=0, keepdims=True),
+        jnp.sum(grad, axis=0, keepdims=True),
+    )
+
+
+def back_kernel(
+    dp_count,
+    head_dim,
+    back_ref,
+    cot_ref,
+    tokens_ref,
+    middle_ref,
+    gains_ref,
+    target_ref,
+    wq_ref,
+    wo_ref,
+    first_ref,
+    proj_ref,
+    log_ref,
+    mixed_ref,
+    result_ref,
+    out_ref,
+    grad_tokens_ref,
+    sums_ref,
+    d_qkv_ref,
+    d_out_ref,
+    returned,
+    stage,
+    far,
+    middle_grad,
+    middle_low,
+    mixed_grad,
+    mixed_sent,
+    qkv_grad,
+    dk_sum,
+    dv_sum,
+    out_pieces,
+    out_held,
+    out_sum,
+    out_sent,
+    out_near,
+    qkv_pieces,
+    qkv_held,
+    qkv_sum,
+    qkv_sent,
+    qkv_near,
+    first_sent,
+    first_near,
+    line_sums,
+    plane_sums,
+    send_sem,
+    recv_sem,
+    local_sem,
+    far_send,
+    far_recv,
+    near_send,
+    near_recv,
+    out_sems,
+    qkv_sems,
+    line_send,
+    line_recv,
+    plane_send,
+    plane_recv,
+):
+    rows, width = tokens_ref.shape
+    experts, line, _, per, _ = result_ref.shape
+    wide = proj_ref.shape[1] // 3
+    share = wq_ref.shape[1]
+    me, place = lax.axis_index("dp"), lax.axis_index("tensor")
+    order = block_order(place)
+    mate, across, last = order[1], lax.rem(place + 2, line), line - 1 - place
+    part = lax.rem(place, 2)
+    greet(dp_count, line)
+    plane = Plane(
+        lambda step, to: result_ref.at[:, order[step], to],
+        lambda step, at: returned.at[step, pl.ds(at * experts, experts)],
+        send_sem,
+        recv_sem,
+        local_sem,
+        dp_count,
+    )
+    for step in range(line):
+        plane.start(step)
+    results = Return(plane, returned, target_ref, stage, far, far_send, far_recv, per)
+    sums_ref[...] = jnp.zeros_like(sums_ref)
+
+    def second_rows(i, carry):
+        here = pl.ds(i * 128, 128)
+        change, gain_sum, bias_sum = norm_back_rows(
+            back_ref[here, :], middle_ref[here, :], gains_ref[2:3, :]
+        )
+        change = cot_ref[here, :].astype(jnp.float32) + change
+        middle_grad[here, :] = change
+        middle_low[here, :] = change.astype(jnp.bfloat16)
+        sums_ref[2:3, :] += gain_sum
+        sums_ref[3:4, :] += bias_sum
+        return carry
+
+    lax.fori_loop(0, rows // 128, second_rows, 0)
+    mixed_sent[...] = dot_plain(
+        middle_low[...], wo_ref[:, :, wide:].reshape(width, wide)
+    ).astype(jnp.bfloat16)
+    mixed_copy = send(
+        mixed_sent,
+        mixed_grad.at[pl.ds(part * rows, rows)],
+        near_send.at[0],
+        near_recv.at[0],
+        tensor=mate,
+    )
+    mixed_copy.start()
+    mixed_grad[pl.ds(part * rows, rows), :] = dot_plain(
+        middle_low[...], wo_ref[:, :, :wide].reshape(width, wide)
+    ).astype(jnp.bfloat16)
+    for group in range(2):
+        product_ = dot_columns(middle_low[...], mixed_ref[group]).astype(jnp.bfloat16)
+        out_pieces[:, :, group * wide : (group + 1) * wide] = product_.reshape(
+            dp_count, share, wide
+        )
+    outs = Pieces(out_pieces, out_held, out_sems, dp_count)
+    outs.start()
+    send(
+        mixed_sent,
+        mixed_grad.at[pl.ds((1 - part) * rows, rows)],
+        near_send.at[0],
+        near_recv.at[0],
+        tensor=mate,
+    ).wait_recv()
+    for pair in range(wide // PAIR):
+        attend_back_pair(
+            proj_ref, log_ref, mixed_grad, qkv_grad, dk_sum, dv_sum, pair, head_dim
+        )
+    first_sent[...] = dot_rows(
+        qkv_grad[pl.ds((1 - part) * rows, rows), :], wq_ref[...].reshape(width, 3 * wide)
+    ).astype(jnp.bfloat16)
+    first_copy = send(first_sent, first_near, near_send.at[1], near_recv.at[1], tensor=mate)
+    first_copy.start()
+    middle_rows = width // 2
+    for half in range(2):
+        total = dot_columns(
+            first_ref[0, :, half * middle_rows : (half + 1) * middle_rows], qkv_grad[:rows, :]
+        )
+        total += dot_columns(
+            first_ref[1, :, half * middle_rows : (half + 1) * middle_rows], qkv_grad[rows:, :]
+        )
+        qkv_pieces[pl.ds(half * dp_count // 2, dp_count // 2)] = total.astype(
+            jnp.bfloat16
+        ).reshape(dp_count // 2, share, 3 * wide)
+    qkvs = Pieces(qkv_pieces, qkv_held, qkv_sems, dp_count)
+    qkvs.start()
+
+    outs.total(out_sum)
+    for i, base in enumerate((wide, PAIR, wide + PAIR)):
+        out_sent[i] = out_sum[:, base : base + 2 * PAIR].astype(jnp.bfloat16)
+    out_copies = [
+        send(out_sent.at[i], out_near.at[i], near_send.at[3 + i], near_recv.at[3 + i], tensor=to)
+        for i, to in enumerate((mate, across, last))
+    ]
+    for copy in out_copies:
+        copy.start()
+
+    def first_rows(i, carry):
+        here = pl.ds(i * 128, 128)
+        grad = dot_rows(
+            qkv_grad[pl.ds(part * rows + i * 128, 128), :], wq_ref[...].reshape(width, 3 * wide)
+        )
+        grad += first_near[here, :].astype(jnp.float32)
+        change, gain_sum, bias_sum = norm_back_rows(
+            grad, tokens_ref[here, :].astype(jnp.float32), gains_ref[0:1, :]
+        )
+        grad_tokens_ref[here, :] = (middle_grad[here, :] + change).astype(jnp.bfloat16)
+        sums_ref[0:1, :] += gain_sum
+        sums_ref[1:2, :] += bias_sum
+        return carry
+
+    first_copy.wait_recv()
+    lax.fori_loop(0, rows // 128, first_rows, 0)
+    line_sums[place] = sums_ref[...]
+
+    def line_copy(i, at, to):
+        return send(line_sums.at[at], line_sums.at[at], line_send.at[i], line_recv.at[i], tensor=to)
+
+    for i in range(1, line):
+        line_copy(i, place, lax.rem(place + i, line)).start()
+    plane.wait_recv(0)
+    middle_grad[...] = middle_ref[...] + results.collect(0)
+    results.step(1)
+    for i in range(1, line):
+        at = lax.rem(place + line - i, line)
+        line_copy(i, at, at).wait_recv()
+    plane_sums[me] = (line_sums[0] + line_sums[1]) + (line_sums[2] + line_sums[3])
+
+    def plane_copy(i, at, to):
+        return send(
+            plane_sums.at[at], plane_sums.at[at], plane_send.at[i], plane_recv.at[i], dp=to
+        )
+
+    def plane_start(i, carry):
+        plane_copy(i, me, lax.rem(me + i, dp_count)).start()
+        return carry
+
+    lax.fori_loop(1, dp_count, plane_start, 0)
+    results.step(2)
+    qkvs.total(qkv_sum)
+    for kind in range(3):
+        base = kind * wide + PAIR
+        qkv_sent[kind] = qkv_sum[:, base : base + 2 * PAIR].astype(jnp.bfloat16)
+    qkv_copy = send(qkv_sent, qkv_near, near_send.at[2], near_recv.at[2], tensor=across)
+    qkv_copy.start()
+    results.step(3)
+
+    def plane_wait(i, carry):
+        at = lax.rem(me + dp_count - i, dp_count)
+        plane_copy(i, at, at).wait_recv()
+        return carry
+
+    lax.fori_loop(1, dp_count, plane_wait, 0)
+    sums_ref[...] = plane_sums[0]
+
+    def plane_add(i, carry):
+        sums_ref[...] += plane_sums[i]
+        return carry
+
+    lax.fori_loop(1, dp_count, plane_add, 0)
+    for copy in out_copies:
+        copy.wait_recv()
+    arrived = [out_near[i].astype(jnp.float32) for i in range(3)]
+    d_out_ref[:, :PAIR] = (
+        out_sum[:, :PAIR] + arrived[0][:, :PAIR] + arrived[1][:, PAIR:] + arrived[2][:, PAIR:]
+    )
+    turned = pltpu.roll(arrived[1][:, :PAIR] + arrived[2][:, :PAIR], head_dim, 1)
+    d_out_ref[:, PAIR:] = out_sum[:, PAIR : 2 * PAIR] + arrived[0][:, PAIR:] + turned
+    qkv_copy.wait_recv()
+    for kind in range(3):
+        base, at = kind * wide, kind * 2 * PAIR
+        come = qkv_near[kind].astype(jnp.float32)
+        d_qkv_ref[:, at : at + PAIR] = qkv_sum[:, base : base + PAIR] + come[:, PAIR:]
+        d_qkv_ref[:, at + PAIR : at + 2 * PAIR] = qkv_sum[
+            :, base + PAIR : base + 2 * PAIR
+        ] + pltpu.roll(come[:, :PAIR], head_dim, 1)
+    results.wait()
+    out_ref[...] = (
+        middle_grad[...] + far[0].astype(jnp.float32) + far[1].astype(jnp.float32)
+    ).astype(jnp.bfloat16)
+    results.drain()
+    outs.drain()
+    qkvs.drain()
+    mixed_copy.wait_send()
+    first_copy.wait_send()
+    qkv_copy.wait_send()
+    for copy in out_copies:
+        copy.wait_send()
+    for i in range(1, line):
+        line_copy(i, place, lax.rem(place + i, line)).wait_send()
+
+    def plane_drain(i, carry):
+        plane_copy(i, me, lax.rem(me + i, dp_count)).wait_send()
+        return carry
+
+    lax.fori_loop(1, dp_count, plane_drain, 0)
+
+
+def run_back(dp_count, head_dim, *args):
+    tokens, wq, proj, result = args[2], args[6], args[9], args[12]
+    rows, width = tokens.shape
+    experts, line, _, per, _ = result.shape
+    share = wq.shape[1]
+    wide = proj.shape[1] // 3
+    low, wider, dma = jnp.bfloat16, jnp.float32, pltpu.SemaphoreType.DMA
+    whole, far = pl.BlockSpec(memory_space=pltpu.VMEM), pl.BlockSpec(memory_space=pl.ANY)
+    shape, vmem = jax.ShapeDtypeStruct, pltpu.VMEM
+    return pl.pallas_call(
+        functools.partial(back_kernel, dp_count, head_dim),
+        in_specs=[whole] * 12 + [far],
+        out_specs=[whole] * 5,
+        out_shape=[
+            shape((rows, width), low),
+            shape((rows, width), low),
+            shape((8, width), wider),
+            shape((share, 6 * PAIR), wider),
+            shape((share, 2 * PAIR), wider),
+        ],
+        scratch_shapes=[
+            vmem((line, dp_count * experts, per, width), low),
+            vmem((line, rows, width), low),
+            vmem((line, rows, width), low),
+            vmem((rows, width), wider),
+            vmem((rows, width), low),
+            vmem((2 * rows, wide), low),
+            vmem((rows, wide), low),
+            vmem((2 * rows, 3 * wide), low),
+            vmem((2 * rows, PAIR), wider),
+            vmem((2 * rows, PAIR), wider),
+            vmem((dp_count, share, 2 * wide), low),
+            vmem((dp_count, share, 2 * wide), low),
+            vmem((share, 2 * wide), wider),
+            vmem((3, share, 2 * PAIR), low),
+            vmem((3, share, 2 * PAIR), low),
+            vmem((dp_count, share, 3 * wide), low),
+            vmem((dp_count, share, 3 * wide), low),
+            vmem((share, 3 * wide), wider),
+            vmem((3, share, 2 * PAIR), low),
+            vmem((3, share, 2 * PAIR), low),
+            vmem((rows, width), low),
+            vmem((rows, width), low),
+            vmem((line, 8, width), wider),
+            vmem((dp_count, 8, width), wider),
+            dma((line, dp_count)),
+            dma((line, dp_count)),
+            dma((line,)),
+            dma((line + 1,)),
+            dma((line + 1,)),
+            dma((6,)),
+            dma((6,)),
+            dma((2, dp_count)),
+            dma((2, dp_count)),
+            dma((line,)),
+            dma((line,)),
+            dma((dp_count,)),
+            dma((dp_count,)),
+        ],
+        compiler_params=pltpu.CompilerParams(
+            collective_id=2, has_side_effects=True, vmem_limit_bytes=58 << 20
+        ),
+        name="back",
+    )(*args)
 
 
 def on_device(
@@ -893,27 +1240,8 @@
     local_experts = expert_in.shape[0]
     dp_count = lax.axis_size("dp")
     line = lax.axis_size("tensor")
-    shares = LEN // row_count
-    place = lax.axis_index("tensor")
-    part = place % shares
-    swap = [(t, t ^ 1) for t in range(line)]
-    hop = [(t, t ^ 2) for t in range(line)]
     head_dim = w_qkv.shape[2] // 3
     heads_shard = w_qkv.shape[1]
-
-    def swapped(values):
-        return lax.ppermute(values, "tensor", swap)
-
-    def joined(own, other):
-        both = jnp.stack([own, other])
-        return jnp.where(part == 0, both, both[::-1]).reshape((-1,) + own.shape[1:])
-
-    def halves(both):
-        pair = both.reshape((shares, -1) + both.shape[1:])
-        return (
-            lax.dynamic_index_in_dim(pair, part, 0, False),
-            lax.dynamic_index_in_dim(pair, 1 - part, 0, False),
-        )
 
     experts_total = dp_count * local_experts
     capacity = 2 * row_count // experts_total
@@ -941,7 +1269,7 @@
     out_a = jnp.pad(out_rows, ((0, 0), (0, head_dim)))
     out_b = jnp.concatenate([out_rows[:, -head_dim:], out_rows[:, :-head_dim]], axis=1)
     out_b = jnp.pad(out_b, ((0, 0), (head_dim, 0)))
-    gains = jnp.stack([ln1_gain, ln1_bias, ln2_gain, ln2_bias])
+    gains = jnp.pad(jnp.stack([ln1_gain, ln1_bias, ln2_gain, ln2_bias]), ((0, 4), (0, 0)))
     sizes = (dp_count, line, local_experts, capacity, head_dim)
     (
         grad_rows,
@@ -959,17 +1287,9 @@
         cotangent,
         own_target,
         (qkv_a.reshape(share, -1), qkv_b, out_a, out_b),
-        jnp.pad(gains, ((0, 4), (0, 0))),
+        gains,
         sizes,
     )
-    qkv_flat = qkv_weight.reshape(model_width, -1)
-    out_weight = out_weight.reshape(model_width, -1)
-    first_all = first_all.reshape(LEN, model_width)
-    residual = tokens.astype(jnp.float32)
-    _, unit_one, scale_one = normalize(residual, ln1_gain, ln1_bias)
-    _, unit_two, scale_two = normalize(middle, ln2_gain, ln2_bias)
-
-    out_grad = cotangent.astype(jnp.float32)
     second_grad, result, grad_expert_in, grad_expert_out = run_experts(
         second_low,
         targets,
@@ -979,68 +1299,35 @@
         dp_count,
         line,
     )
-    gain_two_grad = jnp.sum(second_grad * unit_two, axis=0)
-    bias_two_grad = jnp.sum(second_grad, axis=0)
-    middle_grad = out_grad + norm_back(second_grad, unit_two, scale_two, ln2_gain)
-    middle_low = middle_grad.astype(low)
-    mixed_both = product("td,dk->tk", middle_low, out_weight).astype(low)
-    mixed_grad = joined(mixed_both[:, :wide], swapped(mixed_both[:, wide:]))
-    result, mixed_grad = lax.optimization_barrier((result, mixed_grad))
-    result = lax.all_to_all(result.transpose(2, 0, 1, 3, 4), "dp", split_axis=0, concat_axis=0)
-    result = result.transpose(2, 0, 1, 3, 4).reshape(line, slot_count, model_width)
-    chosen = (
-        jnp.arange(slot_count, dtype=jnp.int32)[None, :, None] == targets[:, :1, :]
-    ).astype(low)
-    rows = product("bsr,bsd->brd", chosen, result).astype(low)
-    rows = rows.reshape(line * row_count, model_width)
-    rows = lax.psum_scatter(rows, "tensor", scatter_dimension=0, tiled=True)
-    mixed_out = middle + rows.astype(jnp.float32)
-    out_wgrad = product("td,ptk->dpk", middle_low, mixed_pair).reshape(model_width, -1).astype(low)
-    out_part = lax.psum_scatter(out_wgrad, "dp", scatter_dimension=0, tiled=True)
+    out, grad_tokens, sums, grad_qkv, grad_out = run_back(
+        dp_count,
+        head_dim,
+        second_grad,
+        cotangent,
+        tokens,
+        middle,
+        gains,
+        targets,
+        qkv_weight,
+        out_weight,
+        first_all,
+        projected,
+        log_total,
+        mixed_pair,
+        result,
+    )
     half = wide // 2
-
-    def swap_last(values):
-        return jnp.concatenate([values[:, head_dim:], values[:, :head_dim]], axis=1)
-
-    pieces = (
-        out_part[:, :half],
-        out_part[:, wide : wide + half],
-        swap_last(out_part[:, half:wide]),
-        swap_last(out_part[:, wide + half :]),
-    )
-    out_total = pieces[0].astype(jnp.float32)
-    for i in range(1, line):
-        sent = lax.ppermute(pieces[i], "tensor", [(t, t ^ i) for t in range(line)])
-        out_total = out_total + sent.astype(jnp.float32)
-    out_total = out_total.T
-
-    qkv_grad = jnp.concatenate(attend_back(projected, log_total, mixed_grad, head_dim), axis=1).astype(low)
-    qkv_wgrad = product("td,tk->dk", first_all, qkv_grad).astype(low)
-    qkv_part = lax.psum_scatter(qkv_wgrad, "dp", scatter_dimension=0, tiled=True)
-    qkv_part = qkv_part.reshape(share, 3, wide)
-    qkv_far = qkv_part[:, :, half:]
-    qkv_far = jnp.concatenate([qkv_far[:, :, head_dim:], qkv_far[:, :, :head_dim]], axis=2)
-    qkv_far = lax.ppermute(qkv_far, "tensor", hop)
-    qkv_total = qkv_part[:, :, :half].astype(jnp.float32) + qkv_far.astype(jnp.float32)
-    qkv_total = qkv_total.reshape(share, 3, heads_shard, head_dim).transpose(0, 2, 1, 3)
-    qkv_total = qkv_total.reshape(w_qkv.shape)
-    first_own, first_sent = halves(product("tk,dk->td", qkv_grad, qkv_flat))
-    first_grad = first_own + swapped(first_sent.astype(low)).astype(jnp.float32)
-    gain_one_grad = jnp.sum(first_grad * unit_one, axis=0)
-    bias_one_grad = jnp.sum(first_grad, axis=0)
-    input_grad = middle_grad + norm_back(first_grad, unit_one, scale_one, ln1_gain)
-    norm_sums = lax.psum(
-        (gain_one_grad, bias_one_grad, gain_two_grad, bias_two_grad), ("dp", "tensor")
-    )
+    grad_qkv = grad_qkv.reshape(share, 3, -1)[:, :, :half]
+    grad_qkv = grad_qkv.reshape(share, 3, heads_shard, head_dim).transpose(0, 2, 1, 3)
     return (
-        mixed_out.astype(low),
-        input_grad.astype(low),
-        norm_sums[0],
-        norm_sums[1],
-        qkv_total,
-        out_total,
-        norm_sums[2],
-        norm_sums[3],
+        out,
+        grad_tokens,
+        sums[0],
+        sums[1],
+        grad_qkv.reshape(w_qkv.shape),
+        grad_out[:, :half].T,
+        sums[2],
+        sums[3],
         grad_expert_in,
         grad_expert_out,
     )

time: 562 us -> 511 us (0.909)
  Pallas kernels: 322 us -> 472 us
  waiting for transfers between devices: 79.8 us -> 0 us
  blocking collectives: 46.2 us -> 0 us
  local copies, waits for them, and re-layouts: 40.1 us -> 21.4 us
  matrix products: 15.5 us -> 0.27 us
  other arithmetic: 22.7 us -> 8.67 us
  between operations: 14.8 us -> 1.15 us
  starting transfers between devices: 13.1 us -> 0 us
    pallas_call x1, Pallas kernels: 17.7 us -> 168 us  [run_back(): pl.pallas_call(functools.partial(back_kernel, dp_count, head_dim), in_spe...]
    all_to_all x1 -> x0, waiting for transfers between devices: 47.3 us -> none  [on_device(): lax.all_to_all(result.transpose(2, 0, 1, 3, 4), 'dp', split_axis=0, conca...]
    psum x1 -> x0, blocking collectives: 46.2 us -> none  [on_device(): lax.psum((gain_one_grad, bias_one_grad, gain_two_grad, bias_two_grad), ('...]
    ppermute x6 -> x0, waiting for transfers between devices: 32.3 us -> none  [the longest x2 24 us: swapped(): return lax.ppermute(values, 'tensor', swap)]
    dot_general x5 -> x0, matrix products: 15.2 us -> none  [product(): return jnp.einsum(spec, left, right, preferred_element_type=jnp.float32)]
    reduce_sum x6 -> x0, other arithmetic: 8.47 us -> none  [the longest x1 3.64 us: on_device(): gain_one_grad = jnp.sum(first_grad * unit_one, axis=0)]
    unnamed x63 -> x34, local copies, waits for them, and re-layouts: 19.5 us -> 11.4 us
    ppermute x6 -> x0, starting transfers between devices: 6.58 us -> none  [the longest x3 3.69 us: on_device(): sent = lax.ppermute(pieces[i], 'tensor', [(t, t ^ i) for t in range(line)])]
  transfers between devices with their start and end apart: 10 -> 0, of which waited for: 6 -> 0; matrix products, arithmetic and copies ran while one was open for 6% -> 0% of each run, Pallas kernels for 3% -> 0%
where the time goes in v4:
time: 511 us; the launch traced here: 504 us
  Pallas kernels  472 us (92%)
  local copies, waits for them, and re-layouts  21.4 us (4%)
  other arithmetic  8.67 us (2%)
    pallas_call x1, Pallas kernels, run_experts(): pl.pallas_call(functools.partial(expert_kernel, dp_count), in_specs=[whol...  186 us
    pallas_call x1, Pallas kernels, run_back(): pl.pallas_call(functools.partial(back_kernel, dp_count, head_dim), in_spe...  168 us
    pallas_call x1, Pallas kernels, run_front(): pl.pallas_call(functools.partial(front_kernel, dp_count, head_dim), in_sp...  118 us
    unnamed x34, local copies, waits for them, and re-layouts  11.4 us

profile of v4, /device:TPU:0, one launch (start us, length us, event | category | flops | bytes accessed | tf_op | source)
XLA Modules:
  0.0 503.5 jit_solution(3047422256667137163)
XLA Ops:
  0.6 0.0 copy-start
  0.7 0.0 copy-start.10
  0.7 0.0 copy-start.9
  0.7 0.0 copy-start.6
  0.7 0.0 copy-start.5
  0.7 0.0 copy-start.8
  0.7 0.0 copy-start.7
  0.7 0.8 compare_select_fusion
  1.6 0.0 copy-done
  1.6 3.1 gather_fusion
  4.7 0.7 and_select_fusion
  5.4 0.3 fusion.1
  5.7 0.0 copy-done.7
  5.7 0.0 copy-done.8
  5.8 0.0 copy-done.9
  5.8 0.0 copy-done.10
  5.8 0.6 select_maximum_fusion.gains_ref
  6.4 0.6 broadcast_in_dim.23.own_target_ref
  7.0 0.0 copy-done.6
  7.0 0.1 copy.32
  7.2 0.6 pad.22.out_a_ref
  7.8 0.7 fusion.4.out_b_ref
  8.5 0.0 copy-done.5
  8.5 0.2 copy.27
  8.8 0.1 copy.31
  8.9 0.8 pad_bitcast_fusion.qkv_b_ref
  9.7 0.1 pad.20
  9.7 0.9 copy.37.qkv_a_ref
  10.6 4.1 convert_element_type.37.w_in_ref
  14.7 0.0 copy-done.2
  14.7 1.6 convert_element_type.38.w_out_ref
  16.4 117.8 %front.1 = (bf16[2,4,8,64,768]{4,3,2,1,0:T(8,128)(2,1)}, s32[4,8,512]{2,1,0:T(8,128)}, bf16[8,96,1152]{2,1,0:T(8,128)(2,1)}, bf16[8,96,768]{2,1,0:T(8,128)(2,1)}...) custom-call(bf16[512,768]{1,0:T(8,128)(2,1)} %tokens_ref.3, ...), custom_call_target="tpu_custom_call" | custom-call | tf_op jit(solution)/shard_map/front/pallas_call | solution.py:763
  134.1 186.0 %experts.1 = (f32[512,768]{1,0:T(8,128)}, bf16[2,4,8,64,768]{4,3,2,1,0:T(8,128)(2,1)}, f32[2,768,768]{2,1,0:T(8,128)}, f32[2,768,768]{2,1,0:T(8,128)}) custom-call(bf16[512,768]{1,0:T(8,128)(2,1)} %get-tuple-element.29.rows_ref, s32[4,8,512]{2,1,0:T(8,128)} %get-tuple-element.30.target_ref, bf16[2,4,8,64,768]{4,3,2,1,0:T(8,128)(2,1)} %get-tuple-element.31.grads_ref, ...), custom_call_target="tpu_custom_call" | custom-call | flops 28991029248 | bytes 25165824 | tf_op jit(solution)/shard_map/experts/pallas_call | solution.py:446
  320.1 168.3 %back.1 = (bf16[512,768]{1,0:T(8,128)(2,1)}, bf16[512,768]{1,0:T(8,128)(2,1)}, f32[8,768]{1,0:T(8,128)}, f32[96,768]{1,0:T(8,128)}, f32[96,256]{1,0:T(8,128)}) custom-call(f32[512,768]{1,0:T(8,128)} %get-tuple-element.32.back_ref, bf16[512,768]{1,0:T(8,128)(2,1)} %cot_ref.3, bf16[512,768]{1,0:T(8,128)(2,1)} %tokens_ref.3, ...), custom_call_target="tpu_custom_call" | custom-call | tf_op jit(solution)/shard_map/back/pallas_call | solution.py:1167
  488.4 0.0 copy-start.4
  488.4 0.0 copy-start.3
  488.4 1.6 slice_reduce_fusion
  490.0 0.9 slice_bitcast_fusion
  490.9 0.7 copy.36
  491.6 1.1 reshape.62
  492.7 0.2 copy.33
  492.9 0.9 copy.35
  493.8 0.0 copy-done.4
  493.8 0.9 copy.42
  494.7 0.0 copy-done.3
  494.7 0.9 copy.43
  495.6 5.5 %copy.44 = f32[2,768,768]{2,1,0:T(8,128)} copy(f32[2,768,768]{2,1,0:T(8,128)} %get-tuple-element.90) | data formatting | bytes 9437184
  501.1 2.2 copy.45
  (22 shorter events, 0.1 us)
Async XLA Ops:
  0.6 1.0 copy-start
  0.7 5.1 %copy-start.10 = (f32[768]{0:T(1024)S(1)}, f32[768]{0:T(1024)}, u32[]{:S(2)}) copy-start(f32[768]{0:T(1024)} %param.20) | copy-start | bytes 9220
  0.7 5.1 %copy-start.9 = (f32[768]{0:T(1024)S(1)}, f32[768]{0:T(1024)}, u32[]{:S(2)}) copy-start(f32[768]{0:T(1024)} %param.19) | copy-start | bytes 9220
  0.7 6.4 %copy-start.6 = (f32[192,96]{1,0:T(8,128)S(1)}, f32[192,96]{1,0:T(8,128)}, u32[]{:S(2)}) copy-start(f32[192,96]{1,0:T(8,128)} %param.18) | copy-start | bytes 221188
  0.7 7.8 %copy-start.5 = (f32[96,3,192]{2,0,1:T(8,128)S(1)}, f32[96,3,192]{2,0,1:T(8,128)}, u32[]{:S(2)}) copy-start(f32[96,3,192]{2,0,1:T(8,128)} %param.17) | copy-start | bytes 663556
  0.7 5.0 %copy-start.8 = (f32[768]{0:T(1024)S(1)}, f32[768]{0:T(1024)}, u32[]{:S(2)}) copy-start(f32[768]{0:T(1024)} %param.16) | copy-start | bytes 9220
  0.7 5.0 copy-start.7
  10.6 4.1 copy-start.2
  488.4 5.4 %copy-start.4 = (bf16[512,768]{1,0:T(8,128)(2,1)S(1)}, bf16[512,768]{1,0:T(8,128)(2,1)}, u32[]{:S(2)}) copy-start(bf16[512,768]{1,0:T(8,128)(2,1)} %get-tuple-element.82) | copy-start | bytes 2359300
  488.4 6.3 %copy-start.3 = (bf16[512,768]{1,0:T(8,128)(2,1)S(1)}, bf16[512,768]{1,0:T(8,128)(2,1)}, u32[]{:S(2)}) copy-start(bf16[512,768]{1,0:T(8,128)(2,1)} %get-tuple-element.83) | copy-start | bytes 2359300
  494.7 6.4 %slice-start = ((s8[4718592]{0:T(1024)(128)(4,1)}), s8[4194304]{0:T(1024)(128)(4,1)S(1)}, s32[]{:S(2)}) async-start(s8[4718592]{0:T(1024)(128)(4,1)} %bitcast.18), calls=%async_computation | async-start | bytes 8388608
  495.6 5.5 %slice-start.1 = ((s8[4718592]{0:T(1024)(128)(4,1)}), s8[524288]{0:T(1024)(128)(4,1)S(1)}, s32[]{:S(2)}) async-start(s8[4718592]{0:T(1024)(128)(4,1)} %bitcast.18), calls=%async_computation.1 | async-start | bytes 1048576
  501.1 2.2 copy-start.1

commit v5 on v4

--- a/solution.py
+++ b/solution.py
@@ -256,13 +256,17 @@
     def collect(self, step):
         return collect_block(self.returned, self.target_ref, self.order[step], step, self.per)
 
-    def step(self, step):
+    def begin(self, step, then=None):
         self.plane.wait_recv(step)
+        if then is not None:
+            self.plane.start(then)
         self.stage[step] = self.collect(step).astype(jnp.bfloat16)
         if step == 1:
             self.mate_copy().start()
-            return
-        self.half_copy(step, self.passed).start()
+        else:
+            self.half_copy(step, self.passed).start()
+
+    def end(self, step):
         self.half_copy(step, self.kept).wait_recv()
         self.stage[step, self.kept] = (
             self.stage[step, self.kept].astype(jnp.float32)
@@ -292,8 +296,8 @@
     rows_ref,
     target_ref,
     grads_ref,
-    w_in_ref,
-    w_out_ref,
+    wide_in_ref,
+    wide_out_ref,
     back_ref,
     result_ref,
     d_in_ref,
@@ -307,6 +311,9 @@
     sent_back,
     returned,
     far,
+    w_in_ref,
+    w_out_ref,
+    loaded,
     line_send,
     line_recv,
     send_sem,
@@ -319,6 +326,7 @@
     far_send,
     far_recv,
     out_sem,
+    load_sem,
 ):
     line = held.shape[0]
     experts, _, _, per, width = arrived.shape
@@ -384,7 +392,8 @@
                 return carry
 
             lax.fori_loop(0, 2, one, 0)
-        back_plane.start(step)
+        if step > 1:
+            back_plane.start(step)
 
     def result_copy(step, expert):
         return pltpu.make_async_copy(
@@ -413,9 +422,29 @@
                 d_in_ref[expert] += dot_columns(x, change)
 
     home = Return(back_plane, returned, target_ref, held, far, far_send, far_recv, per)
+    chunk = loaded.shape[1]
+    loads = [
+        (wide, narrow, expert, i * chunk)
+        for wide, narrow in ((wide_in_ref, w_in_ref), (wide_out_ref, w_out_ref))
+        for expert in range(experts)
+        for i in range(narrow.shape[1] // chunk)
+    ]
+
+    def load(i):
+        wide, _, expert, first = loads[i]
+        return pltpu.make_async_copy(
+            wide.at[expert, pl.ds(first, chunk)], loaded.at[i % 2], load_sem.at[i % 2]
+        )
+
+    load(0).start()
     grad_copy(0).start()
     grad_copy(1).start()
     dispatch(0)
+    for i, (_, narrow, expert, first) in enumerate(loads):
+        if i + 1 < len(loads):
+            load(i + 1).start()
+        load(i).wait()
+        narrow[expert, pl.ds(first, chunk), :] = loaded[i % 2].astype(jnp.bfloat16)
     for step in range(line):
         if step + 1 < line:
             dispatch(step + 1)
@@ -425,10 +454,13 @@
         if step + 2 < line:
             grad_copy(step + 2).start()
     along.finish()
+    home.begin(2, 1)
+    home.end(2)
+    home.begin(3, 0)
+    home.end(3)
+    home.begin(1)
     back_plane.wait_recv(0)
     back_ref[...] = home.collect(0)
-    for step in range(1, line):
-        home.step(step)
     home.wait()
     back_ref[...] += far[0].astype(jnp.float32) + far[1].astype(jnp.float32)
     home.drain()
@@ -445,7 +477,7 @@
     groups = dp_count * experts
     return pl.pallas_call(
         functools.partial(expert_kernel, dp_count),
-        in_specs=[whole, whole, far, whole, whole],
+        in_specs=[whole, whole, far, far, far],
         out_specs=[whole, far, whole, whole],
         out_shape=[
             jax.ShapeDtypeStruct(rows.shape, jnp.float32),
@@ -463,6 +495,9 @@
             pltpu.VMEM(grads.shape, low),
             pltpu.VMEM((line, groups, per, width), low),
             pltpu.VMEM((line,) + rows.shape, low),
+            pltpu.VMEM(w_in.shape, low),
+            pltpu.VMEM(w_out.shape, low),
+            pltpu.VMEM((2, width // 2, width), jnp.float32),
             dma((line + 1,)),
             dma((line,)),
             dma((line, dp_count)),
@@ -475,6 +510,7 @@
             dma((line + 1,)),
             dma((line + 1,)),
             dma((line, experts)),
+            dma((2,)),
         ],
         compiler_params=pltpu.CompilerParams(
             collective_id=0, has_side_effects=True, vmem_limit_bytes=61 << 20
@@ -567,6 +603,7 @@
     dp_count,
     head_dim,
     tokens_ref,
+    mate_tokens_ref,
     cot_ref,
     own_target_ref,
     qkv_a_ref,
@@ -621,6 +658,8 @@
     ]
     for copy in near:
         copy.start()
+    along = Line(cot_ref, held, line_send, line_recv)
+    along.start()
     target_ref[place] = own_target_ref[...]
 
     def target_copy(i, at, to):
@@ -631,20 +670,6 @@
     for i in range(1, line):
         target_copy(i, place, lax.rem(place + i, line)).start()
 
-    def first_rows(i, carry):
-        values = tokens_ref[pl.ds(i * 128, 128), :].astype(jnp.float32)
-        unit, _ = norm_stats(values)
-        unit = unit * gains_ref[0:1, :] + gains_ref[1:2, :]
-        first_ref[part, pl.ds(i * 128, 128), :] = unit.astype(jnp.bfloat16)
-        return carry
-
-    lax.fori_loop(0, rows // 128, first_rows, 0)
-    first_copy = send(
-        first_ref.at[part], first_ref.at[part], near_send.at[4], near_recv.at[4], tensor=mate
-    )
-    first_copy.start()
-    along = Line(cot_ref, held, line_send, line_recv)
-    along.start()
     near[0].wait_recv()
     for kind in range(3):
         base = kind * wide
@@ -668,7 +693,18 @@
         wo_ref[me, :, base + 2 * PAIR : base + wide] = b[:, PAIR:].astype(jnp.bfloat16)
     share_o = Share(wo_ref, o_sems, dp_count)
     share_o.start()
+
+    def first_rows(i, carry):
+        here = pl.ds(i * 128, 128)
+        for which, source in ((part, tokens_ref), (1 - part, mate_tokens_ref)):
+            unit, _ = norm_stats(source[here, :].astype(jnp.float32))
+            unit = unit * gains_ref[0:1, :] + gains_ref[1:2, :]
+            first_ref[which, here, :] = unit.astype(jnp.bfloat16)
+        return carry
+
+    lax.fori_loop(0, rows // 128, first_rows, 0)
     share_q.relay()
+    share_o.relay()
 
     plane = Plane(
         lambda step, to: slots.at[step, pl.ds(to * experts, experts)],
@@ -680,30 +716,31 @@
     )
 
     def dispatch(step):
-        if step:
-            along.take(step)
         source = cot_ref if step == 0 else held.at[order[step]]
         dispatch_block(source, target_ref, order[step], slots, step, per)
         plane.start(step)
 
+    for i in range(1, line):
+        at = lax.rem(place + line - i, line)
+        target_copy(i, at, at).wait_recv()
+    along.take(1)
     dispatch(0)
-    share_o.relay()
+    dispatch(1)
     share_q.finish()
-    send(
-        first_ref.at[1 - part], first_ref.at[1 - part], near_send.at[4], near_recv.at[4], tensor=mate
-    ).wait_recv()
-
-    def project(i, carry):
-        values = first_ref[i // 2, pl.ds(lax.rem(i, 2) * (rows // 2), rows // 2), :]
-        weights = wq_ref[...].reshape(-1, 3 * wide)
-        proj_ref[pl.ds(i * (rows // 2), rows // 2), :] = dot_plain(values, weights).astype(
-            jnp.bfloat16
-        )
-        return carry
-
-    lax.fori_loop(0, 4, project, 0)
-    for i in range(1, line):
-        target_copy(i, lax.rem(place + line - i, line), lax.rem(place + line - i, line)).wait_recv()
+
+    def project(which):
+        def one(i, carry):
+            here = pl.ds(i * (rows // 2), rows // 2)
+            weights = wq_ref[...].reshape(-1, 3 * wide)
+            proj_ref[pl.ds(which * rows + i * (rows // 2), rows // 2), :] = dot_plain(
+                first_ref[which, here, :], weights
+            ).astype(jnp.bfloat16)
+            return carry
+
+        lax.fori_loop(0, 2, one, 0)
+
+    project(0)
+    project(1)
 
     def mix_copy(pair):
         here = pl.ds(pair * PAIR, PAIR)
@@ -716,9 +753,13 @@
         )
 
     for pair in range(wide // PAIR):
-        dispatch(pair + 1)
         attend_pair(proj_ref, mixed_all, log_ref, pair, head_dim)
         mix_copy(pair).start()
+        if pair == 0:
+            along.take(2)
+            dispatch(2)
+    along.take(3)
+    dispatch(3)
     mixed_ref[0] = mixed_all[pl.ds(part * rows, rows), :]
     share_o.finish()
     for pair in range(wide // PAIR):
@@ -741,7 +782,6 @@
     share_o.drain()
     for copy in near:
         copy.wait_send()
-    first_copy.wait_send()
     for i in range(1, line):
         target_copy(i, place, lax.rem(place + i, line)).wait_send()
     for pair in range(wide // PAIR):
@@ -751,7 +791,7 @@
         plane.wait_send(step)
 
 
-def run_front(tokens, cotangent, target, weights, gains, sizes):
+def run_front(tokens, mate_tokens, cotangent, target, weights, gains, sizes):
     dp_count, line, experts, per, head_dim = sizes
     rows, width = tokens.shape
     qkv_a, qkv_b, out_a, out_b = weights
@@ -762,7 +802,7 @@
     shape = jax.ShapeDtypeStruct
     return pl.pallas_call(
         functools.partial(front_kernel, dp_count, head_dim),
-        in_specs=[whole] * 8,
+        in_specs=[whole] * 9,
         out_specs=[far] + [whole] * 9,
         out_shape=[
             shape((experts, line, dp_count, per, width), low),
@@ -789,8 +829,8 @@
             dma((line,)),
             dma((line,)),
             dma((line,)),
-            dma((5,)),
-            dma((5,)),
+            dma((4,)),
+            dma((4,)),
             dma((wide // PAIR,)),
             dma((wide // PAIR,)),
             dma((4, dp_count // 2)),
@@ -800,7 +840,7 @@
             collective_id=1, has_side_effects=True, vmem_limit_bytes=56 << 20
         ),
         name="front",
-    )(tokens, cotangent, target, *weights, gains)
+    )(tokens, mate_tokens, cotangent, target, *weights, gains)
 
 
 def attend_back_pair(proj_ref, log_ref, grad_ref, out_ref, dk_sum, dv_sum, pair, head_dim):
@@ -975,8 +1015,7 @@
         local_sem,
         dp_count,
     )
-    for step in range(line):
-        plane.start(step)
+    plane.start(2)
     results = Return(plane, returned, target_ref, stage, far, far_send, far_recv, per)
     sums_ref[...] = jnp.zeros_like(sums_ref)
 
@@ -1014,6 +1053,7 @@
         )
     outs = Pieces(out_pieces, out_held, out_sems, dp_count)
     outs.start()
+    plane.start(3)
     send(
         mixed_sent,
         mixed_grad.at[pl.ds((1 - part) * rows, rows)],
@@ -1025,6 +1065,10 @@
         attend_back_pair(
             proj_ref, log_ref, mixed_grad, qkv_grad, dk_sum, dv_sum, pair, head_dim
         )
+        if pair == 0:
+            results.begin(2)
+        if pair == 1:
+            results.end(2)
     first_sent[...] = dot_rows(
         qkv_grad[pl.ds((1 - part) * rows, rows), :], wq_ref[...].reshape(width, 3 * wide)
     ).astype(jnp.bfloat16)
@@ -1043,7 +1087,7 @@
         ).reshape(dp_count // 2, share, 3 * wide)
     qkvs = Pieces(qkv_pieces, qkv_held, qkv_sems, dp_count)
     qkvs.start()
-
+    results.begin(3, 1)
     outs.total(out_sum)
     for i, base in enumerate((wide, PAIR, wide + PAIR)):
         out_sent[i] = out_sum[:, base : base + 2 * PAIR].astype(jnp.bfloat16)
@@ -1077,9 +1121,8 @@
 
     for i in range(1, line):
         line_copy(i, place, lax.rem(place + i, line)).start()
-    plane.wait_recv(0)
-    middle_grad[...] = middle_ref[...] + results.collect(0)
-    results.step(1)
+    results.end(3)
+    results.begin(1, 0)
     for i in range(1, line):
         at = lax.rem(place + line - i, line)
         line_copy(i, at, at).wait_recv()
@@ -1095,14 +1138,14 @@
         return carry
 
     lax.fori_loop(1, dp_count, plane_start, 0)
-    results.step(2)
     qkvs.total(qkv_sum)
     for kind in range(3):
         base = kind * wide + PAIR
         qkv_sent[kind] = qkv_sum[:, base : base + 2 * PAIR].astype(jnp.bfloat16)
     qkv_copy = send(qkv_sent, qkv_near, near_send.at[2], near_recv.at[2], tensor=across)
     qkv_copy.start()
-    results.step(3)
+    plane.wait_recv(0)
+    middle_grad[...] = middle_ref[...] + results.collect(0)
 
     def plane_wait(i, carry):
         at = lax.rem(me + dp_count - i, dp_count)
@@ -1243,6 +1286,8 @@
     head_dim = w_qkv.shape[2] // 3
     heads_shard = w_qkv.shape[1]
 
+    mate_tokens = lax.ppermute(tokens, "tensor", [(t, t ^ 1) for t in range(line)])
+
     experts_total = dp_count * local_experts
     capacity = 2 * row_count // experts_total
     slot_count = experts_total * capacity
@@ -1284,6 +1329,7 @@
         second_low,
     ) = run_front(
         tokens,
+        mate_tokens,
         cotangent,
         own_target,
         (qkv_a.reshape(share, -1), qkv_b, out_a, out_b),
@@ -1294,8 +1340,8 @@
         second_low,
         targets,
         grad_rows,
-        expert_in.astype(low),
-        expert_out.astype(low),
+        expert_in,
+        expert_out,
         dp_count,
         line,
     )

time: 511 us -> 446 us (0.87)
  Pallas kernels: 472 us -> 402 us
  other arithmetic: 8.67 us -> 2.07 us
  local copies, waits for them, and re-layouts: 21.4 us -> 27.4 us
    pallas_call x1, Pallas kernels: 168 us -> 118 us  [run_back(): pl.pallas_call(functools.partial(back_kernel, dp_count, head_dim), in_spe...]
    pallas_call x1, Pallas kernels: 186 us -> 170 us  [run_experts(): pl.pallas_call(functools.partial(expert_kernel, dp_count), in_specs=[whol...]
    convert_element_type x2 -> x0, other arithmetic: 5.76 us -> none  [the longest x1 4.12 us: on_device(): expert_in.astype(low)]
    unnamed x34 -> x20, local copies, waits for them, and re-layouts: 11.4 us -> 14.6 us
  transfers between devices with their start and end apart: 0 -> 1, of which waited for: 0 -> 1; matrix products, arithmetic and copies ran while one was open for 0% -> 3% of each run, Pallas kernels for 0% -> 0%
where the time goes in v5:
time: 446 us; the launch traced here: 441 us
  Pallas kernels  402 us (90%)
  local copies, waits for them, and re-layouts  27.4 us (6%)
  waiting for transfers between devices  4.83 us (1%)
    pallas_call x1, Pallas kernels, run_experts(): pl.pallas_call(functools.partial(expert_kernel, dp_count), in_specs=[whol...  170 us
    pallas_call x1, Pallas kernels, run_back(): pl.pallas_call(functools.partial(back_kernel, dp_count, head_dim), in_spe...  118 us
    pallas_call x1, Pallas kernels, run_front(): pl.pallas_call(functools.partial(front_kernel, dp_count, head_dim), in_sp...  113 us
    unnamed x20, local copies, waits for them, and re-layouts  14.6 us
  transfers between devices with their start and end apart: 1, of which 1 were waited for; matrix products, arithmetic and copies ran while one was open for 3% of the time, Pallas kernels for 0%

profile of v5, /device:TPU:0, one launch (start us, length us, event | category | flops | bytes accessed | tf_op | source)
XLA Modules:
  0.0 440.5 jit_solution(5243662105167928522)
XLA Ops:
  0.6 0.0 copy-start
  0.7 0.0 copy-start.3
  0.7 3.1 collective-permute-start
  3.8 1.0 copy.32
  4.8 1.1 copy.27
  5.9 0.7 compare_select_fusion
  6.6 0.7 stack.15
  7.3 0.7 stack.16
  8.0 0.7 stack.17
  8.7 0.7 stack.18
  9.4 0.6 pad.22.out_a_ref
  10.1 0.1 copy.31
  10.2 0.1 pad.20
  10.3 0.9 copy.37.qkv_a_ref
  11.1 0.0 copy-done
  11.1 3.1 gather_fusion
  14.3 0.7 fusion.4.out_b_ref
  15.0 0.6 select_maximum_fusion.gains_ref
  15.6 0.8 pad_bitcast_fusion.qkv_b_ref
  16.4 0.0 copy-done.3
  16.4 0.3 fusion.1
  16.7 4.8 %collective-permute-done.mate_tokens_ref = bf16[512,768]{1,0:T(8,128)(2,1)S(1)} collective-permute-done((bf16[512,768]{1,0:T(8,128)(2,1)}, bf16[512,768]{1,0:T(8,128)(2,1)S(1)}, u32[]{:S(2)}, u32[]{:S(2)}) %collective-permute-start) | collective-permute-done | bytes 786464 | tf_op jit(solution)/shard_map/ppermute | solution.py:1289
  21.5 0.0 copy-start.2
  21.5 0.6 broadcast_in_dim.23.own_target_ref
  22.1 0.3 copy-done.2
  22.4 113.4 %front.1 = (bf16[2,4,8,64,768]{4,3,2,1,0:T(8,128)(2,1)}, s32[4,8,512]{2,1,0:T(8,128)}, bf16[8,96,1152]{2,1,0:T(8,128)(2,1)}, bf16[8,96,768]{2,1,0:T(8,128)(2,1)}...) custom-call(bf16[512,768]{1,0:T(8,128)(2,1)} %tokens_ref.3, ...), custom_call_target="tpu_custom_call" | custom-call | tf_op jit(solution)/shard_map/front/pallas_call | solution.py:803
  135.8 169.9 %experts.1 = (f32[512,768]{1,0:T(8,128)}, bf16[2,4,8,64,768]{4,3,2,1,0:T(8,128)(2,1)}, f32[2,768,768]{2,1,0:T(8,128)}, f32[2,768,768]{2,1,0:T(8,128)}) custom-call(bf16[512,768]{1,0:T(8,128)(2,1)} %get-tuple-element.29.rows_ref, s32[4,8,512]{2,1,0:T(8,128)} %get-tuple-element.30.target_ref, bf16[2,4,8,64,768]{4,3,2,1,0:T(8,128)(2,1)} %get-tuple-element.31.grads_ref, ...), custom_call_target="tpu_custom_call" | custom-call | flops 28991029248 | bytes 25165824 | tf_op jit(solution)/shard_map/experts/pallas_call | solution.py:478
  305.7 118.3 %back.1 = (bf16[512,768]{1,0:T(8,128)(2,1)}, bf16[512,768]{1,0:T(8,128)(2,1)}, f32[8,768]{1,0:T(8,128)}, f32[96,768]{1,0:T(8,128)}, f32[96,256]{1,0:T(8,128)}) custom-call(f32[512,768]{1,0:T(8,128)} %get-tuple-element.32.back_ref, bf16[512,768]{1,0:T(8,128)(2,1)} %cot_ref.3, bf16[512,768]{1,0:T(8,128)(2,1)} %tokens_ref.3, ...), custom_call_target="tpu_custom_call" | custom-call | tf_op jit(solution)/shard_map/back/pallas_call | solution.py:1210
  424.1 0.0 copy-start.1
  424.1 1.5 slice_reduce_fusion
  425.6 0.9 slice_bitcast_fusion
  426.5 0.7 copy.36
  427.2 1.1 reshape.62
  428.4 0.2 copy.33
  428.6 0.9 copy.35
  429.4 2.1 copy.42
  431.5 0.0 copy-done.1
  431.5 0.0 slice-start
  431.5 0.9 copy.43
  432.4 0.0 slice-start.1
  432.4 5.5 %copy.44 = f32[2,768,768]{2,1,0:T(8,128)} copy(f32[2,768,768]{2,1,0:T(8,128)} %get-tuple-element.90) | data formatting | bytes 9437184
  437.9 0.0 slice-done
  437.9 0.0 slice-done.1
  437.9 2.2 copy.45
  (12 shorter events, 0.1 us)
Async XLA Ops:
  0.6 10.5 %copy-start = (s32[50257]{0:T(1024)S(1)}, s32[50257]{0:T(1024)}, u32[]{:S(2)}) copy-start(s32[50257]{0:T(1024)} %param.14) | copy-start | bytes 603088
  0.7 15.7 %copy-start.3 = (s32[512]{0:T(512)S(1)}, s32[512]{0:T(512)}, u32[]{:S(2)}) copy-start(s32[512]{0:T(512)} %param.13) | copy-start | bytes 6148
  0.7 20.8 %collective-permute-start = (bf16[512,768]{1,0:T(8,128)(2,1)}, bf16[512,768]{1,0:T(8,128)(2,1)S(1)}, u32[]{:S(2)}, u32[]{:S(2)}) collective-permute-start(bf16[512,768]{1,0:T(8,128)(2,1)} %tokens_ref.3), channel_id=1, source_target_pairs={{0,1},{1,0},{2,3},{3,2},{4,5},{5,4},{6,7},{7,6},{8,9},{9,8},{10,11... | collective-permute-start | bytes 2359304 | tf_op jit(solution)/shard_map/ppermute | solution.py:1289
  21.5 0.9 copy-start.2
  424.1 7.4 %copy-start.1 = (bf16[512,768]{1,0:T(8,128)(2,1)S(1)}, bf16[512,768]{1,0:T(8,128)(2,1)}, u32[]{:S(2)}) copy-start(bf16[512,768]{1,0:T(8,128)(2,1)} %get-tuple-element.83) | copy-start | bytes 2359300
  431.5 6.4 %slice-start = ((s8[4718592]{0:T(1024)(128)(4,1)}), s8[4194304]{0:T(1024)(128)(4,1)S(1)}, s32[]{:S(2)}) async-start(s8[4718592]{0:T(1024)(128)(4,1)} %bitcast.18), calls=%async_computation | async-start | bytes 8388608
  432.4 5.5 %slice-start.1 = ((s8[4718592]{0:T(1024)(128)(4,1)}), s8[524288]{0:T(1024)(128)(4,1)S(1)}, s32[]{:S(2)}) async-start(s8[4718592]{0:T(1024)(128)(4,1)} %bitcast.18), calls=%async_computation.1 | async-start | bytes 1048576

commit v6 on v5

--- a/solution.py
+++ b/solution.py
@@ -394,6 +394,8 @@
             lax.fori_loop(0, 2, one, 0)
         if step > 1:
             back_plane.start(step)
+        if step == 3:
+            back_plane.start(1)
 
     def result_copy(step, expert):
         return pltpu.make_async_copy(
@@ -445,18 +447,19 @@
             load(i + 1).start()
         load(i).wait()
         narrow[expert, pl.ds(first, chunk), :] = loaded[i % 2].astype(jnp.bfloat16)
+    dispatch(1)
     for step in range(line):
-        if step + 1 < line:
-            dispatch(step + 1)
         out_plane.wait_recv(step)
         forward(step)
+        if step + 2 < line:
+            dispatch(step + 2)
         later(step)
         if step + 2 < line:
             grad_copy(step + 2).start()
     along.finish()
-    home.begin(2, 1)
+    home.begin(2, 0)
     home.end(2)
-    home.begin(3, 0)
+    home.begin(3)
     home.end(3)
     home.begin(1)
     back_plane.wait_recv(0)
@@ -603,15 +606,18 @@
     dp_count,
     head_dim,
     tokens_ref,
-    mate_tokens_ref,
     cot_ref,
     own_target_ref,
     qkv_a_ref,
     qkv_b_ref,
     out_a_ref,
     out_b_ref,
+    gain_one_ref,
+    bias_one_ref,
+    gain_two_ref,
+    bias_two_ref,
+    grads_ref,
     gains_ref,
-    grads_ref,
     target_ref,
     wq_ref,
     wo_ref,
@@ -626,6 +632,7 @@
     hop,
     out_parts,
     mixed_all,
+    mate_tokens_ref,
     line_send,
     line_recv,
     send_sem,
@@ -660,7 +667,13 @@
         copy.start()
     along = Line(cot_ref, held, line_send, line_recv)
     along.start()
-    target_ref[place] = own_target_ref[...]
+    token_copy = send(
+        tokens_ref, mate_tokens_ref, near_send.at[4], near_recv.at[4], tensor=mate
+    )
+    token_copy.start()
+    target_ref[place] = jnp.broadcast_to(own_target_ref[...].reshape(1, rows), (8, rows))
+    for i, values in enumerate((gain_one_ref, bias_one_ref, gain_two_ref, bias_two_ref)):
+        gains_ref[i : i + 1, :] = values[...].reshape(1, -1)
 
     def target_copy(i, at, to):
         return send(
@@ -670,6 +683,21 @@
     for i in range(1, line):
         target_copy(i, place, lax.rem(place + i, line)).start()
 
+    plane = Plane(
+        lambda step, to: slots.at[step, pl.ds(to * experts, experts)],
+        lambda step, at: grads_ref.at[:, step, at],
+        send_sem,
+        recv_sem,
+        local_sem,
+        dp_count,
+    )
+
+    def dispatch(step):
+        source = cot_ref if step == 0 else held.at[order[step]]
+        dispatch_block(source, target_ref, order[step], slots, step, per)
+        plane.start(step)
+
+    dispatch(0)
     near[0].wait_recv()
     for kind in range(3):
         base = kind * wide
@@ -694,38 +722,24 @@
     share_o = Share(wo_ref, o_sems, dp_count)
     share_o.start()
 
-    def first_rows(i, carry):
-        here = pl.ds(i * 128, 128)
-        for which, source in ((part, tokens_ref), (1 - part, mate_tokens_ref)):
+    def first_rows(which, source):
+        def one(i, carry):
+            here = pl.ds(i * 128, 128)
             unit, _ = norm_stats(source[here, :].astype(jnp.float32))
             unit = unit * gains_ref[0:1, :] + gains_ref[1:2, :]
             first_ref[which, here, :] = unit.astype(jnp.bfloat16)
-        return carry
-
-    lax.fori_loop(0, rows // 128, first_rows, 0)
+            return carry
+
+        lax.fori_loop(0, rows // 128, one, 0)
+
+    first_rows(part, tokens_ref)
     share_q.relay()
-    share_o.relay()
-
-    plane = Plane(
-        lambda step, to: slots.at[step, pl.ds(to * experts, experts)],
-        lambda step, at: grads_ref.at[:, step, at],
-        send_sem,
-        recv_sem,
-        local_sem,
-        dp_count,
-    )
-
-    def dispatch(step):
-        source = cot_ref if step == 0 else held.at[order[step]]
-        dispatch_block(source, target_ref, order[step], slots, step, per)
-        plane.start(step)
-
+    along.take(1)
     for i in range(1, line):
         at = lax.rem(place + line - i, line)
         target_copy(i, at, at).wait_recv()
-    along.take(1)
-    dispatch(0)
     dispatch(1)
+    share_o.relay()
     share_q.finish()
 
     def project(which):
@@ -739,8 +753,12 @@
 
         lax.fori_loop(0, 2, one, 0)
 
-    project(0)
-    project(1)
+    project(part)
+    token_copy.wait_recv()
+    first_rows(1 - part, mate_tokens_ref)
+    project(1 - part)
+    along.take(2)
+    dispatch(2)
 
     def mix_copy(pair):
         here = pl.ds(pair * PAIR, PAIR)
@@ -755,11 +773,9 @@
     for pair in range(wide // PAIR):
         attend_pair(proj_ref, mixed_all, log_ref, pair, head_dim)
         mix_copy(pair).start()
-        if pair == 0:
-            along.take(2)
-            dispatch(2)
-    along.take(3)
-    dispatch(3)
+        if pair == 1:
+            along.take(3)
+            dispatch(3)
     mixed_ref[0] = mixed_all[pl.ds(part * rows, rows), :]
     share_o.finish()
     for pair in range(wide // PAIR):
@@ -778,6 +794,7 @@
 
     lax.fori_loop(0, rows // 128, finish_rows, 0)
     along.finish()
+    token_copy.wait_send()
     share_q.drain()
     share_o.drain()
     for copy in near:
@@ -791,7 +808,7 @@
         plane.wait_send(step)
 
 
-def run_front(tokens, mate_tokens, cotangent, target, weights, gains, sizes):
+def run_front(tokens, cotangent, target, weights, gains, sizes):
     dp_count, line, experts, per, head_dim = sizes
     rows, width = tokens.shape
     qkv_a, qkv_b, out_a, out_b = weights
@@ -802,11 +819,12 @@
     shape = jax.ShapeDtypeStruct
     return pl.pallas_call(
         functools.partial(front_kernel, dp_count, head_dim),
-        in_specs=[whole] * 9,
-        out_specs=[far] + [whole] * 9,
+        in_specs=[whole] * 11,
+        out_specs=[far] + [whole] * 10,
         out_shape=[
             shape((experts, line, dp_count, per, width), low),
-            shape((line,) + target.shape, jnp.int32),
+            shape((8, width), jnp.float32),
+            shape((line, 8, rows), jnp.int32),
             shape((dp_count, share, columns), low),
             shape((dp_count, share, 2 * wide), low),
             shape((2, rows, width), low),
@@ -822,6 +840,7 @@
             pltpu.VMEM(qkv_b.shape, low),
             pltpu.VMEM((3,) + out_b.shape, low),
             pltpu.VMEM((2 * rows, wide), low),
+            pltpu.VMEM((rows, width), low),
             dma((line + 1,)),
             dma((line,)),
             dma((line, dp_count)),
@@ -829,8 +848,8 @@
             dma((line,)),
             dma((line,)),
             dma((line,)),
-            dma((4,)),
-            dma((4,)),
+            dma((5,)),
+            dma((5,)),
             dma((wide // PAIR,)),
             dma((wide // PAIR,)),
             dma((4, dp_count // 2)),
@@ -840,7 +859,7 @@
             collective_id=1, has_side_effects=True, vmem_limit_bytes=56 << 20
         ),
         name="front",
-    )(tokens, mate_tokens, cotangent, target, *weights, gains)
+    )(tokens, cotangent, target, *weights, *gains)
 
 
 def attend_back_pair(proj_ref, log_ref, grad_ref, out_ref, dk_sum, dv_sum, pair, head_dim):
@@ -1069,6 +1088,7 @@
             results.begin(2)
         if pair == 1:
             results.end(2)
+            plane.start(1)
     first_sent[...] = dot_rows(
         qkv_grad[pl.ds((1 - part) * rows, rows), :], wq_ref[...].reshape(width, 3 * wide)
     ).astype(jnp.bfloat16)
@@ -1087,7 +1107,7 @@
         ).reshape(dp_count // 2, share, 3 * wide)
     qkvs = Pieces(qkv_pieces, qkv_held, qkv_sems, dp_count)
     qkvs.start()
-    results.begin(3, 1)
+    results.begin(3, 0)
     outs.total(out_sum)
     for i, base in enumerate((wide, PAIR, wide + PAIR)):
         out_sent[i] = out_sum[:, base : base + 2 * PAIR].astype(jnp.bfloat16)
@@ -1122,7 +1142,7 @@
     for i in range(1, line):
         line_copy(i, place, lax.rem(place + i, line)).start()
     results.end(3)
-    results.begin(1, 0)
+    results.begin(1)
     for i in range(1, line):
         at = lax.rem(place + line - i, line)
         line_copy(i, at, at).wait_recv()
@@ -1286,8 +1306,6 @@
     head_dim = w_qkv.shape[2] // 3
     heads_shard = w_qkv.shape[1]
 
-    mate_tokens = lax.ppermute(tokens, "tensor", [(t, t ^ 1) for t in range(line)])
-
     experts_total = dp_count * local_experts
     capacity = 2 * row_count // experts_total
     slot_count = experts_total * capacity
@@ -1302,7 +1320,6 @@
     earlier = jnp.dot(before, one_hot.astype(low), preferred_element_type=jnp.float32)
     slot_rank = jnp.sum(earlier.astype(jnp.int32) * one_hot, axis=1)
     target = jnp.where(slot_rank < capacity, expert_of * capacity + slot_rank, slot_count)
-    own_target = jnp.broadcast_to(target[None, :], (8, row_count))
 
     share = w_qkv.shape[0]
     wide = 2 * heads_shard * head_dim
@@ -1314,10 +1331,10 @@
     out_a = jnp.pad(out_rows, ((0, 0), (0, head_dim)))
     out_b = jnp.concatenate([out_rows[:, -head_dim:], out_rows[:, :-head_dim]], axis=1)
     out_b = jnp.pad(out_b, ((0, 0), (head_dim, 0)))
-    gains = jnp.pad(jnp.stack([ln1_gain, ln1_bias, ln2_gain, ln2_bias]), ((0, 4), (0, 0)))
     sizes = (dp_count, line, local_experts, capacity, head_dim)
     (
         grad_rows,
+        gains,
         targets,
         qkv_weight,
         out_weight,
@@ -1329,11 +1346,10 @@
         second_low,
     ) = run_front(
         tokens,
-        mate_tokens,
         cotangent,
-        own_target,
+        target,
         (qkv_a.reshape(share, -1), qkv_b, out_a, out_b),
-        gains,
+        (ln1_gain, ln1_bias, ln2_gain, ln2_bias),
         sizes,
     )
     second_grad, result, grad_expert_in, grad_expert_out = run_experts(

time: 446 us -> 439 us (0.984)
  waiting for transfers between devices: 4.83 us -> 0 us
    pallas_call x1, Pallas kernels: 113 us -> 119 us  [run_front(): pl.pallas_call(functools.partial(front_kernel, dp_count, head_dim), in_sp...]
    ppermute x1 -> x0, waiting for transfers between devices: 4.83 us -> none  [on_device(): lax.ppermute(tokens, 'tensor', [(t, t ^ 1) for t in range(line)])]
    unnamed x20 -> x16, local copies, waits for them, and re-layouts: 14.6 us -> 14.6 us
  transfers between devices with their start and end apart: 1 -> 0, of which waited for: 1 -> 0; matrix products, arithmetic and copies ran while one was open for 3% -> 0% of each run, Pallas kernels for 0% -> 0%
where the time goes in v6:
time: 439 us; the launch traced here: 431 us
  Pallas kernels  403 us (92%)
  local copies, waits for them, and re-layouts  23.9 us (5%)
    pallas_call x1, Pallas kernels, run_experts(): pl.pallas_call(functools.partial(expert_kernel, dp_count), in_specs=[whol...  166 us
    pallas_call x1, Pallas kernels, run_front(): pl.pallas_call(functools.partial(front_kernel, dp_count, head_dim), in_sp...  119 us
    pallas_call x1, Pallas kernels, run_back(): pl.pallas_call(functools.partial(back_kernel, dp_count, head_dim), in_spe...  118 us
    unnamed x16, local copies, waits for them, and re-layouts  14.6 us

profile of v6, /device:TPU:0, one launch (start us, length us, event | category | flops | bytes accessed | tf_op | source)
XLA Modules:
  0.0 430.9 jit_solution(2147070350138366758)
XLA Ops:
  0.6 0.0 copy-start
  0.7 0.7 compare_select_fusion
  1.4 0.2 copy-done
  1.6 3.1 gather_fusion
  4.7 0.7 and_select_fusion
  5.4 0.3 fusion.1
  5.7 0.6 add_select_fusion.own_target_ref
  6.3 1.0 copy.32
  7.3 0.6 pad.18.out_a_ref
  7.9 0.7 fusion.4.out_b_ref
  8.6 1.1 copy.27
  9.9 0.1 copy.31
  10.0 0.8 pad_bitcast_fusion.qkv_b_ref
  10.8 0.1 pad.16
  10.8 0.9 copy.37.qkv_a_ref
  11.7 119.0 %front.1 = (bf16[2,4,8,64,768]{4,3,2,1,0:T(8,128)(2,1)}, f32[8,768]{1,0:T(8,128)}, s32[4,8,512]{2,1,0:T(8,128)}, bf16[8,96,1152]{2,1,0:T(8,128)(2,1)}, bf16[8,96...) custom-call(bf16[512,768]{1,0:T(8,128)(2,1)} %tokens_ref.3, ...), custom_call_target="tpu_custom_call" | custom-call | tf_op jit(solution)/shard_map/front/pallas_call | solution.py:820
  130.6 165.8 %experts.1 = (f32[512,768]{1,0:T(8,128)}, bf16[2,4,8,64,768]{4,3,2,1,0:T(8,128)(2,1)}, f32[2,768,768]{2,1,0:T(8,128)}, f32[2,768,768]{2,1,0:T(8,128)}) custom-call(bf16[512,768]{1,0:T(8,128)(2,1)} %get-tuple-element.30.rows_ref, s32[4,8,512]{2,1,0:T(8,128)} %get-tuple-element.31.target_ref, bf16[2,4,8,64,768]{4,3,2,1,0:T(8,128)(2,1)} %get-tuple-element.32.grads_ref, ...), custom_call_target="tpu_custom_call" | custom-call | flops 28991029248 | bytes 25165824 | tf_op jit(solution)/shard_map/experts/pallas_call | solution.py:481
  296.4 118.0 %back.1 = (bf16[512,768]{1,0:T(8,128)(2,1)}, bf16[512,768]{1,0:T(8,128)(2,1)}, f32[8,768]{1,0:T(8,128)}, f32[96,768]{1,0:T(8,128)}, f32[96,256]{1,0:T(8,128)}) custom-call(f32[512,768]{1,0:T(8,128)} %get-tuple-element.33.back_ref, bf16[512,768]{1,0:T(8,128)(2,1)} %cot_ref.3, bf16[512,768]{1,0:T(8,128)(2,1)} %tokens_ref.3, ...), custom_call_target="tpu_custom_call" | custom-call | tf_op jit(solution)/shard_map/back/pallas_call | solution.py:1230
  414.5 0.0 copy-start.1
  414.5 1.5 slice_reduce_fusion
  416.0 0.9 slice_bitcast_fusion
  416.9 0.7 copy.36
  417.6 1.1 reshape.53
  418.8 0.2 copy.33
  419.0 0.9 copy.35
  419.8 2.1 copy.42
  421.9 0.0 copy-done.1
  421.9 0.0 slice-start
  421.9 0.9 copy.43
  422.8 0.0 slice-start.1
  422.8 5.5 %copy.44 = f32[2,768,768]{2,1,0:T(8,128)} copy(f32[2,768,768]{2,1,0:T(8,128)} %get-tuple-element.92) | data formatting | bytes 9437184
  428.3 0.0 slice-done
  428.3 0.0 slice-done.1
  428.3 2.2 copy.45
  (10 shorter events, 0.1 us)
Async XLA Ops:
  0.6 1.0 copy-start
  414.5 7.4 %copy-start.1 = (bf16[512,768]{1,0:T(8,128)(2,1)S(1)}, bf16[512,768]{1,0:T(8,128)(2,1)}, u32[]{:S(2)}) copy-start(bf16[512,768]{1,0:T(8,128)(2,1)} %get-tuple-element.85) | copy-start | bytes 2359300
  421.9 6.4 %slice-start = ((s8[4718592]{0:T(1024)(128)(4,1)}), s8[4194304]{0:T(1024)(128)(4,1)S(1)}, s32[]{:S(2)}) async-start(s8[4718592]{0:T(1024)(128)(4,1)} %bitcast.18), calls=%async_computation | async-start | bytes 8388608
  422.8 5.5 %slice-start.1 = ((s8[4718592]{0:T(1024)(128)(4,1)}), s8[524288]{0:T(1024)(128)(4,1)S(1)}, s32[]{:S(2)}) async-start(s8[4718592]{0:T(1024)(128)(4,1)} %bitcast.18), calls=%async_computation.1 | async-start | bytes 1048576

commit v7 on v6

--- a/solution.py
+++ b/solution.py
@@ -300,8 +300,8 @@
     wide_out_ref,
     back_ref,
     result_ref,
-    d_in_ref,
-    d_out_ref,
+    d_in_out_ref,
+    d_out_out_ref,
     held,
     slots,
     arrived,
@@ -314,6 +314,8 @@
     w_in_ref,
     w_out_ref,
     loaded,
+    d_in_ref,
+    d_out_ref,
     line_send,
     line_recv,
     send_sem,
@@ -327,6 +329,7 @@
     far_recv,
     out_sem,
     load_sem,
+    d_sem,
 ):
     line = held.shape[0]
     experts, _, _, per, width = arrived.shape
@@ -396,6 +399,7 @@
             back_plane.start(step)
         if step == 3:
             back_plane.start(1)
+            back_plane.start(0)
 
     def result_copy(step, expert):
         return pltpu.make_async_copy(
@@ -456,8 +460,14 @@
         later(step)
         if step + 2 < line:
             grad_copy(step + 2).start()
+    d_copies = [
+        pltpu.make_async_copy(d_in_ref, d_in_out_ref, d_sem.at[0]),
+        pltpu.make_async_copy(d_out_ref, d_out_out_ref, d_sem.at[1]),
+    ]
+    for copy in d_copies:
+        copy.start()
     along.finish()
-    home.begin(2, 0)
+    home.begin(2)
     home.end(2)
     home.begin(3)
     home.end(3)
@@ -467,6 +477,8 @@
     home.wait()
     back_ref[...] += far[0].astype(jnp.float32) + far[1].astype(jnp.float32)
     home.drain()
+    for copy in d_copies:
+        copy.wait()
     for step in range(line):
         for expert in range(experts):
             result_copy(step, expert).wait()
@@ -481,7 +493,7 @@
     return pl.pallas_call(
         functools.partial(expert_kernel, dp_count),
         in_specs=[whole, whole, far, far, far],
-        out_specs=[whole, far, whole, whole],
+        out_specs=[whole, far, far, far],
         out_shape=[
             jax.ShapeDtypeStruct(rows.shape, jnp.float32),
             jax.ShapeDtypeStruct(grads.shape, low),
@@ -501,6 +513,8 @@
             pltpu.VMEM(w_in.shape, low),
             pltpu.VMEM(w_out.shape, low),
             pltpu.VMEM((2, width // 2, width), jnp.float32),
+            pltpu.VMEM((experts, width, units), jnp.float32),
+            pltpu.VMEM((experts, units, width), jnp.float32),
             dma((line + 1,)),
             dma((line,)),
             dma((line, dp_count)),
@@ -513,6 +527,7 @@
             dma((line + 1,)),
             dma((line + 1,)),
             dma((line, experts)),
+            dma((2,)),
             dma((2,)),
         ],
         compiler_params=pltpu.CompilerParams(
@@ -753,12 +768,12 @@
 
         lax.fori_loop(0, 2, one, 0)
 
+    token_copy.wait_recv()
     project(part)
-    token_copy.wait_recv()
     first_rows(1 - part, mate_tokens_ref)
-    project(1 - part)
     along.take(2)
     dispatch(2)
+    project(1 - part)
 
     def mix_copy(pair):
         here = pl.ds(pair * PAIR, PAIR)

time: 439 us -> 434 us (0.989)
  Pallas kernels: 403 us -> 398 us
where the time goes in v7:
time: 434 us; the launch traced here: 427 us
  Pallas kernels  398 us (92%)
  local copies, waits for them, and re-layouts  23.9 us (6%)
    pallas_call x1, Pallas kernels, run_experts(): pl.pallas_call(functools.partial(expert_kernel, dp_count), in_specs=[whol...  163 us
    pallas_call x1, Pallas kernels, run_back(): pl.pallas_call(functools.partial(back_kernel, dp_count, head_dim), in_spe...  118 us
    pallas_call x1, Pallas kernels, run_front(): pl.pallas_call(functools.partial(front_kernel, dp_count, head_dim), in_sp...  118 us
    unnamed x16, local copies, waits for them, and re-layouts  14.6 us

profile of v7, /device:TPU:0, one launch (start us, length us, event | category | flops | bytes accessed | tf_op | source)
XLA Modules:
  0.0 426.6 jit_solution(1830611920421482161)
XLA Ops:
  0.6 0.0 copy-start
  0.7 0.7 compare_select_fusion
  1.4 0.2 copy-done
  1.6 3.1 gather_fusion
  4.7 0.7 and_select_fusion
  5.4 0.3 fusion.1
  5.7 0.6 add_select_fusion.own_target_ref
  6.3 1.0 copy.32
  7.3 0.6 pad.18.out_a_ref
  7.9 0.7 fusion.4.out_b_ref
  8.6 1.1 copy.27
  9.9 0.1 copy.31
  10.0 0.8 pad_bitcast_fusion.qkv_b_ref
  10.8 0.1 pad.16
  10.8 0.9 copy.37.qkv_a_ref
  11.7 117.5 %front.1 = (bf16[2,4,8,64,768]{4,3,2,1,0:T(8,128)(2,1)}, f32[8,768]{1,0:T(8,128)}, s32[4,8,512]{2,1,0:T(8,128)}, bf16[8,96,1152]{2,1,0:T(8,128)(2,1)}, bf16[8,96...) custom-call(bf16[512,768]{1,0:T(8,128)(2,1)} %tokens_ref.3, ...), custom_call_target="tpu_custom_call" | custom-call | tf_op jit(solution)/shard_map/front/pallas_call | solution.py:835
  129.2 162.9 %experts.1 = (f32[512,768]{1,0:T(8,128)}, bf16[2,4,8,64,768]{4,3,2,1,0:T(8,128)(2,1)}, f32[2,768,768]{2,1,0:T(8,128)}, f32[2,768,768]{2,1,0:T(8,128)}) custom-call(bf16[512,768]{1,0:T(8,128)(2,1)} %get-tuple-element.30.rows_ref, s32[4,8,512]{2,1,0:T(8,128)} %get-tuple-element.31.target_ref, bf16[2,4,8,64,768]{4,3,2,1,0:T(8,128)(2,1)} %get-tuple-element.32.grads_ref, ...), custom_call_target="tpu_custom_call" | custom-call | flops 28991029248 | bytes 25165824 | tf_op jit(solution)/shard_map/experts/pallas_call | solution.py:493
  292.2 118.0 %back.1 = (bf16[512,768]{1,0:T(8,128)(2,1)}, bf16[512,768]{1,0:T(8,128)(2,1)}, f32[8,768]{1,0:T(8,128)}, f32[96,768]{1,0:T(8,128)}, f32[96,256]{1,0:T(8,128)}) custom-call(f32[512,768]{1,0:T(8,128)} %get-tuple-element.33.back_ref, bf16[512,768]{1,0:T(8,128)(2,1)} %cot_ref.3, bf16[512,768]{1,0:T(8,128)(2,1)} %tokens_ref.3, ...), custom_call_target="tpu_custom_call" | custom-call | tf_op jit(solution)/shard_map/back/pallas_call | solution.py:1245
  410.2 0.0 copy-start.1
  410.2 1.5 slice_reduce_fusion
  411.7 0.9 slice_bitcast_fusion
  412.6 0.7 copy.36
  413.4 1.1 reshape.53
  414.5 0.2 copy.33
  414.7 0.9 copy.35
  415.6 2.1 copy.42
  417.6 0.0 copy-done.1
  417.6 0.0 slice-start
  417.6 0.9 copy.43
  418.5 0.0 slice-start.1
  418.5 5.5 %copy.44 = f32[2,768,768]{2,1,0:T(8,128)} copy(f32[2,768,768]{2,1,0:T(8,128)} %get-tuple-element.92) | data formatting | bytes 9437184
  424.0 0.0 slice-done
  424.0 0.0 slice-done.1
  424.0 2.2 copy.45
  (10 shorter events, 0.1 us)
Async XLA Ops:
  0.6 1.0 copy-start
  410.2 7.4 %copy-start.1 = (bf16[512,768]{1,0:T(8,128)(2,1)S(1)}, bf16[512,768]{1,0:T(8,128)(2,1)}, u32[]{:S(2)}) copy-start(bf16[512,768]{1,0:T(8,128)(2,1)} %get-tuple-element.85) | copy-start | bytes 2359300
  417.6 6.4 %slice-start = ((s8[4718592]{0:T(1024)(128)(4,1)}), s8[4194304]{0:T(1024)(128)(4,1)S(1)}, s32[]{:S(2)}) async-start(s8[4718592]{0:T(1024)(128)(4,1)} %bitcast.18), calls=%async_computation | async-start | bytes 8388608
  418.5 5.5 %slice-start.1 = ((s8[4718592]{0:T(1024)(128)(4,1)}), s8[524288]{0:T(1024)(128)(4,1)S(1)}, s32[]{:S(2)}) async-start(s8[4718592]{0:T(1024)(128)(4,1)} %bitcast.18), calls=%async_computation.1 | async-start | bytes 1048576
